TPU v7x, 32 devices: a whole 2x2x4 slice. The times are simulated.
32 devices in a mesh: groups: 2 (over y), rep: 4 (over z), tp: 4 (over x, core).
Axes of the slice: x: 2, y: 2, z: 4, core: 2. Of those that a mesh axis runs over, the one named last changes fastest.
Arguments:
- tokens_in: bfloat16 [16384, 8192], P(('groups', 'rep'), 'tp'), parts along dimension 0, may hold values from -6 to 6
- upstream: bfloat16 [16384, 1024], P(('groups', 'rep')), parts along dimension 0, may hold values from -6 to 6
- base_weight: bfloat16 [8192, 1024], P('tp'), may hold values from -0.1875 to 0.1875
- bank_a: bfloat16 [32, 16, 8192], P('rep', None, 'tp'), may hold values from -0.125 to 0.125
- bank_b: bfloat16 [32, 16, 1024], P('rep', None, 'tp'), may hold values from -0.1875 to 0.1875
- slot_ids: int32 [16384], P(('groups', 'rep')), parts along dimension 0, may hold values from 0 to 7, as said below
- used_lists: int32 [8, 8], P(('groups', 'rep')), parts along dimension 0, may hold values from 0 to 31, as said below
Outputs:
- token_gradient: bfloat16 [16384, 8192], P(('groups', 'rep'), 'tp'), parts along dimension 0
- grad_a: float32 [64, 16, 8192], P(('groups', 'rep'), None, 'tp'), parts along dimension 0
- grad_b: float32 [64, 16, 1024], P(('groups', 'rep'), None, 'tp'), parts along dimension 0
There are 2 independent parts, one for each index of `groups`. A program takes and returns all parts, laid end to end along the dimension named above; an argument that names none is the same for every part. Nothing has to cross between parts.
Inputs may be any that keep to these rules, and one draw needn't show every extreme that they name: `slot_ids`: constant within aligned blocks of 128 rows, never falling within one replica's 2048 rows, and every value 0 to 7 appears in every replica. `used_lists`: A replica's 8 ids are distinct; replica o owns ids o * 8 to (o + 1) * 8 - 1, and at most 2 ids of one list have the same owner, exactly 2 for some owner in every list.
All inputs are finite; a program needn't handle non-finite values.
Results may differ from a plain program's by a relative error of at most 0.0034.
Values may be sent and summed in bfloat16 or wider, within the bound.
No kernel may reach another device: no remote copies, remote signals or barrier semaphores. Data moves between devices by JAX's collectives and lax.ppermute only.
A program may use at most 128 MiB of HBM per device.

v0:
```python
import jax
import jax.numpy as jnp
from jax import lax
from jax.sharding import PartitionSpec as P

BLOCK = 128


adapter_scale = 2.0


def owner_place(owners):
    count = owners.shape[-1]
    before = jnp.arange(count)[:, None] > jnp.arange(count)[None, :]
    same_owner = owners[..., :, None] == owners[..., None, :]
    return jnp.sum((same_owner & before).astype(jnp.int32), axis=-1)


def local(tokens_in, upstream, base_weight, bank_a, bank_b, slot_ids, used_lists):
    row_count = tokens_in.shape[0]
    width_local = tokens_in.shape[1]
    cols_local = bank_b.shape[2]
    rank_dim = bank_a.shape[1]
    adapters_held = bank_a.shape[0]
    slot_count = used_lists.shape[1]
    n_blocks = row_count // BLOCK
    rep_count = lax.axis_size("rep")
    cap_count = (slot_count + rep_count - 1) // rep_count
    my_rank = lax.axis_index("rep")
    tp_rank = lax.axis_index("tp")
    all_lists = lax.all_gather(used_lists, "rep", axis=0, tiled=True)
    owners = all_lists // adapters_held
    local_ids = all_lists % adapters_held
    places = owner_place(owners)
    owned_here = owners == my_rank
    picks = (
        owned_here[:, :, None, None]
        & (places[:, :, None, None] == jnp.arange(cap_count)[None, None, :, None])
        & (local_ids[:, :, None, None] == jnp.arange(adapters_held)[None, None, None, :])
    )
    selector = jnp.sum(picks.astype(jnp.float32), axis=1)
    selector_half = selector.astype(jnp.bfloat16)
    send_a = jnp.einsum(
        "rcj,jqd->rcqd", selector_half, bank_a, preferred_element_type=jnp.float32
    ).astype(jnp.bfloat16)
    send_b = jnp.einsum(
        "rcj,jqd->rcqd", selector_half, bank_b, preferred_element_type=jnp.float32
    ).astype(jnp.bfloat16)
    recv_a, recv_b = (
        lax.all_to_all(send_a, "rep", split_axis=0, concat_axis=0, tiled=True),
        lax.all_to_all(send_b, "rep", split_axis=0, concat_axis=0, tiled=True),
    )
    my_list = used_lists[0]
    my_owner = my_list // adapters_held
    my_place = owner_place(my_owner)
    source_row = my_owner * cap_count + my_place
    fetched_a = recv_a.reshape(rep_count * cap_count, rank_dim, width_local)[source_row]
    fetched_b = recv_b.reshape(rep_count * cap_count, rank_dim, cols_local)[source_row]
    block_slot = slot_ids.reshape(n_blocks, BLOCK)[:, 0]
    block_a = fetched_a[block_slot]
    token_blocks = tokens_in.reshape(n_blocks, BLOCK, width_local)
    grad_blocks = upstream.reshape(n_blocks, BLOCK, upstream.shape[1])
    local_grad = lax.dynamic_slice_in_dim(upstream, tp_rank * cols_local, cols_local, 1).reshape(
        n_blocks, BLOCK, cols_local
    )
    down_part = jnp.einsum(
        "brd,btd->brt", block_a, token_blocks, preferred_element_type=jnp.float32
    )
    whole_b = lax.all_gather(fetched_b, "tp", axis=2, tiled=True)
    up_weight_complete = jnp.einsum(
        "brf,btf->brt", whole_b[block_slot], grad_blocks, preferred_element_type=jnp.float32
    )
    down_weight_complete = lax.psum(down_part, "tp")
    scaled_down_weight = (adapter_scale * down_weight_complete).astype(jnp.bfloat16)
    scaled_up_weight = (adapter_scale * up_weight_complete).astype(jnp.bfloat16)
    frozen_value_term = lax.dot_general(
        upstream, base_weight, (((1,), (1,)), ((), ())), preferred_element_type=jnp.float32
    )
    adapter_term = jnp.einsum(
        "brt,brd->btd", scaled_up_weight, block_a, preferred_element_type=jnp.float32
    ).reshape(row_count, width_local)
    token_gradient = (frozen_value_term + adapter_term).astype(jnp.bfloat16)
    block_grad_a = jnp.einsum(
        "brt,btd->brd", scaled_up_weight, token_blocks, preferred_element_type=jnp.float32
    )
    block_grad_b = jnp.einsum(
        "brt,btf->brf", scaled_down_weight, local_grad, preferred_element_type=jnp.float32
    )
    slot_onehot = (block_slot[:, None] == jnp.arange(slot_count)[None, :]).astype(jnp.float32)
    slot_grad_a = jnp.einsum(
        "bk,brd->krd", slot_onehot, block_grad_a, precision=lax.Precision.HIGHEST
    )
    slot_grad_b = jnp.einsum(
        "bk,brd->krd", slot_onehot, block_grad_b, precision=lax.Precision.HIGHEST
    )
    backward_pick = (
        (my_owner[None, None, :] == jnp.arange(rep_count)[:, None, None])
        & (my_place[None, None, :] == jnp.arange(cap_count)[None, :, None])
    ).astype(jnp.float32)
    outgoing_a = jnp.einsum(
        "ock,krd->ocrd", backward_pick, slot_grad_a, precision=lax.Precision.HIGHEST
    )
    outgoing_b = jnp.einsum(
        "ock,krd->ocrd", backward_pick, slot_grad_b, precision=lax.Precision.HIGHEST
    )
    incoming_a, incoming_b = (
        lax.all_to_all(outgoing_a, "rep", split_axis=0, concat_axis=0, tiled=True),
        lax.all_to_all(outgoing_b, "rep", split_axis=0, concat_axis=0, tiled=True),
    )
    grad_a = jnp.einsum("rcj,rcqd->jqd", selector, incoming_a, precision=lax.Precision.HIGHEST)
    grad_b = jnp.einsum("rcj,rcqd->jqd", selector, incoming_b, precision=lax.Precision.HIGHEST)
    return (token_gradient, grad_a, grad_b)


def solution(mesh):
    in_specs = (
        P(("groups", "rep"), "tp"),
        P(("groups", "rep"), None),
        P("tp", None),
        P("rep", None, "tp"),
        P("rep", None, "tp"),
        P(("groups", "rep")),
        P(("groups", "rep"), None),
    )
    out_specs = (
        P(("groups", "rep"), "tp"),
        P(("groups", "rep"), None, "tp"),
        P(("groups", "rep"), None, "tp"),
    )
    return jax.shard_map(local, mesh=mesh, in_specs=in_specs, out_specs=out_specs, check_vma=False)
```

profile of v0, /device:TPU:0, one launch (start us, length us, event | category | flops | bytes accessed | tf_op | source)
XLA Modules:
  0.0 150.8 jit_solution(8430332495411160686)
XLA Ops:
  7.2 12.7 %all-gather.1 = s32[4,1,8]{2,1,0:T(1,128)S(1)} all-gather(s32[1,1,8]{2,1,0:T(1,128)} %bitcast.100), channel_id=1, replica_groups=mesh['groups'=2,'rep'=4,'tp'=4] {'rep'}, dimensions={0}, use_global_device_ids=true | all-gather | bytes 160 | tf_op jit(solution)/shard_map/all_gather | solution.py:31
  19.9 0.1 iota_compare_fusion
  20.0 0.2 convert_reduce_fusion.1
  20.2 0.1 convert_reduce_fusion
  20.3 1.0 convolution_convert_fusion.1
  21.3 0.6 copy.42
  22.0 3.3 %all-to-all-start = ((bf16[4,2,16,256]{3,2,1,0:T(8,128)(2,1)}), bf16[4,2,16,256]{3,2,1,0:T(8,128)(2,1)S(1)}, u32[]{:S(2)}, u32[]{:S(2)}) async-start(bf16[4,2,16,256]{3,2,1,0:T(8,128)(2,1)} %copy.42), calls=%async_computation | async-start | bytes 131072 | tf_op jit(solution)/shard_map/all_to_all | solution.py:51
  25.3 0.7 and_select_fusion.1
  25.9 0.7 fusion.26
  26.6 0.2 convert_reduce_fusion.2
  26.8 0.7 fusion.25
  27.5 1.5 convolution_convert_fusion
  29.0 1.1 copy.45
  30.1 0.8 slice_reduce_fusion
  30.9 1.3 constant_dynamic-slice_fusion
  32.2 0.0 all-to-all-done
  32.2 5.1 %all-to-all-start.1 = ((bf16[4,2,16,2048]{3,2,1,0:T(8,128)(2,1)}), bf16[4,2,16,2048]{3,2,1,0:T(8,128)(2,1)S(1)}, u32[]{:S(2)}, u32[]{:S(2)}) async-start(bf16[4,2,16,2048]{3,2,1,0:T(8,128)(2,1)} %copy.45), calls=%async_computation.1 | async-start | bytes 1048576 | tf_op jit(solution)/shard_map/all_to_all | solution.py:50
  37.3 0.0 all-reduce.2.cloned.1.call-start
  37.3 0.5 gather_fusion
  37.8 5.8 %all-gather = bf16[8,16,1024]{2,1,0:T(8,128)(2,1)S(1)} all-gather(bf16[8,16,256]{2,1,0:T(8,128)(2,1)S(1)} %gather_fusion), channel_id=2, replica_groups=mesh['groups'=2,'rep'=4,'tp'=4] {'tp'}, dimensions={2}, use_global_device_ids=true | all-gather | bytes 327680 | tf_op jit(solution)/shard_map/all_gather | solution.py:69
  43.6 0.6 gather_fusion.1
  44.2 3.4 %fusion.2 = bf16[16,16,128]{2,1,0:T(8,128)(2,1)S(1)} fusion(bf16[16,16,1024]{2,1,0:T(8,128)(2,1)S(1)} %gather_fusion.1, bf16[16,128,1024]{2,1,0:T(8,128)(2,1)} %bitcast.93), kind=kOutput, calls=%fused_computation.13 | convolution fusion | flops 67174400 | bytes 4784128 | tf_op jit(solution)/shard_map/brf,btf->brt/dot_general | solution.py:70
  47.6 4.6 %fusion.29 = f32[16,16,2048]{2,1,0:T(8,128)S(1)} fusion(bf16[16,16,128]{2,1,0:T(8,128)(2,1)S(1)} %fusion.2, bf16[16,128,2048]{2,1,0:T(8,128)(2,1)} %bitcast.91), kind=kOutput, calls=%fused_computation.80 | convolution fusion | flops 134217728 | bytes 10551296 | tf_op jit(solution)/shard_map/brt,btd->brd/dot_general | solution.py:83
  52.2 3.0 %convolution_bitcast_fusion.1 = f32[8,16,2048,1]{2,0,1,3:T(8,128)} fusion(f32[16,16,2048]{2,1,0:T(8,128)S(1)} %fusion.29, s32[16]{0:T(128)S(1)} %get-tuple-element.18), kind=kOutput, calls=%fused_computation.7 | convolution fusion | flops 50331776 | bytes 3145792 | tf_op jit(solution)/shard_map/bk,brd->krd/dot_general | solution.py:90
  55.2 0.0 all-to-all-done.1
  55.2 0.6 gather_fusion.2
  55.8 0.6 gather_fusion.3
  56.4 0.0 copy-start
  56.4 6.4 %fusion.30 = f32[16,16,128]{2,1,0:T(8,128)} fusion(bf16[16,16,2048]{2,1,0:T(8,128)(2,1)S(1)} %gather_fusion.3, bf16[16,128,2048]{2,1,0:T(8,128)(2,1)} %bitcast.92), kind=kOutput, calls=%fused_computation.81 | convolution fusion | flops 134217728 | bytes 9568256 | tf_op jit(solution)/shard_map/brd,btd->brt/dot_general | solution.py:66
  62.8 0.0 all-reduce.2.cloned.1.call-update
  62.9 0.0 copy-done
  62.9 2.3 %fusion.13 = f32[4,2,16,2048]{3,1,2,0:T(2,128)} fusion(f32[8,16,2048,1]{2,0,1,3:T(8,128)S(1)} %copy-done, pred[4,2,8,1]{2,0,1,3:T(4,128)(4,1)S(1)} %and_bitcast_fusion), kind=kOutput, calls=%fused_computation.32 | convolution fusion | flops 25165824 | bytes 2097216 | tf_op jit(solution)/shard_map/ock,krd->ocrd/dot_general | solution.py:100
  65.2 30.7 %all-reduce.2.cloned.1.call-done = f32[16,16,128]{2,1,0:T(8,128)} async-done(((f32[16,16,128]{2,1,0:T(8,128)}), f32[16,16,128]{2,1,0:T(8,128)}) %all-reduce.2.cloned.1.call-update) | async-done | bytes 131088 | tf_op jit(solution)/shard_map/psum | solution.py:73
  95.9 1.1 fusion.6
  97.1 0.4 convolution_bitcast_fusion.3
  97.4 0.9 fusion.11
  98.4 4.6 %all-to-all-start.3 = ((f32[4,2,16,256]{3,1,2,0:T(2,128)}), f32[4,2,16,256]{3,1,2,0:T(2,128)S(1)}, u32[]{:S(2)}, u32[]{:S(2)}) async-start(f32[4,2,16,256]{3,1,2,0:T(2,128)} %fusion.11), calls=%async_computation.3 | async-start | bytes 262144 | tf_op jit(solution)/shard_map/all_to_all | solution.py:108
  103.0 8.1 %fusion.28 = f32[16,128,2048]{2,1,0:T(8,128)} fusion(bf16[16,16,128]{2,1,0:T(8,128)(2,1)S(1)} %fusion.2, bf16[16,16,2048]{2,1,0:T(8,128)(2,1)S(1)} %gather_fusion.3), kind=kOutput, calls=%fused_computation.79 | convolution fusion | flops 134217728 | bytes 17891328 | tf_op jit(solution)/shard_map/brt,brd->btd/dot_general | solution.py:79
  111.0 0.0 all-to-all-done.3
  111.0 5.1 %all-to-all-start.2 = ((f32[4,2,16,2048]{3,1,2,0:T(2,128)}), f32[4,2,16,2048]{3,1,2,0:T(2,128)S(1)}, u32[]{:S(2)}, u32[]{:S(2)}) async-start(f32[4,2,16,2048]{3,1,2,0:T(2,128)} %fusion.13), calls=%async_computation.2 | async-start | bytes 2097152 | tf_op jit(solution)/shard_map/all_to_all | solution.py:107
  116.1 16.4 %fusion = bf16[2048,2048]{1,0:T(8,128)(2,1)} fusion(f32[16,128,2048]{2,1,0:T(8,128)} %fusion.28, bf16[2048,1024]{1,0:T(8,128)(2,1)} %param.8, bf16[2048,1024]{1,0:T(8,128)(2,1)} %param.9), kind=kOutput, calls=%fused_computation.5 | convolution fusion | flops 8598323200 | bytes 33554432 | tf_op jit(solution)/shard_map/dot_general | solution.py:76
  132.5 0.3 convolution_bitcast_fusion.2
  132.9 0.7 copy.55
  133.6 6.7 %all-to-all-done.2 = f32[4,2,16,2048]{3,1,2,0:T(2,128)S(1)} async-done(((f32[4,2,16,2048]{3,1,2,0:T(2,128)}), f32[4,2,16,2048]{3,1,2,0:T(2,128)S(1)}, u32[]{:S(2)}, u32[]{:S(2)}) %all-to-all-start.2) | async-done | bytes 1048608 | tf_op jit(solution)/shard_map/all_to_all | solution.py:107
  140.3 2.1 %convolution_bitcast_fusion = f32[8,16,2048]{2,0,1:T(8,128)S(1)} fusion(f32[4,2,16,2048]{3,1,2,0:T(2,128)S(1)} %all-to-all-done.2, f32[4,2,8]{2,1,0:T(2,128)S(1)} %convert_reduce_fusion), kind=kOutput, calls=%fused_computation.6 | convolution fusion | flops 25165824 | bytes 2097408 | tf_op jit(solution)/shard_map/rcj,rcqd->jqd/dot_general | solution.py:110
  142.4 1.6 %copy.54 = f32[8,16,2048]{2,1,0:T(8,128)} copy(f32[8,16,2048]{2,0,1:T(8,128)S(1)} %convolution_bitcast_fusion) | data formatting | bytes 2097152
  (10 shorter events, 0.1 us)
Async XLA Ops:
  22.0 10.2 %all-to-all-start = ((bf16[4,2,16,256]{3,2,1,0:T(8,128)(2,1)}), bf16[4,2,16,256]{3,2,1,0:T(8,128)(2,1)S(1)}, u32[]{:S(2)}, u32[]{:S(2)}) async-start(bf16[4,2,16,256]{3,2,1,0:T(8,128)(2,1)} %copy.42), calls=%async_computation | async-start | bytes 131072 | tf_op jit(solution)/shard_map/all_to_all | solution.py:51
  32.2 23.0 %all-to-all-start.1 = ((bf16[4,2,16,2048]{3,2,1,0:T(8,128)(2,1)}), bf16[4,2,16,2048]{3,2,1,0:T(8,128)(2,1)S(1)}, u32[]{:S(2)}, u32[]{:S(2)}) async-start(bf16[4,2,16,2048]{3,2,1,0:T(8,128)(2,1)} %copy.45), calls=%async_computation.1 | async-start | bytes 1048576 | tf_op jit(solution)/shard_map/all_to_all | solution.py:50
  37.3 58.6 %all-reduce.2.cloned.1.call-start = ((), (), s32[]{:S(2)}) async-start(), calls=%async_computation.4 | async-start | bytes 262144 | tf_op jit(solution)/shard_map/psum | solution.py:73
  56.4 6.4 %copy-start = (f32[8,16,2048,1]{2,0,1,3:T(8,128)S(1)}, f32[8,16,2048,1]{2,0,1,3:T(8,128)}, u32[]{:S(2)}) copy-start(f32[8,16,2048,1]{2,0,1,3:T(8,128)} %convolution_bitcast_fusion.1) | copy-start | bytes 3145732
  98.4 12.7 %all-to-all-start.3 = ((f32[4,2,16,256]{3,1,2,0:T(2,128)}), f32[4,2,16,256]{3,1,2,0:T(2,128)S(1)}, u32[]{:S(2)}, u32[]{:S(2)}) async-start(f32[4,2,16,256]{3,1,2,0:T(2,128)} %fusion.11), calls=%async_computation.3 | async-start | bytes 262144 | tf_op jit(solution)/shard_map/all_to_all | solution.py:108
  111.0 29.2 %all-to-all-start.2 = ((f32[4,2,16,2048]{3,1,2,0:T(2,128)}), f32[4,2,16,2048]{3,1,2,0:T(2,128)S(1)}, u32[]{:S(2)}, u32[]{:S(2)}) async-start(f32[4,2,16,2048]{3,1,2,0:T(2,128)} %fusion.13), calls=%async_computation.2 | async-start | bytes 2097152 | tf_op jit(solution)/shard_map/all_to_all | solution.py:107
Sparse Core Ops, SparseCore 0:
  63.0 32.8 all-reduce.1
where the time goes:
time: 152 us; the launch traced here: 151 us
  matrix products  51.6 us (34%)
  waiting for transfers between devices  37.5 us (25%)
  blocking collectives  18.5 us (12%)
  starting transfers between devices  18 us (12%)
  between operations  14.2 us (9%)
  local copies, waits for them, and re-layouts  7.63 us (5%)
  other arithmetic  3.45 us (2%)
    psum x1, waiting for transfers between devices, local(): down_weight_complete = lax.psum(down_part, 'tp')  30.7 us
    dot_general x1, matrix products, local(): lax.dot_general(upstream, base_weight, (((1,), (1,)), ((), ())), preferre...  16.4 us
    all_gather x1, blocking collectives, local(): all_lists = lax.all_gather(used_lists, 'rep', axis=0, tiled=True)  12.7 us
    dot_general x1, matrix products, local(): jnp.einsum('brt,brd->btd', scaled_up_weight, block_a, preferred_element_t...  8.09 us
    all_to_all x1, waiting for transfers between devices, local(): lax.all_to_all(outgoing_a, 'rep', split_axis=0, concat_axis=0, tiled=True)  6.7 us
    dot_general x1, matrix products, local(): jnp.einsum('brd,btd->brt', block_a, token_blocks, preferred_element_type=...  6.41 us
    all_gather x1, blocking collectives, local(): whole_b = lax.all_gather(fetched_b, 'tp', axis=2, tiled=True)  5.79 us
    all_to_all x1, starting transfers between devices, local(): lax.all_to_all(outgoing_a, 'rep', split_axis=0, concat_axis=0, tiled=True)  5.09 us
  transfers between devices with their start and end apart: 5, of which 2 were waited for; matrix products, arithmetic and copies ran while one was open for 31% of the time, Pallas kernels for 0%

commit v1 on v0

v1 whole, which is shorter than its diff:
```python
import functools

import jax
import jax.numpy as jnp
from jax import lax
from jax.experimental import pallas as pl
from jax.experimental.pallas import tpu as pltpu
from jax.sharding import PartitionSpec as P

BLOCK = 128
SCALE = 2.0
VMEM_LIMIT = 48 * 1024 * 1024

F32 = jnp.float32
BF16 = jnp.bfloat16
ANY = pl.BlockSpec(memory_space=pl.ANY)
SMEM = pl.BlockSpec(memory_space=pltpu.SMEM)
VMEM = pl.BlockSpec(memory_space=pltpu.VMEM)
NT = (((1,), (1,)), ((), ()))
TN = (((0,), (0,)), ((), ()))


def params(**kw):
    return pltpu.CompilerParams(vmem_limit_bytes=VMEM_LIMIT, **kw)


def cost(flops, nbytes):
    return pl.CostEstimate(flops=int(flops), bytes_accessed=int(nbytes), transcendentals=0)


def whole(shape):
    return pl.BlockSpec(shape, lambda *_: (0,) * len(shape))


def owner_of(ident, held):
    return lax.div(ident, jnp.int32(held))


def pick_kernel(rep, cap, held, slots, nb, *refs):
    lists = refs[:rep]
    slot_ids, bank_a = refs[rep : rep + 2]
    outs = refs[rep + 2 : rep + 2 + rep]
    pick, sel, vslot = refs[2 * rep + 2 : 2 * rep + 5]
    place_v, sems = refs[2 * rep + 5 :]
    me = lax.axis_index("rep")
    for s in range(rep):
        count = jnp.int32(0)
        idx = [jnp.int32(-1)] * cap
        for k in range(slots):
            ident = lists[s][0, k]
            mine = owner_of(ident, held) == me
            for c in range(cap):
                idx[c] = jnp.where(mine & (count == c), lax.rem(ident, jnp.int32(held)), idx[c])
            count = count + mine.astype(jnp.int32)
        for c in range(cap):
            pick[s * cap + c] = idx[c]
            pltpu.make_async_copy(
                bank_a.at[jnp.maximum(idx[c], 0)], outs[s].at[c], sems.at[s, c]
            ).start()
    ids = [lists[0][0, k] for k in range(slots)]
    owners = [owner_of(i, held) for i in ids]
    for v in range(rep * cap):
        sel[v] = jnp.int32(0)
    for k in range(slots):
        place = jnp.int32(0)
        for j in range(k):
            place = place + (owners[j] == owners[k]).astype(jnp.int32)
        v = jnp.bitwise_xor(owners[k], me) * cap + place
        place_v[k] = v
        sel[v] = lax.rem(ids[k], jnp.int32(held))
    for b in range(nb):
        vslot[b] = place_v[slot_ids[b, 0]]
    for s in range(rep):
        for c in range(cap):
            pltpu.make_async_copy(bank_a.at[0], outs[s].at[c], sems.at[s, c]).wait()


def select_kernel(rep, cap, rank, *refs):
    sel = refs[0]
    banks = refs[1 : 1 + rep]
    out = refs[1 + rep]
    for v in range(rep * cap):
        start = pl.multiple_of(sel[v] * rank, rank)
        out[v * rank : (v + 1) * rank, :] = banks[v // cap][pl.ds(start, rank), :]


def up_kernel(rep, cap, rank, tp, nb, *refs):
    vslot, upstream = refs[:2]
    quarters = refs[2 : 2 + tp]
    tokens = refs[2 + tp]
    up_out = refs[3 + tp]
    grads = refs[4 + tp :]
    width = rep * cap * rank
    per = cap * rank
    cols = quarters[0].shape[1]
    tp_rank = lax.axis_index("tp")

    @pl.when(pl.program_id(0) == 0)
    def _():
        chunk = 4
        lane_slot = lax.broadcasted_iota(jnp.int32, (BLOCK, width), 1) // rank
        for r in range(nb // chunk):
            rows = slice(r * chunk * BLOCK, (r + 1) * chunk * BLOCK)
            acc = None
            for s in range(tp):
                at = pl.multiple_of(jnp.bitwise_xor(tp_rank, s) * cols, cols)
                part = lax.dot_general(
                    upstream[rows, pl.ds(at, cols)], quarters[s][...], NT, preferred_element_type=F32
                )
                acc = part if acc is None else acc + part
            acc = (SCALE * acc).astype(BF16)
            for b in range(chunk):
                blk = r * chunk + b
                keep = lane_slot == vslot[blk]
                part = acc[b * BLOCK : (b + 1) * BLOCK, :]
                up_out[blk * BLOCK : (blk + 1) * BLOCK, :] = jnp.where(keep, part, jnp.zeros_like(part))

    grad = lax.dot_general(up_out[...], tokens[...], TN, preferred_element_type=F32)
    for s in range(rep):
        grads[s][...] = grad[s * per : (s + 1) * per, :].astype(grads[s].dtype)


def down_kernel(rep, cap, rank, blocks, *refs):
    vslot, tokens = refs[:2]
    parts = refs[2 : 2 + rep]
    down, a_all = refs[2 + rep : 4 + rep]
    turned = refs[4 + rep]
    per = cap * rank
    step = pl.program_id(0)

    @pl.when(step == 0)
    def _():
        for s in range(rep):
            a_all[s * per : (s + 1) * per, :] = parts[s][...]

    prod = lax.dot_general(tokens[...], a_all[...], NT, preferred_element_type=F32)
    for b in range(blocks):
        turned[b] = prod[b * BLOCK : (b + 1) * BLOCK, :].T
    for b in range(blocks):
        start = pl.multiple_of(vslot[step * blocks + b] * rank, rank)
        down[:, b * BLOCK : (b + 1) * BLOCK] = turned[b, pl.ds(start, rank), :]


def grad_b_kernel(rep, cap, rank, nb, *refs):
    vslot, down_here, down_there, upstream = refs[:4]
    grads = refs[4 : 4 + rep]
    spread, mine, sem = refs[4 + rep :]
    per = cap * rank
    cols = mine.shape[1]
    at = pl.multiple_of(lax.axis_index("tp") * cols, cols)
    copy = pltpu.make_async_copy(upstream.at[:, pl.ds(at, cols)], mine, sem)
    copy.start()
    spread[...] = jnp.zeros_like(spread)
    total = (SCALE * (down_here[...] + down_there[...])).astype(BF16)
    for b in range(nb):
        start = pl.multiple_of(vslot[b] * rank, rank)
        spread[pl.ds(start, rank), b * BLOCK : (b + 1) * BLOCK] = total[:, b * BLOCK : (b + 1) * BLOCK]
    copy.wait()
    grad = jnp.dot(spread[...], mine[...], preferred_element_type=F32)
    for s in range(rep):
        grads[s][...] = grad[s * per : (s + 1) * per, :].astype(grads[s].dtype)


def token_kernel(aliased, chunk, *refs):
    upstream, up_scaled, weight, a_all = refs[:4]
    out = refs[-1]
    rows = upstream.shape[0]
    for r in range(rows // chunk):
        at = slice(r * chunk, (r + 1) * chunk)
        frozen = lax.dot_general(upstream[at, :], weight[...], NT, preferred_element_type=F32)
        low = jnp.dot(up_scaled[at, :], a_all[...], preferred_element_type=F32)
        out[at, :] = (frozen + low).astype(BF16)


def token_part(upstream, up_scaled, weight, a_all, tile, first, count, before=None):
    rows, outs = upstream.shape
    width = weight.shape[0]
    depth = a_all.shape[0]
    args = [upstream, up_scaled, weight, a_all]
    specs = [
        whole((rows, outs)),
        whole((rows, depth)),
        pl.BlockSpec((tile, outs), lambda i: (i + first, 0)),
        pl.BlockSpec((depth, tile), lambda i: (0, i + first)),
    ]
    alias = {}
    if before is not None:
        args.append(before)
        specs.append(ANY)
        alias = {4: 0}
    return pl.pallas_call(
        functools.partial(token_kernel, before is not None, 512),
        out_shape=jax.ShapeDtypeStruct((rows, width), BF16),
        grid=(count,),
        in_specs=specs,
        out_specs=pl.BlockSpec((rows, tile), lambda i: (0, i + first)),
        input_output_aliases=alias,
        compiler_params=params(),
        cost_estimate=cost(2 * rows * (outs + 256) * tile * count, 2 * rows * (outs + tile * count)),
        name="token_gradient",
    )(*args)


def finish_kernel(rep, cap, rank, *refs):
    pick = refs[0]
    in_a = refs[1 : 1 + rep]
    in_b = refs[1 + rep : 1 + 2 * rep]
    out_a, out_b = refs[1 + 2 * rep :]
    out_a[...] = jnp.zeros_like(out_a)
    out_b[...] = jnp.zeros_like(out_b)
    for s in range(rep):
        for c in range(cap):
            to = pick[s * cap + c]

            @pl.when(to >= 0)
            def _():
                out_a[to] += in_a[s][c * rank : (c + 1) * rank, :].astype(F32)
                out_b[to] += in_b[s][c * rank : (c + 1) * rank, :].astype(F32)


def local(tokens_in, upstream, base_weight, bank_a, bank_b, slot_ids, used_lists):
    rows, width = tokens_in.shape
    outs = upstream.shape[1]
    held, rank, cols = bank_b.shape
    slots = used_lists.shape[1]
    nb = rows // BLOCK
    rep = lax.axis_size("rep")
    tp = lax.axis_size("tp")
    cap = (slots + rep - 1) // rep
    per = cap * rank
    depth = rep * per

    def along(axis, size, x, s):
        return lax.ppermute(x, axis, [(i, i ^ s) for i in range(size)])

    def rep_swap(x, s):
        return along("rep", rep, x, s)

    def tp_swap(x, s):
        return along("tp", tp, x, s)

    struct = jax.ShapeDtypeStruct
    lists = [used_lists] + [rep_swap(used_lists, s) for s in range(1, rep)]
    b_flat = bank_b.reshape(held * rank, cols)
    banks = [b_flat] + [rep_swap(b_flat, s) for s in range(1, rep)]

    picked = pl.pallas_call(
        functools.partial(pick_kernel, rep, cap, held, slots, nb),
        out_shape=[struct((cap, rank, width), BF16)] * rep
        + [struct((rep * cap,), jnp.int32), struct((rep * cap,), jnp.int32), struct((nb,), jnp.int32)],
        in_specs=[SMEM] * (rep + 1) + [ANY],
        out_specs=[ANY] * rep + [SMEM] * 3,
        scratch_shapes=[pltpu.SMEM((slots,), jnp.int32), pltpu.SemaphoreType.DMA((rep, cap))],
        compiler_params=params(),
        cost_estimate=cost(0, 4 * depth * width),
        name="pick",
    )(*lists, slot_ids.reshape(nb, BLOCK), bank_a)
    send_a = [x.reshape(per, width) for x in picked[:rep]]
    pick, sel, vslot = picked[rep:]
    recv_a = [send_a[0]] + [rep_swap(send_a[s], s) for s in range(1, rep)]

    quarter = pl.pallas_call(
        functools.partial(select_kernel, rep, cap, rank),
        out_shape=struct((depth, cols), BF16),
        in_specs=[SMEM] + [VMEM] * rep,
        out_specs=VMEM,
        compiler_params=params(),
        cost_estimate=cost(0, 4 * depth * cols),
        name="select_b",
    )(sel, *banks)
    quarters = {0: quarter}
    bit = tp // 2
    while bit:
        quarters.update({s | bit: tp_swap(q, bit) for s, q in quarters.items()})
        bit //= 2

    tile = 512
    steps = width // tile
    up_scaled, *grads_a = pl.pallas_call(
        functools.partial(up_kernel, rep, cap, rank, tp, nb),
        out_shape=[struct((rows, depth), BF16), struct((per, width), F32)] + [struct((per, width), BF16)] * (rep - 1),
        grid=(steps,),
        in_specs=[SMEM, whole((rows, outs))]
        + [whole((depth, cols))] * tp
        + [pl.BlockSpec((rows, tile), lambda i: (0, i))],
        out_specs=[whole((rows, depth))] + [pl.BlockSpec((per, tile), lambda i: (0, i))] * rep,
        compiler_params=params(),
        cost_estimate=cost(2 * rows * depth * (width + outs), 2 * rows * (width + outs)),
        name="up_grad_a",
    )(vslot, upstream, *[quarters[s] for s in range(tp)], tokens_in)
    recv_ga = [grads_a[0]] + [rep_swap(grads_a[s], s) for s in range(1, rep)]

    blocks = 4
    down, a_all = pl.pallas_call(
        functools.partial(down_kernel, rep, cap, rank, blocks),
        out_shape=[struct((rank, rows), F32), struct((depth, width), BF16)],
        grid=(nb // blocks,),
        in_specs=[SMEM, pl.BlockSpec((blocks * BLOCK, width), lambda i: (i, 0))] + [whole((per, width))] * rep,
        out_specs=[pl.BlockSpec((rank, blocks * BLOCK), lambda i: (0, i)), whole((depth, width))],
        scratch_shapes=[pltpu.VMEM((blocks, depth, BLOCK), F32)],
        compiler_params=params(),
        cost_estimate=cost(2 * rows * depth * width, 2 * rows * width),
        name="down",
    )(vslot, tokens_in, *recv_a)
    bit = 1
    while 2 * bit < tp:
        down = down + tp_swap(down, bit)
        bit *= 2
    down_there = tp_swap(down, bit)

    half = steps // 2
    token_gradient = token_part(upstream, up_scaled, base_weight, a_all, tile, 0, half)
    token_gradient = token_part(upstream, up_scaled, base_weight, a_all, tile, half, steps - half, token_gradient)

    grads_b = pl.pallas_call(
        functools.partial(grad_b_kernel, rep, cap, rank, nb),
        out_shape=[struct((per, cols), F32)] + [struct((per, cols), F32)] * (rep - 1),
        in_specs=[SMEM, VMEM, VMEM, ANY],
        out_specs=[VMEM] * rep,
        scratch_shapes=[
            pltpu.VMEM((depth, rows), BF16),
            pltpu.VMEM((rows, cols), BF16),
            pltpu.SemaphoreType.DMA,
        ],
        compiler_params=params(),
        cost_estimate=cost(2 * rows * depth * cols, 2 * rows * cols),
        name="grad_b",
    )(vslot, down, down_there, upstream)
    recv_gb = [grads_b[0]] + [rep_swap(grads_b[s], s) for s in range(1, rep)]

    grad_a, grad_b = pl.pallas_call(
        functools.partial(finish_kernel, rep, cap, rank),
        out_shape=[struct((held, rank, width), F32), struct((held, rank, cols), F32)],
        in_specs=[SMEM] + [VMEM] * (2 * rep),
        out_specs=[VMEM] * 2,
        compiler_params=params(),
        cost_estimate=cost(0, 4 * held * rank * width),
        name="finish",
    )(pick, *recv_ga, *recv_gb)
    return token_gradient, grad_a, grad_b


def solution(mesh):
    in_specs = (
        P(("groups", "rep"), "tp"),
        P(("groups", "rep"), None),
        P("tp", None),
        P("rep", None, "tp"),
        P("rep", None, "tp"),
        P(("groups", "rep")),
        P(("groups", "rep"), None),
    )
    out_specs = (
        P(("groups", "rep"), "tp"),
        P(("groups", "rep"), None, "tp"),
        P(("groups", "rep"), None, "tp"),
    )
    return jax.shard_map(local, mesh=mesh, in_specs=in_specs, out_specs=out_specs, check_vma=False)
```

time: 152 us -> 70.9 us (0.47)
  matrix products: 51.6 us -> 0 us
  Pallas kernels: 0 us -> 34.4 us
  waiting for transfers between devices: 37.5 us -> 5.5 us
  blocking collectives: 18.5 us -> 0 us
  between operations: 14.2 us -> 0.77 us
  starting transfers between devices: 18 us -> 26.6 us
  local copies, waits for them, and re-layouts: 7.63 us -> 3.24 us
  other arithmetic: 3.45 us -> 0.02 us
    dot_general x14 -> x0, matrix products: 51.6 us -> none  [the longest x1 16.4 us: local(): lax.dot_general(upstream, base_weight, (((1,), (1,)), ((), ())), preferre...]
    pallas_call x0 -> x8, Pallas kernels: none -> 34.4 us  [the longest x2 16.6 us: token_part(): pl.pallas_call(functools.partial(token_kernel, before is not None, 512),...]
    psum x1 -> x0, waiting for transfers between devices: 30.7 us -> none  [local(): down_weight_complete = lax.psum(down_part, 'tp')]
    ppermute x0 -> x20, starting transfers between devices: none -> 26.6 us  [along(): return lax.ppermute(x, axis, [(i, i ^ s) for i in range(size)])]
    all_gather x2 -> x0, blocking collectives: 18.5 us -> none  [the longest x1 12.7 us: local(): all_lists = lax.all_gather(used_lists, 'rep', axis=0, tiled=True)]
    all_to_all x4 -> x0, starting transfers between devices: 18 us -> none  [the longest x1 5.09 us: local(): lax.all_to_all(outgoing_a, 'rep', split_axis=0, concat_axis=0, tiled=True)]
    all_to_all x4 -> x0, waiting for transfers between devices: 6.71 us -> none  [the longest x1 6.7 us: local(): lax.all_to_all(outgoing_a, 'rep', split_axis=0, concat_axis=0, tiled=True)]
    ppermute x0 -> x20, waiting for transfers between devices: none -> 5.5 us  [along(): return lax.ppermute(x, axis, [(i, i ^ s) for i in range(size)])]
  transfers between devices with their start and end apart: 5 -> 20, of which waited for: 2 -> 3; matrix products, arithmetic and copies ran while one was open for 31% -> 0% of each run, Pallas kernels for 0% -> 46%
where the time goes in v1:
time: 70.9 us; the launch traced here: 70.6 us
  Pallas kernels  34.4 us (49%)
  starting transfers between devices  26.6 us (38%)
  waiting for transfers between devices  5.5 us (8%)
  local copies, waits for them, and re-layouts  3.24 us (5%)
  between operations  0.77 us (1%)
    ppermute x20, starting transfers between devices, along(): return lax.ppermute(x, axis, [(i, i ^ s) for i in range(size)])  26.6 us
    pallas_call x2, Pallas kernels, token_part(): pl.pallas_call(functools.partial(token_kernel, before is not None, 512),...  16.6 us
    pallas_call x1, Pallas kernels, local(): pl.pallas_call(functools.partial(up_kernel, rep, cap, rank, tp, nb), out_...  6.32 us
    pallas_call x1, Pallas kernels, local(): pl.pallas_call(functools.partial(down_kernel, rep, cap, rank, blocks), ou...  5.8 us
    ppermute x20, waiting for transfers between devices, along(): return lax.ppermute(x, axis, [(i, i ^ s) for i in range(size)])  5.5 us
    unnamed x10, local copies, waits for them, and re-layouts  3.24 us
    pallas_call x1, Pallas kernels, local(): pl.pallas_call(functools.partial(pick_kernel, rep, cap, held, slots, nb),...  2.34 us
    pallas_call x1, Pallas kernels, local(): pl.pallas_call(functools.partial(finish_kernel, rep, cap, rank), out_shap...  1.76 us
  transfers between devices with their start and end apart: 20, of which 3 were waited for; matrix products, arithmetic and copies ran while one was open for 0% of the time, Pallas kernels for 46%

profile of v1, /device:TPU:0, one launch (start us, length us, event | category | flops | bytes accessed | tf_op | source)
XLA Modules:
  0.0 70.6 jit_solution(6601412023141896702)
XLA Ops:
  0.6 3.1 %collective-permute-start.3 = (bf16[128,256]{1,0:T(8,128)(2,1)}, bf16[128,256]{1,0:T(8,128)(2,1)S(1)}, u32[]{:S(2)}, u32[]{:S(2)}) collective-permute-start(bf16[128,256]{1,0:T(8,128)(2,1)} %bitcast.7), channel_id=1, source_target_pairs={{0,4},{4,0},{8,12},{12,8},{1,5},{5,1},{9,13},{13,9},{2,6},{6,2},{1... | collective-permute-start | bytes 196616 | tf_op jit(solution)/shard_map/ppermute | solution.py:234
  3.7 0.1 collective-permute-start
  3.8 3.0 %collective-permute-start.1 = (s32[1,8]{1,0:T(1,128)}, s32[1,8]{1,0:T(1,128)S(1)}, u32[]{:S(2)}, u32[]{:S(2)}) collective-permute-start(s32[1,8]{1,0:T(1,128)} %refs_0_.3), channel_id=1, source_target_pairs={{0,8},{4,12},{8,0},{12,4},{1,9},{5,13},{9,1},{13,5},{2,10},{6,14},... | collective-permute-start | bytes 104 | tf_op jit(solution)/shard_map/ppermute | solution.py:234
  6.8 1.3 %collective-permute-start.2 = (s32[1,8]{1,0:T(1,128)}, s32[1,8]{1,0:T(1,128)S(1)}, u32[]{:S(2)}, u32[]{:S(2)}) collective-permute-start(s32[1,8]{1,0:T(1,128)} %refs_0_.3), channel_id=1, source_target_pairs={{0,12},{4,8},{8,4},{12,0},{1,13},{5,9},{9,5},{13,1},{2,14},{6,10},... | collective-permute-start | bytes 104 | tf_op jit(solution)/shard_map/ppermute | solution.py:234
  8.1 1.7 %collective-permute-start.4 = (bf16[128,256]{1,0:T(8,128)(2,1)}, bf16[128,256]{1,0:T(8,128)(2,1)S(1)}, u32[]{:S(2)}, u32[]{:S(2)}) collective-permute-start(bf16[128,256]{1,0:T(8,128)(2,1)} %bitcast.8), channel_id=1, source_target_pairs={{0,8},{4,12},{8,0},{12,4},{1,9},{5,13},{9,1},{13,5},{2,10},{6,14},... | collective-permute-start | bytes 196616 | tf_op jit(solution)/shard_map/ppermute | solution.py:234
  9.8 0.0 collective-permute-done.refs_1_
  9.8 0.9 %collective-permute-start.5 = (bf16[128,256]{1,0:T(8,128)(2,1)}, bf16[128,256]{1,0:T(8,128)(2,1)S(1)}, u32[]{:S(2)}, u32[]{:S(2)}) collective-permute-start(bf16[128,256]{1,0:T(8,128)(2,1)} %bitcast.9), channel_id=1, source_target_pairs={{0,12},{4,8},{8,4},{12,0},{1,13},{5,9},{9,5},{13,1},{2,14},{6,10},... | collective-permute-start | bytes 196616 | tf_op jit(solution)/shard_map/ppermute | solution.py:234
  10.7 0.0 collective-permute-done.1.refs_2_
  10.7 1.5 %collective-permute-done.2.refs_3_ = s32[1,8]{1,0:T(1,128)S(1)} collective-permute-done((s32[1,8]{1,0:T(1,128)}, s32[1,8]{1,0:T(1,128)S(1)}, u32[]{:S(2)}, u32[]{:S(2)}) %collective-permute-start.2) | collective-permute-done | bytes 64 | tf_op jit(solution)/shard_map/ppermute | solution.py:234
  12.2 1.0 %copy-done.1 = bf16[8,16,2048]{2,1,0:T(8,128)(2,1)S(1)} copy-done((bf16[8,16,2048]{2,1,0:T(8,128)(2,1)S(1)}, bf16[8,16,2048]{2,1,0:T(8,128)(2,1)}, u32[]{:S(2)}) %copy-start.1) | copy-done | bytes 524312
  13.3 0.7 copy-done.3
  14.0 0.7 copy-done.4
  14.6 2.3 %pick.1 = (bf16[2,16,2048]{2,1,0:T(8,128)(2,1)S(1)}, bf16[2,16,2048]{2,1,0:T(8,128)(2,1)S(1)}, bf16[2,16,2048]{2,1,0:T(8,128)(2,1)S(1)}, bf16[2,16,2048]{2,1,0:T...) custom-call(s32[1,8]{1,0:T(1,128)S(1)} %copy-done.4, s32[1,8]{1,0:T(1,128)S(1)} %collective-permute-done.refs_1_, ...), custom_call_target="tpu_custom_call" | custom-call | bytes 1048576 | tf_op jit(solution)/shard_map/pick/pallas_call | solution.py:247
  17.0 0.1 collective-permute-start.9
  17.1 2.0 %collective-permute-start.10 = (bf16[32,2048]{1,0:T(8,128)(2,1)S(1)}, bf16[32,2048]{1,0:T(8,128)(2,1)S(1)}, u32[]{:S(2)}, u32[]{:S(2)}) collective-permute-start(bf16[32,2048]{1,0:T(8,128)(2,1)S(1)} %bitcast.13), channel_id=1, source_target_pairs={{0,8},{4,12},{8,0},{12,4},{1,9},{5,13},{9,1},{13,5},{2,10},{6,14},... | collective-permute-start | bytes 393224 | tf_op jit(solution)/shard_map/ppermute | solution.py:234
  19.1 2.4 %collective-permute-start.11 = (bf16[32,2048]{1,0:T(8,128)(2,1)S(1)}, bf16[32,2048]{1,0:T(8,128)(2,1)S(1)}, u32[]{:S(2)}, u32[]{:S(2)}) collective-permute-start(bf16[32,2048]{1,0:T(8,128)(2,1)S(1)} %bitcast.12), channel_id=1, source_target_pairs={{0,12},{4,8},{8,4},{12,0},{1,13},{5,9},{9,5},{13,1},{2,14},{6,10},... | collective-permute-start | bytes 393224 | tf_op jit(solution)/shard_map/ppermute | solution.py:234
  21.4 0.0 collective-permute-done.4.refs_3_
  21.4 0.0 collective-permute-done.5.refs_4_
  21.5 0.8 %copy-done.2 = bf16[8,16,256]{2,1,0:T(8,128)(2,1)S(1)} copy-done((bf16[8,16,256]{2,1,0:T(8,128)(2,1)S(1)}, bf16[8,16,256]{2,1,0:T(8,128)(2,1)}, u32[]{:S(2)}) %copy-start.2) | copy-done | bytes 65560
  22.3 0.5 select_b.1.refs_2_
  22.8 1.6 %collective-permute-start.7 = (bf16[128,256]{1,0:T(8,128)(2,1)S(1)}, bf16[128,256]{1,0:T(8,128)(2,1)S(1)}, u32[]{:S(2)}, u32[]{:S(2)}) collective-permute-start(bf16[128,256]{1,0:T(8,128)(2,1)S(1)} %select_b.1.refs_2_), channel_id=1, source_target_pairs={{0,2},{1,3},{2,0},{3,1},{4,6},{5,7},{6,4},{7,5},{8,10},{9,11},{10,... | collective-permute-start | bytes 196616 | tf_op jit(solution)/shard_map/ppermute | solution.py:234
  24.4 0.0 collective-permute-start.6
  24.4 2.8 %collective-permute-done.7.refs_4_ = bf16[128,256]{1,0:T(8,128)(2,1)S(1)} collective-permute-done((bf16[128,256]{1,0:T(8,128)(2,1)S(1)}, bf16[128,256]{1,0:T(8,128)(2,1)S(1)}, u32[]{:S(2)}, u32[]{:S(2)}) %collective-permute-start.7) | collective-permute-done | bytes 65568 | tf_op jit(solution)/shard_map/ppermute | solution.py:234
  27.2 0.0 collective-permute-start.8
  27.2 0.0 collective-permute-done.9.refs_3_
  27.2 1.2 %collective-permute-done.10.refs_4_ = bf16[32,2048]{1,0:T(8,128)(2,1)S(1)} collective-permute-done((bf16[32,2048]{1,0:T(8,128)(2,1)S(1)}, bf16[32,2048]{1,0:T(8,128)(2,1)S(1)}, u32[]{:S(2)}, u32[]{:S(2)}) %collective-permute-start.10) | collective-permute-done | bytes 131104 | tf_op jit(solution)/shard_map/ppermute | solution.py:234
  28.3 5.8 %down.1 = (f32[16,2048]{1,0:T(8,128)S(1)}, bf16[128,2048]{1,0:T(8,128)(2,1)S(1)}) custom-call(s32[16]{0:T(128)S(1)} %get-tuple-element.23.refs_0_, bf16[2048,2048]{1,0:T(8,128)(2,1)} %refs_1_.3, bf16[32,2048]{1,0:T(8,128)(2,1)S(1)} %bitcast.6, bf16[32,2048]{1,0:T(8,128)(2,1)S(1)} %collective-permute-done.9.refs_3_, ...), custom_call_target="tpu_custom_call" | custom-call | flops 1073741824 | bytes 8388608 | tf_op jit(solution)/shard_map/down/pallas_call | solution.py:294
  34.1 0.1 collective-permute-start.15
  34.2 0.0 collective-permute-done.8.refs_5_
  34.3 6.3 %up_grad_a.1 = (bf16[2048,128]{1,0:T(8,128)(2,1)S(1)}, f32[32,2048]{1,0:T(8,128)S(1)}, bf16[32,2048]{1,0:T(8,128)(2,1)S(1)}, bf16[32,2048]{1,0:T(8,128)(2,1)S(1)}, bf16[32,2048]{1,0:T(8,128)(2,1)S(1)}) custom-call(s32[16]{0:T(128)S(1)} %get-tuple-element.23.refs_0_, bf16[2048,1024]{1,0:T(8,128)(2,1)S(1)} %copy-done, bf16[128,256]{1,0:T(8,128)(2,1)S(1)} %select_b.1.refs_2_, ...), custom_call_target="tpu_custom_call" | custom-call | flops 1610612736 | bytes 12582912 | tf_op jit(solution)/shard_map/up_grad_a/pallas_call | solution.py:279
  40.6 2.0 %collective-permute-start.12 = (bf16[32,2048]{1,0:T(8,128)(2,1)S(1)}, bf16[32,2048]{1,0:T(8,128)(2,1)S(1)}, u32[]{:S(2)}, u32[]{:S(2)}) collective-permute-start(bf16[32,2048]{1,0:T(8,128)(2,1)S(1)} %get-tuple-element.33), channel_id=1, source_target_pairs={{0,4},{4,0},{8,12},{12,8},{1,5},{5,1},{9,13},{13,9},{2,6},{6,2},{1... | collective-permute-start | bytes 393224 | tf_op jit(solution)/shard_map/ppermute | solution.py:234
  42.6 0.4 collective-permute-start.13
  43.0 2.0 %collective-permute-start.14 = (bf16[32,2048]{1,0:T(8,128)(2,1)S(1)}, bf16[32,2048]{1,0:T(8,128)(2,1)S(1)}, u32[]{:S(2)}, u32[]{:S(2)}) collective-permute-start(bf16[32,2048]{1,0:T(8,128)(2,1)S(1)} %get-tuple-element.35), channel_id=1, source_target_pairs={{0,12},{4,8},{8,4},{12,0},{1,13},{5,9},{9,5},{13,1},{2,14},{6,10},... | collective-permute-start | bytes 393224 | tf_op jit(solution)/shard_map/ppermute | solution.py:234
  45.1 0.0 collective-permute-done.15
  45.1 1.6 %collective-permute-start.16 = (f32[16,2048]{1,0:T(8,128)S(1)}, f32[16,2048]{1,0:T(8,128)S(1)}, u32[]{:S(2)}, u32[]{:S(2)}) collective-permute-start(f32[16,2048]{1,0:T(8,128)S(1)} %add.3.refs_1_), channel_id=1, source_target_pairs={{0,2},{1,3},{2,0},{3,1},{4,6},{5,7},{6,4},{7,5},{8,10},{9,11},{10,... | collective-permute-start | bytes 393224 | tf_op jit(solution)/shard_map/ppermute | solution.py:234
  46.6 8.3 %token_gradient.2.refs_4_ = bf16[2048,2048]{1,0:T(8,128)(2,1)} custom-call(bf16[2048,1024]{1,0:T(8,128)(2,1)S(1)} %copy-done, bf16[2048,128]{1,0:T(8,128)(2,1)S(1)} %get-tuple-element.25.refs_1_, bf16[2048,1024]{1,0:T(8,128)(2,1)} %refs_2_.3, bf16[128,2048]{1,0:T(8,128)(2,1)S(1)} %get-tuple-element.30.refs_3_), custom_call_target="tpu_custom_call" | custom-call | flops 5368709120 | bytes 8388608 | tf_op jit(solution)/shard_map/token_gradient/pallas_call | solution.py:191
  55.0 0.0 collective-permute-done.16.refs_2_
  55.0 1.1 %grad_b.1 = (f32[32,256]{1,0:T(8,128)S(1)}, f32[32,256]{1,0:T(8,128)S(1)}, f32[32,256]{1,0:T(8,128)S(1)}, f32[32,256]{1,0:T(8,128)S(1)}) custom-call(s32[16]{0:T(128)S(1)} %get-tuple-element.23.refs_0_, f32[16,2048]{1,0:T(8,128)S(1)} %add.3.refs_1_, f32[16,2048]{1,0:T(8,128)S(1)} %collective-permute-done.16.refs_2_, bf16[2048,1024]{1,0:T(8,128)(2,1)S(1)} %copy-done), custom_call_target="tpu_custom_call" | custom-call | flops 134217728 | bytes 1048576 | tf_op jit(solution)/shard_map/grad_b/pallas_call | solution.py:315
  56.0 1.1 %collective-permute-start.17 = (f32[32,256]{1,0:T(8,128)S(1)}, f32[32,256]{1,0:T(8,128)S(1)}, u32[]{:S(2)}, u32[]{:S(2)}) collective-permute-start(f32[32,256]{1,0:T(8,128)S(1)} %get-tuple-element.38), channel_id=1, source_target_pairs={{0,4},{4,0},{8,12},{12,8},{1,5},{5,1},{9,13},{13,9},{2,6},{6,2},{1... | collective-permute-start | bytes 98312 | tf_op jit(solution)/shard_map/ppermute | solution.py:234
  57.1 1.3 %collective-permute-start.18 = (f32[32,256]{1,0:T(8,128)S(1)}, f32[32,256]{1,0:T(8,128)S(1)}, u32[]{:S(2)}, u32[]{:S(2)}) collective-permute-start(f32[32,256]{1,0:T(8,128)S(1)} %get-tuple-element.39), channel_id=1, source_target_pairs={{0,8},{4,12},{8,0},{12,4},{1,9},{5,13},{9,1},{13,5},{2,10},{6,14},... | collective-permute-start | bytes 98312 | tf_op jit(solution)/shard_map/ppermute | solution.py:234
  58.4 0.0 collective-permute-done.12.refs_2_
  58.4 2.0 %collective-permute-start.19 = (f32[32,256]{1,0:T(8,128)S(1)}, f32[32,256]{1,0:T(8,128)S(1)}, u32[]{:S(2)}, u32[]{:S(2)}) collective-permute-start(f32[32,256]{1,0:T(8,128)S(1)} %get-tuple-element.40), channel_id=1, source_target_pairs={{0,12},{4,8},{8,4},{12,0},{1,13},{5,9},{9,5},{13,1},{2,14},{6,10},... | collective-permute-start | bytes 98312 | tf_op jit(solution)/shard_map/ppermute | solution.py:234
  60.5 8.3 %token_gradient.3 = bf16[2048,2048]{1,0:T(8,128)(2,1)} custom-call(bf16[2048,1024]{1,0:T(8,128)(2,1)S(1)} %copy-done, bf16[2048,128]{1,0:T(8,128)(2,1)S(1)} %get-tuple-element.25.refs_1_, bf16[2048,1024]{1,0:T(8,128)(2,1)} %refs_2_.3, bf16[128,2048]{1,0:T(8,128)(2,1)S(1)} %get-tuple-element.30.refs_3_, ...), custom_call_target="tpu_custom_call", output_to_operand_aliasing={{}: (4, {})} | custom-call | flops 5368709120 | bytes 8388608 | tf_op jit(solution)/shard_map/token_gradient/pallas_call | solution.py:191
  68.8 0.0 collective-permute-done.13.refs_3_
  68.8 0.0 collective-permute-done.14.refs_4_
  68.8 0.0 collective-permute-done.17.refs_6_
  68.8 0.0 collective-permute-done.18.refs_7_
  68.8 1.8 %finish.1 = (f32[8,16,2048]{2,1,0:T(8,128)}, f32[8,16,256]{2,1,0:T(8,128)}) custom-call(s32[8]{0:T(128)S(1)} %get-tuple-element.31.refs_0_, f32[32,2048]{1,0:T(8,128)S(1)} %get-tuple-element.32.refs_1_, bf16[32,2048]{1,0:T(8,128)(2,1)S(1)} %collective-permute-done.12.refs_2_, bf16[32,2048]{1,0:T(8,128)(2,1)S(1)} %collective-permute-done.13.refs_3_, ...), custom_call_target="tpu_custom_call" | custom-call | bytes 1048576 | tf_op jit(solution)/shard_map/finish/pallas_call | solution.py:331
  (11 shorter events, 0.0 us)
Async XLA Ops:
  0.6 33.6 %copy-start = (bf16[2048,1024]{1,0:T(8,128)(2,1)S(1)}, bf16[2048,1024]{1,0:T(8,128)(2,1)}, u32[]{:S(2)}) copy-start(bf16[2048,1024]{1,0:T(8,128)(2,1)} %refs_3_.1) | copy-start | bytes 12582916
  0.6 18.4 %collective-permute-start.3 = (bf16[128,256]{1,0:T(8,128)(2,1)}, bf16[128,256]{1,0:T(8,128)(2,1)S(1)}, u32[]{:S(2)}, u32[]{:S(2)}) collective-permute-start(bf16[128,256]{1,0:T(8,128)(2,1)} %bitcast.7), channel_id=1, source_target_pairs={{0,4},{4,0},{8,12},{12,8},{1,5},{5,1},{9,13},{13,9},{2,6},{6,2},{1... | collective-permute-start | bytes 196616 | tf_op jit(solution)/shard_map/ppermute | solution.py:234
  3.7 6.1 %collective-permute-start = (s32[1,8]{1,0:T(1,128)}, s32[1,8]{1,0:T(1,128)S(1)}, u32[]{:S(2)}, u32[]{:S(2)}) collective-permute-start(s32[1,8]{1,0:T(1,128)} %refs_0_.3), channel_id=1, source_target_pairs={{0,4},{4,0},{8,12},{12,8},{1,5},{5,1},{9,13},{13,9},{2,6},{6,2},{1... | collective-permute-start | bytes 104 | tf_op jit(solution)/shard_map/ppermute | solution.py:234
  3.8 6.9 %collective-permute-start.1 = (s32[1,8]{1,0:T(1,128)}, s32[1,8]{1,0:T(1,128)S(1)}, u32[]{:S(2)}, u32[]{:S(2)}) collective-permute-start(s32[1,8]{1,0:T(1,128)} %refs_0_.3), channel_id=1, source_target_pairs={{0,8},{4,12},{8,0},{12,4},{1,9},{5,13},{9,1},{13,5},{2,10},{6,14},... | collective-permute-start | bytes 104 | tf_op jit(solution)/shard_map/ppermute | solution.py:234
  6.8 5.5 %collective-permute-start.2 = (s32[1,8]{1,0:T(1,128)}, s32[1,8]{1,0:T(1,128)S(1)}, u32[]{:S(2)}, u32[]{:S(2)}) collective-permute-start(s32[1,8]{1,0:T(1,128)} %refs_0_.3), channel_id=1, source_target_pairs={{0,12},{4,8},{8,4},{12,0},{1,13},{5,9},{9,5},{13,1},{2,14},{6,10},... | collective-permute-start | bytes 104 | tf_op jit(solution)/shard_map/ppermute | solution.py:234
  8.1 13.3 %collective-permute-start.4 = (bf16[128,256]{1,0:T(8,128)(2,1)}, bf16[128,256]{1,0:T(8,128)(2,1)S(1)}, u32[]{:S(2)}, u32[]{:S(2)}) collective-permute-start(bf16[128,256]{1,0:T(8,128)(2,1)} %bitcast.8), channel_id=1, source_target_pairs={{0,8},{4,12},{8,0},{12,4},{1,9},{5,13},{9,1},{13,5},{2,10},{6,14},... | collective-permute-start | bytes 196616 | tf_op jit(solution)/shard_map/ppermute | solution.py:234
  9.8 11.6 %collective-permute-start.5 = (bf16[128,256]{1,0:T(8,128)(2,1)}, bf16[128,256]{1,0:T(8,128)(2,1)S(1)}, u32[]{:S(2)}, u32[]{:S(2)}) collective-permute-start(bf16[128,256]{1,0:T(8,128)(2,1)} %bitcast.9), channel_id=1, source_target_pairs={{0,12},{4,8},{8,4},{12,0},{1,13},{5,9},{9,5},{13,1},{2,14},{6,10},... | collective-permute-start | bytes 196616 | tf_op jit(solution)/shard_map/ppermute | solution.py:234
  12.2 1.0 %copy-start.1 = (bf16[8,16,2048]{2,1,0:T(8,128)(2,1)S(1)}, bf16[8,16,2048]{2,1,0:T(8,128)(2,1)}, u32[]{:S(2)}) copy-start(bf16[8,16,2048]{2,1,0:T(8,128)(2,1)} %refs_5_.1) | copy-start | bytes 1572868
  13.3 0.7 copy-start.3
  14.0 0.7 copy-start.4
  17.0 10.2 %collective-permute-start.9 = (bf16[32,2048]{1,0:T(8,128)(2,1)S(1)}, bf16[32,2048]{1,0:T(8,128)(2,1)S(1)}, u32[]{:S(2)}, u32[]{:S(2)}) collective-permute-start(bf16[32,2048]{1,0:T(8,128)(2,1)S(1)} %bitcast.14), channel_id=1, source_target_pairs={{0,4},{4,0},{8,12},{12,8},{1,5},{5,1},{9,13},{13,9},{2,6},{6,2},{1... | collective-permute-start | bytes 393224 | tf_op jit(solution)/shard_map/ppermute | solution.py:234
  17.1 11.3 %collective-permute-start.10 = (bf16[32,2048]{1,0:T(8,128)(2,1)S(1)}, bf16[32,2048]{1,0:T(8,128)(2,1)S(1)}, u32[]{:S(2)}, u32[]{:S(2)}) collective-permute-start(bf16[32,2048]{1,0:T(8,128)(2,1)S(1)} %bitcast.13), channel_id=1, source_target_pairs={{0,8},{4,12},{8,0},{12,4},{1,9},{5,13},{9,1},{13,5},{2,10},{6,14},... | collective-permute-start | bytes 393224 | tf_op jit(solution)/shard_map/ppermute | solution.py:234
  19.1 9.3 %collective-permute-start.11 = (bf16[32,2048]{1,0:T(8,128)(2,1)S(1)}, bf16[32,2048]{1,0:T(8,128)(2,1)S(1)}, u32[]{:S(2)}, u32[]{:S(2)}) collective-permute-start(bf16[32,2048]{1,0:T(8,128)(2,1)S(1)} %bitcast.12), channel_id=1, source_target_pairs={{0,12},{4,8},{8,4},{12,0},{1,13},{5,9},{9,5},{13,1},{2,14},{6,10},... | collective-permute-start | bytes 393224 | tf_op jit(solution)/shard_map/ppermute | solution.py:234
  21.4 0.8 %copy-start.2 = (bf16[8,16,256]{2,1,0:T(8,128)(2,1)S(1)}, bf16[8,16,256]{2,1,0:T(8,128)(2,1)}, u32[]{:S(2)}) copy-start(bf16[8,16,256]{2,1,0:T(8,128)(2,1)} %param.11) | copy-start | bytes 196612
  22.8 4.3 %collective-permute-start.7 = (bf16[128,256]{1,0:T(8,128)(2,1)S(1)}, bf16[128,256]{1,0:T(8,128)(2,1)S(1)}, u32[]{:S(2)}, u32[]{:S(2)}) collective-permute-start(bf16[128,256]{1,0:T(8,128)(2,1)S(1)} %select_b.1.refs_2_), channel_id=1, source_target_pairs={{0,2},{1,3},{2,0},{3,1},{4,6},{5,7},{6,4},{7,5},{8,10},{9,11},{10,... | collective-permute-start | bytes 196616 | tf_op jit(solution)/shard_map/ppermute | solution.py:234
  24.4 9.8 %collective-permute-start.6 = (bf16[128,256]{1,0:T(8,128)(2,1)S(1)}, bf16[128,256]{1,0:T(8,128)(2,1)S(1)}, u32[]{:S(2)}, u32[]{:S(2)}) collective-permute-start(bf16[128,256]{1,0:T(8,128)(2,1)S(1)} %select_b.1.refs_2_), channel_id=1, source_target_pairs={{0,1},{1,0},{2,3},{3,2},{4,5},{5,4},{6,7},{7,6},{8,9},{9,8},{10,11... | collective-permute-start | bytes 196616 | tf_op jit(solution)/shard_map/ppermute | solution.py:234
  27.2 7.1 %collective-permute-start.8 = (bf16[128,256]{1,0:T(8,128)(2,1)S(1)}, bf16[128,256]{1,0:T(8,128)(2,1)S(1)}, u32[]{:S(2)}, u32[]{:S(2)}) collective-permute-start(bf16[128,256]{1,0:T(8,128)(2,1)S(1)} %collective-permute-done.7.refs_4_), channel_id=1, source_target_pairs={{0,1},{1,0},{2,3},{3,2},{4,5},{5,4},{6,7},{7,6},{8,9},{9,8},{10,11... | collective-permute-start | bytes 196616 | tf_op jit(solution)/shard_map/ppermute | solution.py:234
  34.1 10.9 %collective-permute-start.15 = (f32[16,2048]{1,0:T(8,128)S(1)}, f32[16,2048]{1,0:T(8,128)S(1)}, u32[]{:S(2)}, u32[]{:S(2)}) collective-permute-start(f32[16,2048]{1,0:T(8,128)S(1)} %get-tuple-element.36), channel_id=1, source_target_pairs={{0,1},{1,0},{2,3},{3,2},{4,5},{5,4},{6,7},{7,6},{8,9},{9,8},{10,11... | collective-permute-start | bytes 393224 | tf_op jit(solution)/shard_map/ppermute | solution.py:234
  40.6 17.9 %collective-permute-start.12 = (bf16[32,2048]{1,0:T(8,128)(2,1)S(1)}, bf16[32,2048]{1,0:T(8,128)(2,1)S(1)}, u32[]{:S(2)}, u32[]{:S(2)}) collective-permute-start(bf16[32,2048]{1,0:T(8,128)(2,1)S(1)} %get-tuple-element.33), channel_id=1, source_target_pairs={{0,4},{4,0},{8,12},{12,8},{1,5},{5,1},{9,13},{13,9},{2,6},{6,2},{1... | collective-permute-start | bytes 393224 | tf_op jit(solution)/shard_map/ppermute | solution.py:234
  42.6 26.2 %collective-permute-start.13 = (bf16[32,2048]{1,0:T(8,128)(2,1)S(1)}, bf16[32,2048]{1,0:T(8,128)(2,1)S(1)}, u32[]{:S(2)}, u32[]{:S(2)}) collective-permute-start(bf16[32,2048]{1,0:T(8,128)(2,1)S(1)} %get-tuple-element.34), channel_id=1, source_target_pairs={{0,8},{4,12},{8,0},{12,4},{1,9},{5,13},{9,1},{13,5},{2,10},{6,14},... | collective-permute-start | bytes 393224 | tf_op jit(solution)/shard_map/ppermute | solution.py:234
  43.0 25.8 %collective-permute-start.14 = (bf16[32,2048]{1,0:T(8,128)(2,1)S(1)}, bf16[32,2048]{1,0:T(8,128)(2,1)S(1)}, u32[]{:S(2)}, u32[]{:S(2)}) collective-permute-start(bf16[32,2048]{1,0:T(8,128)(2,1)S(1)} %get-tuple-element.35), channel_id=1, source_target_pairs={{0,12},{4,8},{8,4},{12,0},{1,13},{5,9},{9,5},{13,1},{2,14},{6,10},... | collective-permute-start | bytes 393224 | tf_op jit(solution)/shard_map/ppermute | solution.py:234
  45.1 9.9 %collective-permute-start.16 = (f32[16,2048]{1,0:T(8,128)S(1)}, f32[16,2048]{1,0:T(8,128)S(1)}, u32[]{:S(2)}, u32[]{:S(2)}) collective-permute-start(f32[16,2048]{1,0:T(8,128)S(1)} %add.3.refs_1_), channel_id=1, source_target_pairs={{0,2},{1,3},{2,0},{3,1},{4,6},{5,7},{6,4},{7,5},{8,10},{9,11},{10,... | collective-permute-start | bytes 393224 | tf_op jit(solution)/shard_map/ppermute | solution.py:234
  56.0 12.8 %collective-permute-start.17 = (f32[32,256]{1,0:T(8,128)S(1)}, f32[32,256]{1,0:T(8,128)S(1)}, u32[]{:S(2)}, u32[]{:S(2)}) collective-permute-start(f32[32,256]{1,0:T(8,128)S(1)} %get-tuple-element.38), channel_id=1, source_target_pairs={{0,4},{4,0},{8,12},{12,8},{1,5},{5,1},{9,13},{13,9},{2,6},{6,2},{1... | collective-permute-start | bytes 98312 | tf_op jit(solution)/shard_map/ppermute | solution.py:234
  57.1 11.7 %collective-permute-start.18 = (f32[32,256]{1,0:T(8,128)S(1)}, f32[32,256]{1,0:T(8,128)S(1)}, u32[]{:S(2)}, u32[]{:S(2)}) collective-permute-start(f32[32,256]{1,0:T(8,128)S(1)} %get-tuple-element.39), channel_id=1, source_target_pairs={{0,8},{4,12},{8,0},{12,4},{1,9},{5,13},{9,1},{13,5},{2,10},{6,14},... | collective-permute-start | bytes 98312 | tf_op jit(solution)/shard_map/ppermute | solution.py:234
  58.4 10.4 %collective-permute-start.19 = (f32[32,256]{1,0:T(8,128)S(1)}, f32[32,256]{1,0:T(8,128)S(1)}, u32[]{:S(2)}, u32[]{:S(2)}) collective-permute-start(f32[32,256]{1,0:T(8,128)S(1)} %get-tuple-element.40), channel_id=1, source_target_pairs={{0,12},{4,8},{8,4},{12,0},{1,13},{5,9},{9,5},{13,1},{2,14},{6,10},... | collective-permute-start | bytes 98312 | tf_op jit(solution)/shard_map/ppermute | solution.py:234

commit v2 on v0

v2 whole, which is shorter than its diff:
```python
import functools

import jax
import jax.numpy as jnp
from jax import lax
from jax.experimental import pallas as pl
from jax.experimental.pallas import tpu as pltpu
from jax.sharding import PartitionSpec as P

BLOCK = 128
SCALE = 2.0
VMEM_LIMIT = 12 * 1024 * 1024

F32 = jnp.float32
BF16 = jnp.bfloat16
I32 = jnp.int32
ANY = pl.BlockSpec(memory_space=pl.ANY)
HBM = pl.BlockSpec(memory_space=pltpu.HBM)
SMEM = pl.BlockSpec(memory_space=pltpu.SMEM)
VMEM = pl.BlockSpec(memory_space=pltpu.VMEM)
NT = (((1,), (1,)), ((), ()))
TN = (((0,), (0,)), ((), ()))
struct = jax.ShapeDtypeStruct


def in_hbm(x):
    return pltpu.with_memory_space_constraint(x, pltpu.HBM)


def kernel(body, name, outs, in_specs, out_specs, args, scratch=()):
    return pl.pallas_call(
        body,
        out_shape=outs,
        in_specs=in_specs,
        out_specs=out_specs,
        scratch_shapes=list(scratch),
        compiler_params=pltpu.CompilerParams(vmem_limit_bytes=VMEM_LIMIT),
        cost_estimate=pl.CostEstimate(flops=0, bytes_accessed=0, transcendentals=0),
        name=name,
    )(*args)


def start_all(copies):
    for copy in copies:
        copy.start()
    return copies


def wait_all(copies):
    for copy in copies:
        copy.wait()


def split(ident, held):
    if held & (held - 1) == 0:
        shift = held.bit_length() - 1
        return lax.shift_right_logical(ident, I32(shift)), jnp.bitwise_and(ident, I32(held - 1))
    return lax.div(ident, I32(held)), lax.rem(ident, I32(held))


def plan_kernel(cap, held, my_list, slot_ids, bank_a, bank_b, vslot, bank, lists, ids, place_v, sems):
    slots = lists.shape[1]
    width = bank_a.shape[1]
    copies = start_all(
        [
            pltpu.make_async_copy(my_list, lists, sems.at[0]),
            pltpu.make_async_copy(slot_ids, ids, sems.at[1]),
            pltpu.make_async_copy(bank_a, bank.at[:, pl.ds(0, width)], sems.at[2]),
            pltpu.make_async_copy(bank_b, bank.at[:, pl.ds(width, bank_b.shape[1])], sems.at[3]),
        ]
    )
    me = lax.axis_index("rep")
    copies[0].wait()
    owners = [split(lists[0, k], held)[0] for k in range(slots)]
    for k in range(slots):
        place = I32(0)
        for j in range(k):
            place = place + (owners[j] == owners[k]).astype(I32)
        place_v[k] = jnp.bitwise_xor(owners[k], me) * cap + place
    copies[1].wait()
    for b in range(vslot.shape[0]):
        vslot[b] = place_v[ids[b, 0]]
    wait_all(copies[2:])


def pick_kernel(rep, cap, held, *refs):
    sources = refs[:rep]
    bank = refs[rep]
    outs = refs[rep + 1 : 2 * rep + 1]
    pick = refs[2 * rep + 1]
    lists = refs[2 * rep + 2 : 3 * rep + 2]
    sems = refs[3 * rep + 2]
    rank = outs[0].shape[0] // cap
    slots = lists[0].shape[1]
    me = lax.axis_index("rep")
    loads = start_all([pltpu.make_async_copy(sources[s], lists[s], sems.at[s]) for s in range(rep)])
    wait_all(loads)
    for s in range(rep):
        count = I32(0)
        idx = [I32(-1)] * cap
        for k in range(slots):
            owner, number = split(lists[s][0, k], held)
            mine = owner == me
            for c in range(cap):
                idx[c] = jnp.where(mine & (count == c), number, idx[c])
            count = count + mine.astype(I32)
        for c in range(cap):
            pick[s * cap + c] = idx[c]
            start = pl.multiple_of(jnp.maximum(idx[c], 0) * rank, rank)
            outs[s][c * rank : (c + 1) * rank, :] = bank[pl.ds(start, rank), :]


def frozen_kernel(chunk, tile, upstream, weight, tokens, after, out, upstream_v, tokens_v, weight_v, sems):
    del after
    rows = upstream.shape[0]
    width = weight.shape[0]
    n_rows, n_cols = rows // chunk, width // tile

    def fetch(source, to, i, size, sem):
        at = pl.ds(i * size, size)
        return pltpu.make_async_copy(source.at[at, :], to.at[at, :], sems.at[sem])

    weights = [fetch(weight, weight_v, t, tile, t) for t in range(n_cols)]
    ups = [fetch(upstream, upstream_v, r, chunk, n_cols + r) for r in range(n_rows)]
    toks = [fetch(tokens, tokens_v, r, chunk, n_cols + n_rows + r) for r in range(n_rows)]
    start_all(weights[:1] + ups + weights[1:] + toks)
    for t in range(n_cols):
        weights[t].wait()
        cols = slice(t * tile, (t + 1) * tile)
        for r in range(n_rows):
            if t == 0:
                ups[r].wait()
            at = slice(r * chunk, (r + 1) * chunk)
            out[at, cols] = lax.dot_general(
                upstream_v[at, :], weight_v[cols, :], NT, preferred_element_type=F32
            )
    wait_all(toks)


def up_kernel(rep, cap, rank, nb, order, *refs):
    vslot, upstream, held_q, came_q, tokens = refs[:5]
    up_out = refs[6]
    grads = refs[7:]
    width = rep * cap * rank
    per = cap * rank
    cols = held_q.shape[1]
    tp_rank = lax.axis_index("tp")
    chunk = 4
    lane_slot = lax.broadcasted_iota(I32, (BLOCK, width), 1) // rank
    for r in range(nb // chunk):
        rows = slice(r * chunk * BLOCK, (r + 1) * chunk * BLOCK)
        acc = None
        for i, s in enumerate(order):
            for j, piece in ((0, held_q), (1, came_q)):
                at = pl.multiple_of(jnp.bitwise_xor(tp_rank, s ^ j) * cols, cols)
                part = lax.dot_general(
                    upstream[rows, pl.ds(at, cols)],
                    piece[i * width : (i + 1) * width, :],
                    NT,
                    preferred_element_type=F32,
                )
                acc = part if acc is None else acc + part
        acc = (SCALE * acc).astype(BF16)
        for b in range(chunk):
            blk = r * chunk + b
            part = acc[b * BLOCK : (b + 1) * BLOCK, :]
            up_out[blk * BLOCK : (blk + 1) * BLOCK, :] = jnp.where(
                lane_slot == vslot[blk], part, jnp.zeros_like(part)
            )
    tile = 512
    for t in range(tokens.shape[1] // tile):
        at = slice(t * tile, (t + 1) * tile)
        grad = lax.dot_general(up_out[...], tokens[:, at], TN, preferred_element_type=F32)
        for s in range(rep):
            grads[s][:, at] = grad[s * per : (s + 1) * per, :].astype(grads[s].dtype)


def down_kernel(rep, cap, rank, nb, *refs):
    vslot, tokens = refs[:2]
    parts = refs[2 : 2 + rep]
    down, a_all = refs[3 + rep : 5 + rep]
    turned = refs[5 + rep]
    per = cap * rank
    width = a_all.shape[1]
    for s in range(rep):
        a_all[s * per : (s + 1) * per, :] = parts[s][:, :width]
    chunk = 4
    for r in range(nb // chunk):
        prod = lax.dot_general(
            tokens[r * chunk * BLOCK : (r + 1) * chunk * BLOCK, :], a_all[...], NT, preferred_element_type=F32
        )
        for b in range(chunk):
            turned[r * chunk + b] = prod[b * BLOCK : (b + 1) * BLOCK, :].T
    for b in range(nb):
        start = pl.multiple_of(vslot[b] * rank, rank)
        down[:, b * BLOCK : (b + 1) * BLOCK] = turned[b, pl.ds(start, rank), :]


def grad_b_kernel(rep, cap, rank, nb, *refs):
    vslot, down_here, down_there, upstream = refs[:4]
    grads = refs[5:-1]
    spread = refs[-1]
    per = cap * rank
    cols = grads[0].shape[1]
    at = pl.multiple_of(lax.axis_index("tp") * cols, cols)
    spread[...] = jnp.zeros_like(spread)
    total = (SCALE * (down_here[...] + down_there[...])).astype(BF16)
    for b in range(nb):
        start = pl.multiple_of(vslot[b] * rank, rank)
        spread[pl.ds(start, rank), b * BLOCK : (b + 1) * BLOCK] = total[:, b * BLOCK : (b + 1) * BLOCK]
    grad = jnp.dot(spread[...], upstream[:, pl.ds(at, cols)], preferred_element_type=F32)
    for s in range(rep):
        grads[s][...] = grad[s * per : (s + 1) * per, :].astype(grads[s].dtype)


def token_kernel(chunk, tile, *refs):
    frozen, up_scaled, a_all = refs[:3]
    out, buf, sems = refs[-3:]
    rows, width = frozen.shape
    pending = {}
    for t in range(width // tile):
        slot = t % 2
        cols = slice(t * tile, (t + 1) * tile)
        for r in range(rows // chunk):
            at = slice(r * chunk, (r + 1) * chunk)
            if (slot, r) in pending:
                pending.pop((slot, r)).wait()
            low = jnp.dot(up_scaled[at, :], a_all[:, cols], preferred_element_type=F32)
            buf[slot, at, :] = (frozen[at, cols] + low).astype(BF16)
            copy = pltpu.make_async_copy(
                buf.at[slot, pl.ds(r * chunk, chunk), :],
                out.at[pl.ds(r * chunk, chunk), pl.ds(t * tile, tile)],
                sems.at[slot, r],
            )
            copy.start()
            pending[slot, r] = copy
    wait_all(pending.values())


def finish_kernel(rep, cap, rank, *refs):
    pick = refs[0]
    in_a = refs[1 : 1 + rep]
    in_b = refs[1 + rep : 1 + 2 * rep]
    out_a, out_b, sum_a, sum_b, sem = refs[2 + 2 * rep :]
    sum_a[...] = jnp.zeros_like(sum_a)
    sum_b[...] = jnp.zeros_like(sum_b)
    for s in range(rep):
        for c in range(cap):
            to = pick[s * cap + c]

            @pl.when(to >= 0)
            def _():
                sum_a[to] += in_a[s][c * rank : (c + 1) * rank, :].astype(F32)
                sum_b[to] += in_b[s][c * rank : (c + 1) * rank, :].astype(F32)

    wait_all(
        start_all(
            [pltpu.make_async_copy(sum_a, out_a, sem.at[0]), pltpu.make_async_copy(sum_b, out_b, sem.at[1])]
        )
    )


def local(tokens_in, upstream, base_weight, bank_a, bank_b, slot_ids, used_lists):
    rows, width = tokens_in.shape
    outs = upstream.shape[1]
    held, rank, cols = bank_b.shape
    slots = used_lists.shape[1]
    nb = rows // BLOCK
    rep = lax.axis_size("rep")
    tp = lax.axis_size("tp")
    cap = (slots + rep - 1) // rep
    per = cap * rank
    depth = rep * per
    tile = chunk = 512
    tie = lax.optimization_barrier

    def swap(axis, x, s):
        return lax.ppermute(x, axis, [(i, i ^ s) for i in range(lax.axis_size(axis))])

    def bits(n):
        return [1 << i for i in range(n.bit_length() - 1)]

    a_flat = in_hbm(bank_a.reshape(held * rank, width))
    b_flat = in_hbm(bank_b.reshape(held * rank, cols))
    vslot, bank = kernel(
        functools.partial(plan_kernel, cap, held),
        "plan",
        [struct((nb,), I32), pltpu.VMEM((held * rank, width + cols), BF16)],
        [HBM, HBM, HBM, HBM],
        [SMEM, VMEM],
        [in_hbm(used_lists), in_hbm(slot_ids.reshape(nb, BLOCK)), a_flat, b_flat],
        [
            pltpu.SMEM((1, slots), I32),
            pltpu.SMEM((nb, BLOCK), I32),
            pltpu.SMEM((slots,), I32),
            pltpu.SemaphoreType.DMA((4,)),
        ],
    )

    lists = tie((*[swap("rep", used_lists, s) for s in range(1, rep)], vslot, bank))
    *sends, pick = kernel(
        functools.partial(pick_kernel, rep, cap, held),
        "pick",
        [struct((per, width + cols), BF16)] * rep + [struct((rep * cap,), I32)],
        [ANY] * rep + [VMEM],
        [VMEM] * rep + [SMEM],
        [used_lists, *lists[: rep - 1], lists[rep]],
        [pltpu.SMEM((1, slots), I32)] * rep + [pltpu.SemaphoreType.DMA((rep,))],
    )
    vslot = lists[rep - 1]
    fetched = {s: swap("rep", sends[s], s) for s in range(rep - 1, 0, -1)}
    fetched[0] = sends[0]

    n_fetch = width // tile + 2 * (rows // chunk)
    frozen, upstream_v, tokens_v = kernel(
        functools.partial(frozen_kernel, chunk, tile),
        "frozen",
        [pltpu.VMEM((rows, width), F32), pltpu.VMEM((rows, outs), BF16), pltpu.VMEM((rows, width), BF16)],
        [HBM, HBM, HBM, ANY],
        [VMEM, VMEM, VMEM],
        [in_hbm(upstream), in_hbm(base_weight), in_hbm(tokens_in), sends[0]],
        [pltpu.VMEM((width, outs), BF16), pltpu.SemaphoreType.DMA((n_fetch,))],
    )
    *fetched, upstream_v, tokens_v, frozen = tie(
        (*[fetched[s] for s in range(rep)], upstream_v, tokens_v, frozen)
    )

    quarter = jnp.concatenate([x[:, width:] for x in fetched], axis=0)
    down, a_all = kernel(
        functools.partial(down_kernel, rep, cap, rank, nb),
        "down",
        [struct((rank, rows), F32), struct((depth, width), BF16)],
        [SMEM, VMEM] + [VMEM] * rep + [ANY],
        [VMEM, VMEM],
        [vslot, tokens_v, *fetched, quarter],
        [pltpu.VMEM((nb, depth, BLOCK), F32)],
    )
    held_q, came_q, order = quarter, None, [0]
    for bit in bits(tp)[::-1]:
        if came_q is not None:
            held_q = jnp.concatenate([held_q, came_q], axis=0)
            order += [s ^ (2 * bit) for s in order]
        came_q = swap("tp", held_q, bit)
        if bit == tp // 2:
            came_q, down = tie((came_q, down))
    for bit in bits(tp)[:-1]:
        down = down + swap("tp", down, bit)
    down_there = swap("tp", down, tp // 2)

    up_scaled, *grads_a = kernel(
        functools.partial(up_kernel, rep, cap, rank, nb, order),
        "up_grad_a",
        [struct((rows, depth), BF16), struct((per, width), F32)] + [struct((per, width), BF16)] * (rep - 1),
        [SMEM] + [VMEM] * 4 + [ANY],
        [VMEM] * (rep + 1),
        [vslot, upstream_v, held_q, came_q, tokens_v, down],
    )
    recv_ga = {s: swap("rep", grads_a[s], s) for s in range(rep - 1, 0, -1)}
    recv_ga[0] = grads_a[0]

    grads_b = kernel(
        functools.partial(grad_b_kernel, rep, cap, rank, nb),
        "grad_b",
        [struct((per, cols), F32)] + [struct((per, cols), BF16)] * (rep - 1),
        [SMEM, VMEM, VMEM, VMEM, ANY],
        [VMEM] * rep,
        [vslot, down, down_there, upstream_v, up_scaled],
        [pltpu.VMEM((depth, rows), BF16)],
    )
    recv_gb = {s: swap("rep", grads_b[s], s) for s in range(rep - 1, 0, -1)}
    recv_gb[0] = grads_b[0]

    token_gradient = kernel(
        functools.partial(token_kernel, chunk, tile),
        "token_gradient",
        pltpu.HBM((rows, width), BF16),
        [VMEM] * 3 + [ANY],
        HBM,
        [frozen, up_scaled, a_all, grads_b[0]],
        [pltpu.VMEM((2, rows, tile), BF16), pltpu.SemaphoreType.DMA((2, rows // chunk))],
    )

    grad_a, grad_b = kernel(
        functools.partial(finish_kernel, rep, cap, rank),
        "finish",
        [pltpu.HBM((held, rank, width), F32), pltpu.HBM((held, rank, cols), F32)],
        [SMEM] + [VMEM] * (2 * rep) + [HBM],
        [HBM] * 2,
        [pick, *[recv_ga[s] for s in range(rep)], *[recv_gb[s] for s in range(rep)], in_hbm(token_gradient)],
        [
            pltpu.VMEM((held, rank, width), F32),
            pltpu.VMEM((held, rank, cols), F32),
            pltpu.SemaphoreType.DMA((2,)),
        ],
    )
    return token_gradient, grad_a, grad_b


def solution(mesh):
    in_specs = (
        P(("groups", "rep"), "tp"),
        P(("groups", "rep"), None),
        P("tp", None),
        P("rep", None, "tp"),
        P("rep", None, "tp"),
        P(("groups", "rep")),
        P(("groups", "rep"), None),
    )
    out_specs = (
        P(("groups", "rep"), "tp"),
        P(("groups", "rep"), None, "tp"),
        P(("groups", "rep"), None, "tp"),
    )
    return jax.shard_map(local, mesh=mesh, in_specs=in_specs, out_specs=out_specs, check_vma=False)
```

time: 152 us -> 57.3 us (0.38)
  matrix products: 51.6 us -> 0 us
  waiting for transfers between devices: 37.5 us -> 4.96 us
  Pallas kernels: 0 us -> 28.1 us
  blocking collectives: 18.5 us -> 0 us
  between operations: 14.2 us -> 1 us
  local copies, waits for them, and re-layouts: 7.63 us -> 0.68 us
  starting transfers between devices: 18 us -> 22.4 us
  other arithmetic: 3.45 us -> 0.02 us
    dot_general x14 -> x0, matrix products: 51.6 us -> none  [the longest x1 16.4 us: local(): lax.dot_general(upstream, base_weight, (((1,), (1,)), ((), ())), preferre...]
    psum x1 -> x0, waiting for transfers between devices: 30.7 us -> none  [local(): down_weight_complete = lax.psum(down_part, 'tp')]
    pallas_call x0 -> x8, Pallas kernels: none -> 28.1 us  [kernel(): pl.pallas_call(body, out_shape=outs, in_specs=in_specs, out_specs=out_spe...]
    ppermute x0 -> x16, starting transfers between devices: none -> 22.4 us  [swap(): lax.ppermute(x, axis, [(i, i ^ s) for i in range(lax.axis_size(axis))])]
    all_gather x2 -> x0, blocking collectives: 18.5 us -> none  [the longest x1 12.7 us: local(): all_lists = lax.all_gather(used_lists, 'rep', axis=0, tiled=True)]
    all_to_all x4 -> x0, starting transfers between devices: 18 us -> none  [the longest x1 5.09 us: local(): lax.all_to_all(outgoing_a, 'rep', split_axis=0, concat_axis=0, tiled=True)]
    all_to_all x4 -> x0, waiting for transfers between devices: 6.71 us -> none  [the longest x1 6.7 us: local(): lax.all_to_all(outgoing_a, 'rep', split_axis=0, concat_axis=0, tiled=True)]
    ppermute x0 -> x16, waiting for transfers between devices: none -> 4.96 us  [swap(): lax.ppermute(x, axis, [(i, i ^ s) for i in range(lax.axis_size(axis))])]
  transfers between devices with their start and end apart: 5 -> 16, of which waited for: 2 -> 4; matrix products, arithmetic and copies ran while one was open for 31% -> 0% of each run, Pallas kernels for 0% -> 44%
where the time goes in v2:
time: 57.3 us; the launch traced here: 57.1 us
  Pallas kernels  28.1 us (49%)
  starting transfers between devices  22.4 us (39%)
  waiting for transfers between devices  4.96 us (9%)
  between operations  1 us (2%)
  local copies, waits for them, and re-layouts  0.68 us (1%)
    pallas_call x8, Pallas kernels, kernel(): pl.pallas_call(body, out_shape=outs, in_specs=in_specs, out_specs=out_spe...  28.1 us
    ppermute x16, starting transfers between devices, swap(): lax.ppermute(x, axis, [(i, i ^ s) for i in range(lax.axis_size(axis))])  22.4 us
    ppermute x16, waiting for transfers between devices, swap(): lax.ppermute(x, axis, [(i, i ^ s) for i in range(lax.axis_size(axis))])  4.96 us
  transfers between devices with their start and end apart: 16, of which 4 were waited for; matrix products, arithmetic and copies ran while one was open for 0% of the time, Pallas kernels for 44%

profile of v2, /device:TPU:0, one launch (start us, length us, event | category | flops | bytes accessed | tf_op | source)
XLA Modules:
  0.0 57.1 jit_solution(2821039849134728985)
XLA Ops:
  0.6 5.1 %collective-permute-start.2 = (s32[1,8]{1,0:T(1,128)}, s32[1,8]{1,0:T(1,128)S(1)}, u32[]{:S(2)}, u32[]{:S(2)}) collective-permute-start(s32[1,8]{1,0:T(1,128)} %refs_0_.1), channel_id=1, source_target_pairs={{0,12},{4,8},{8,4},{12,0},{1,13},{5,9},{9,5},{13,1},{2,14},{6,10},... | collective-permute-start | bytes 104 | tf_op jit(solution)/shard_map/ppermute | solution.py:278
  5.7 0.0 collective-permute-start.1
  5.7 0.6 %collective-permute-start = (s32[1,8]{1,0:T(1,128)}, s32[1,8]{1,0:T(1,128)S(1)}, u32[]{:S(2)}, u32[]{:S(2)}) collective-permute-start(s32[1,8]{1,0:T(1,128)} %refs_0_.1), channel_id=1, source_target_pairs={{0,4},{4,0},{8,12},{12,8},{1,5},{5,1},{9,13},{13,9},{2,6},{6,2},{1... | collective-permute-start | bytes 104 | tf_op jit(solution)/shard_map/ppermute | solution.py:278
  6.4 1.7 %plan.1 = (s32[16]{0:T(128)S(1)}, bf16[128,2304]{1,0:T(8,128)(2,1)S(1)}) custom-call(s32[1,8]{1,0:T(1,128)} %refs_0_.1, s32[16,128]{1,0:T(8,128)} %bitcast.5, bf16[128,2048]{1,0:T(8,128)(2,1)} %bitcast.3, bf16[128,256]{1,0:T(8,128)(2,1)} %bitcast.4), custom_call_target="tpu_custom_call" | custom-call | tf_op jit(solution)/shard_map/plan/pallas_call | solution.py:31
  8.1 0.0 collective-permute-done.2.refs_3_
  8.1 2.2 %collective-permute-done.1.refs_2_ = s32[1,8]{1,0:T(1,128)S(1)} collective-permute-done((s32[1,8]{1,0:T(1,128)}, s32[1,8]{1,0:T(1,128)S(1)}, u32[]{:S(2)}, u32[]{:S(2)}) %collective-permute-start.1) | collective-permute-done | bytes 64 | tf_op jit(solution)/shard_map/ppermute | solution.py:278
  10.3 0.0 collective-permute-done.refs_1_
  10.3 0.0 copy-start
  10.3 0.7 %copy-done = s32[1,8]{1,0:T(1,128)S(1)} copy-done((s32[1,8]{1,0:T(1,128)S(1)}, s32[1,8]{1,0:T(1,128)}, u32[]{:S(2)}) %copy-start) | copy-done | bytes 56
  11.0 1.3 %pick.1 = (bf16[32,2304]{1,0:T(8,128)(2,1)S(1)}, bf16[32,2304]{1,0:T(8,128)(2,1)S(1)}, bf16[32,2304]{1,0:T(8,128)(2,1)S(1)}, bf16[32,2304]{1,0:T(8,128)(2,1)S(1)}, s32[8]{0:T(128)S(1)}) custom-call(s32[1,8]{1,0:T(1,128)S(1)} %copy-done, s32[1,8]{1,0:T(1,128)S(1)} %collective-permute-done.refs_1_, s32[1,8]{1,0:T(1,128)S(1)} %collective-permute-done.1.refs_2_, ...), custom_call_target="tpu_custom_call" | custom-call | tf_op jit(solution)/shard_map/pick/pallas_call | solution.py:31
  12.3 0.1 collective-permute-start.3
  12.4 2.1 %collective-permute-start.4 = (bf16[32,2304]{1,0:T(8,128)(2,1)S(1)}, bf16[32,2304]{1,0:T(8,128)(2,1)S(1)}, u32[]{:S(2)}, u32[]{:S(2)}) collective-permute-start(bf16[32,2304]{1,0:T(8,128)(2,1)S(1)} %get-tuple-element.48), channel_id=1, source_target_pairs={{0,8},{4,12},{8,0},{12,4},{1,9},{5,13},{9,1},{13,5},{2,10},{6,14},... | collective-permute-start | bytes 442376 | tf_op jit(solution)/shard_map/ppermute | solution.py:278
  14.5 2.3 %collective-permute-start.5 = (bf16[32,2304]{1,0:T(8,128)(2,1)S(1)}, bf16[32,2304]{1,0:T(8,128)(2,1)S(1)}, u32[]{:S(2)}, u32[]{:S(2)}) collective-permute-start(bf16[32,2304]{1,0:T(8,128)(2,1)S(1)} %get-tuple-element.49), channel_id=1, source_target_pairs={{0,12},{4,8},{8,4},{12,0},{1,13},{5,9},{9,5},{13,1},{2,14},{6,10},... | collective-permute-start | bytes 442376 | tf_op jit(solution)/shard_map/ppermute | solution.py:278
  16.8 11.8 %frozen.1 = (f32[2048,2048]{1,0:T(8,128)S(1)}, bf16[2048,1024]{1,0:T(8,128)(2,1)S(1)}, bf16[2048,2048]{1,0:T(8,128)(2,1)S(1)}) custom-call(bf16[2048,1024]{1,0:T(8,128)(2,1)} %upstream.1, bf16[2048,1024]{1,0:T(8,128)(2,1)} %weight.1, bf16[2048,2048]{1,0:T(8,128)(2,1)} %tokens.1, bf16[32,2304]{1,0:T(8,128)(2,1)S(1)} %get-tuple-element.56.after.refs_2_), custom_call_target="tpu_custom_call" | custom-call | tf_op jit(solution)/shard_map/frozen/pallas_call | solution.py:31
  28.6 0.0 collective-permute-done.3.refs_3_
  28.6 0.0 collective-permute-done.4.refs_4_
  28.6 0.0 collective-permute-done.5.refs_5_
  28.6 1.6 %collective-permute-start.6 = (bf16[128,256]{1,0:T(8,128)(2,1)S(1)}, bf16[128,256]{1,0:T(8,128)(2,1)S(1)}, u32[]{:S(2)}, u32[]{:S(2)}) collective-permute-start(bf16[128,256]{1,0:T(8,128)(2,1)S(1)} %pad_maximum_fusion.refs_6_), channel_id=1, source_target_pairs={{0,2},{1,3},{2,0},{3,1},{4,6},{5,7},{6,4},{7,5},{8,10},{9,11},{10,... | collective-permute-start | bytes 196616 | tf_op jit(solution)/shard_map/ppermute | solution.py:278
  30.2 3.0 %down.1 = (f32[16,2048]{1,0:T(8,128)S(1)}, bf16[128,2048]{1,0:T(8,128)(2,1)S(1)}) custom-call(s32[16]{0:T(128)S(1)} %get-tuple-element.54.refs_0_, bf16[2048,2048]{1,0:T(8,128)(2,1)S(1)} %get-tuple-element.60.refs_1_.refs_4_, bf16[32,2304]{1,0:T(8,128)(2,1)S(1)} %get-tuple-element.56.after.refs_2_, bf16[32,2304]{1,0:T(8,128)(2,1)S(1)} %collective-permute-done.3.refs_3_, ...), custom_call_target="tpu_custom_call" | custom-call | tf_op jit(solution)/shard_map/down/pallas_call | solution.py:31
  33.2 0.0 collective-permute-done.6
  33.2 0.1 collective-permute-start.8
  33.3 0.5 collective-permute-start.7
  33.8 0.8 %collective-permute-done.8 = f32[16,2048]{1,0:T(8,128)S(1)} collective-permute-done((f32[16,2048]{1,0:T(8,128)S(1)}, f32[16,2048]{1,0:T(8,128)S(1)}, u32[]{:S(2)}, u32[]{:S(2)}) %collective-permute-start.8) | collective-permute-done | bytes 131104 | tf_op jit(solution)/shard_map/ppermute | solution.py:278
  34.6 1.3 %collective-permute-start.9 = (f32[16,2048]{1,0:T(8,128)S(1)}, f32[16,2048]{1,0:T(8,128)S(1)}, u32[]{:S(2)}, u32[]{:S(2)}) collective-permute-start(f32[16,2048]{1,0:T(8,128)S(1)} %add.3.refs_5_.refs_1_), channel_id=1, source_target_pairs={{0,2},{1,3},{2,0},{3,1},{4,6},{5,7},{6,4},{7,5},{8,10},{9,11},{10,... | collective-permute-start | bytes 393224 | tf_op jit(solution)/shard_map/ppermute | solution.py:278
  35.9 0.0 collective-permute-done.7.refs_3_
  35.9 3.2 %up_grad_a.1 = (bf16[2048,128]{1,0:T(8,128)(2,1)S(1)}, f32[32,2048]{1,0:T(8,128)S(1)}, bf16[32,2048]{1,0:T(8,128)(2,1)S(1)}, bf16[32,2048]{1,0:T(8,128)(2,1)S(1)}, bf16[32,2048]{1,0:T(8,128)(2,1)S(1)}) custom-call(s32[16]{0:T(128)S(1)} %get-tuple-element.54.refs_0_, bf16[2048,1024]{1,0:T(8,128)(2,1)S(1)} %get-tuple-element.55.refs_1_.refs_3_, ...), custom_call_target="tpu_custom_call" | custom-call | tf_op jit(solution)/shard_map/up_grad_a/pallas_call | solution.py:31
  39.1 0.1 collective-permute-start.10
  39.2 2.1 %collective-permute-start.11 = (bf16[32,2048]{1,0:T(8,128)(2,1)S(1)}, bf16[32,2048]{1,0:T(8,128)(2,1)S(1)}, u32[]{:S(2)}, u32[]{:S(2)}) collective-permute-start(bf16[32,2048]{1,0:T(8,128)(2,1)S(1)} %get-tuple-element.70), channel_id=1, source_target_pairs={{0,8},{4,12},{8,0},{12,4},{1,9},{5,13},{9,1},{13,5},{2,10},{6,14},... | collective-permute-start | bytes 393224 | tf_op jit(solution)/shard_map/ppermute | solution.py:278
  41.3 2.3 %collective-permute-start.12 = (bf16[32,2048]{1,0:T(8,128)(2,1)S(1)}, bf16[32,2048]{1,0:T(8,128)(2,1)S(1)}, u32[]{:S(2)}, u32[]{:S(2)}) collective-permute-start(bf16[32,2048]{1,0:T(8,128)(2,1)S(1)} %get-tuple-element.71), channel_id=1, source_target_pairs={{0,12},{4,8},{8,4},{12,0},{1,13},{5,9},{9,5},{13,1},{2,14},{6,10},... | collective-permute-start | bytes 393224 | tf_op jit(solution)/shard_map/ppermute | solution.py:278
  43.6 0.0 collective-permute-done.9.refs_2_
  43.6 0.9 %grad_b.1 = (f32[32,256]{1,0:T(8,128)S(1)}, bf16[32,256]{1,0:T(8,128)(2,1)S(1)}, bf16[32,256]{1,0:T(8,128)(2,1)S(1)}, bf16[32,256]{1,0:T(8,128)(2,1)S(1)}) custom-call(s32[16]{0:T(128)S(1)} %get-tuple-element.54.refs_0_, f32[16,2048]{1,0:T(8,128)S(1)} %add.3.refs_5_.refs_1_, f32[16,2048]{1,0:T(8,128)S(1)} %collective-permute-done.9.refs_2_, ...), custom_call_target="tpu_custom_call" | custom-call | tf_op jit(solution)/shard_map/grad_b/pallas_call | solution.py:31
  44.5 0.1 collective-permute-start.13
  44.6 2.1 %collective-permute-start.14 = (bf16[32,256]{1,0:T(8,128)(2,1)S(1)}, bf16[32,256]{1,0:T(8,128)(2,1)S(1)}, u32[]{:S(2)}, u32[]{:S(2)}) collective-permute-start(bf16[32,256]{1,0:T(8,128)(2,1)S(1)} %get-tuple-element.73), channel_id=1, source_target_pairs={{0,8},{4,12},{8,0},{12,4},{1,9},{5,13},{9,1},{13,5},{2,10},{6,14},... | collective-permute-start | bytes 49160 | tf_op jit(solution)/shard_map/ppermute | solution.py:278
  46.7 0.1 collective-permute-done.10.refs_2_
  46.8 2.2 %collective-permute-start.15 = (bf16[32,256]{1,0:T(8,128)(2,1)S(1)}, bf16[32,256]{1,0:T(8,128)(2,1)S(1)}, u32[]{:S(2)}, u32[]{:S(2)}) collective-permute-start(bf16[32,256]{1,0:T(8,128)(2,1)S(1)} %get-tuple-element.74), channel_id=1, source_target_pairs={{0,12},{4,8},{8,4},{12,0},{1,13},{5,9},{9,5},{13,1},{2,14},{6,10},... | collective-permute-start | bytes 49160 | tf_op jit(solution)/shard_map/ppermute | solution.py:278
  49.0 4.4 %token_gradient.1.refs_9_ = bf16[2048,2048]{1,0:T(8,128)(2,1)} custom-call(f32[2048,2048]{1,0:T(8,128)S(1)} %get-tuple-element.53.refs_0_, bf16[2048,128]{1,0:T(8,128)(2,1)S(1)} %get-tuple-element.64.refs_4_.refs_1_, bf16[128,2048]{1,0:T(8,128)(2,1)S(1)} %get-tuple-element.65.refs_2_, f32[32,256]{1,0:T(8,128)S(1)} %get-tuple-element.66.refs_3_.refs_5_), custom_call_target="tpu_custom_call" | custom-call | tf_op jit(solution)/shard_map/token_gradient/pallas_call | solution.py:31
  53.4 0.0 collective-permute-done.11.refs_3_
  53.4 0.0 collective-permute-done.12.refs_4_
  53.4 0.0 collective-permute-done.13.refs_6_
  53.4 1.8 %collective-permute-done.14.refs_7_ = bf16[32,256]{1,0:T(8,128)(2,1)S(1)} collective-permute-done((bf16[32,256]{1,0:T(8,128)(2,1)S(1)}, bf16[32,256]{1,0:T(8,128)(2,1)S(1)}, u32[]{:S(2)}, u32[]{:S(2)}) %collective-permute-start.14) | collective-permute-done | bytes 16416 | tf_op jit(solution)/shard_map/ppermute | solution.py:278
  55.2 0.0 collective-permute-done.15.refs_8_
  55.2 1.8 %finish.1 = (f32[8,16,2048]{2,1,0:T(8,128)}, f32[8,16,256]{2,1,0:T(8,128)}) custom-call(s32[8]{0:T(128)S(1)} %get-tuple-element.67.refs_0_, f32[32,2048]{1,0:T(8,128)S(1)} %get-tuple-element.68.refs_1_, bf16[32,2048]{1,0:T(8,128)(2,1)S(1)} %collective-permute-done.10.refs_2_, bf16[32,2048]{1,0:T(8,128)(2,1)S(1)} %collective-permute-done.11.refs_3_, ...), custom_call_target="tpu_custom_call" | custom-call | tf_op jit(solution)/shard_map/finish/pallas_call | solution.py:31
  (7 shorter events, 0.0 us)
Async XLA Ops:
  0.6 7.4 %collective-permute-start.2 = (s32[1,8]{1,0:T(1,128)}, s32[1,8]{1,0:T(1,128)S(1)}, u32[]{:S(2)}, u32[]{:S(2)}) collective-permute-start(s32[1,8]{1,0:T(1,128)} %refs_0_.1), channel_id=1, source_target_pairs={{0,12},{4,8},{8,4},{12,0},{1,13},{5,9},{9,5},{13,1},{2,14},{6,10},... | collective-permute-start | bytes 104 | tf_op jit(solution)/shard_map/ppermute | solution.py:278
  5.7 4.6 %collective-permute-start.1 = (s32[1,8]{1,0:T(1,128)}, s32[1,8]{1,0:T(1,128)S(1)}, u32[]{:S(2)}, u32[]{:S(2)}) collective-permute-start(s32[1,8]{1,0:T(1,128)} %refs_0_.1), channel_id=1, source_target_pairs={{0,8},{4,12},{8,0},{12,4},{1,9},{5,13},{9,1},{13,5},{2,10},{6,14},... | collective-permute-start | bytes 104 | tf_op jit(solution)/shard_map/ppermute | solution.py:278
  5.7 4.6 %collective-permute-start = (s32[1,8]{1,0:T(1,128)}, s32[1,8]{1,0:T(1,128)S(1)}, u32[]{:S(2)}, u32[]{:S(2)}) collective-permute-start(s32[1,8]{1,0:T(1,128)} %refs_0_.1), channel_id=1, source_target_pairs={{0,4},{4,0},{8,12},{12,8},{1,5},{5,1},{9,13},{13,9},{2,6},{6,2},{1... | collective-permute-start | bytes 104 | tf_op jit(solution)/shard_map/ppermute | solution.py:278
  10.3 0.7 %copy-start = (s32[1,8]{1,0:T(1,128)S(1)}, s32[1,8]{1,0:T(1,128)}, u32[]{:S(2)}) copy-start(s32[1,8]{1,0:T(1,128)} %refs_0_.1) | copy-start | bytes 100
  12.3 16.3 %collective-permute-start.3 = (bf16[32,2304]{1,0:T(8,128)(2,1)S(1)}, bf16[32,2304]{1,0:T(8,128)(2,1)S(1)}, u32[]{:S(2)}, u32[]{:S(2)}) collective-permute-start(bf16[32,2304]{1,0:T(8,128)(2,1)S(1)} %get-tuple-element.47), channel_id=1, source_target_pairs={{0,4},{4,0},{8,12},{12,8},{1,5},{5,1},{9,13},{13,9},{2,6},{6,2},{1... | collective-permute-start | bytes 442376 | tf_op jit(solution)/shard_map/ppermute | solution.py:278
  12.4 16.2 %collective-permute-start.4 = (bf16[32,2304]{1,0:T(8,128)(2,1)S(1)}, bf16[32,2304]{1,0:T(8,128)(2,1)S(1)}, u32[]{:S(2)}, u32[]{:S(2)}) collective-permute-start(bf16[32,2304]{1,0:T(8,128)(2,1)S(1)} %get-tuple-element.48), channel_id=1, source_target_pairs={{0,8},{4,12},{8,0},{12,4},{1,9},{5,13},{9,1},{13,5},{2,10},{6,14},... | collective-permute-start | bytes 442376 | tf_op jit(solution)/shard_map/ppermute | solution.py:278
  14.5 14.1 %collective-permute-start.5 = (bf16[32,2304]{1,0:T(8,128)(2,1)S(1)}, bf16[32,2304]{1,0:T(8,128)(2,1)S(1)}, u32[]{:S(2)}, u32[]{:S(2)}) collective-permute-start(bf16[32,2304]{1,0:T(8,128)(2,1)S(1)} %get-tuple-element.49), channel_id=1, source_target_pairs={{0,12},{4,8},{8,4},{12,0},{1,13},{5,9},{9,5},{13,1},{2,14},{6,10},... | collective-permute-start | bytes 442376 | tf_op jit(solution)/shard_map/ppermute | solution.py:278
  28.6 4.5 %collective-permute-start.6 = (bf16[128,256]{1,0:T(8,128)(2,1)S(1)}, bf16[128,256]{1,0:T(8,128)(2,1)S(1)}, u32[]{:S(2)}, u32[]{:S(2)}) collective-permute-start(bf16[128,256]{1,0:T(8,128)(2,1)S(1)} %pad_maximum_fusion.refs_6_), channel_id=1, source_target_pairs={{0,2},{1,3},{2,0},{3,1},{4,6},{5,7},{6,4},{7,5},{8,10},{9,11},{10,... | collective-permute-start | bytes 196616 | tf_op jit(solution)/shard_map/ppermute | solution.py:278
  33.2 1.4 %collective-permute-start.8 = (f32[16,2048]{1,0:T(8,128)S(1)}, f32[16,2048]{1,0:T(8,128)S(1)}, u32[]{:S(2)}, u32[]{:S(2)}) collective-permute-start(f32[16,2048]{1,0:T(8,128)S(1)} %get-tuple-element.63), channel_id=1, source_target_pairs={{0,1},{1,0},{2,3},{3,2},{4,5},{5,4},{6,7},{7,6},{8,9},{9,8},{10,11... | collective-permute-start | bytes 393224 | tf_op jit(solution)/shard_map/ppermute | solution.py:278
  33.3 2.6 %collective-permute-start.7 = (bf16[256,256]{1,0:T(8,128)(2,1)S(1)}, bf16[256,256]{1,0:T(8,128)(2,1)S(1)}, u32[]{:S(2)}, u32[]{:S(2)}) collective-permute-start(bf16[256,256]{1,0:T(8,128)(2,1)S(1)} %constant_dynamic-update-slice_fusion.refs_2_), channel_id=1, source_target_pairs={{0,1},{1,0},{2,3},{3,2},{4,5},{5,4},{6,7},{7,6},{8,9},{9,8},{10,11... | collective-permute-start | bytes 393224 | tf_op jit(solution)/shard_map/ppermute | solution.py:278
  34.6 9.0 %collective-permute-start.9 = (f32[16,2048]{1,0:T(8,128)S(1)}, f32[16,2048]{1,0:T(8,128)S(1)}, u32[]{:S(2)}, u32[]{:S(2)}) collective-permute-start(f32[16,2048]{1,0:T(8,128)S(1)} %add.3.refs_5_.refs_1_), channel_id=1, source_target_pairs={{0,2},{1,3},{2,0},{3,1},{4,6},{5,7},{6,4},{7,5},{8,10},{9,11},{10,... | collective-permute-start | bytes 393224 | tf_op jit(solution)/shard_map/ppermute | solution.py:278
  39.1 7.6 %collective-permute-start.10 = (bf16[32,2048]{1,0:T(8,128)(2,1)S(1)}, bf16[32,2048]{1,0:T(8,128)(2,1)S(1)}, u32[]{:S(2)}, u32[]{:S(2)}) collective-permute-start(bf16[32,2048]{1,0:T(8,128)(2,1)S(1)} %get-tuple-element.69), channel_id=1, source_target_pairs={{0,4},{4,0},{8,12},{12,8},{1,5},{5,1},{9,13},{13,9},{2,6},{6,2},{1... | collective-permute-start | bytes 393224 | tf_op jit(solution)/shard_map/ppermute | solution.py:278
  39.2 14.1 %collective-permute-start.11 = (bf16[32,2048]{1,0:T(8,128)(2,1)S(1)}, bf16[32,2048]{1,0:T(8,128)(2,1)S(1)}, u32[]{:S(2)}, u32[]{:S(2)}) collective-permute-start(bf16[32,2048]{1,0:T(8,128)(2,1)S(1)} %get-tuple-element.70), channel_id=1, source_target_pairs={{0,8},{4,12},{8,0},{12,4},{1,9},{5,13},{9,1},{13,5},{2,10},{6,14},... | collective-permute-start | bytes 393224 | tf_op jit(solution)/shard_map/ppermute | solution.py:278
  41.3 12.1 %collective-permute-start.12 = (bf16[32,2048]{1,0:T(8,128)(2,1)S(1)}, bf16[32,2048]{1,0:T(8,128)(2,1)S(1)}, u32[]{:S(2)}, u32[]{:S(2)}) collective-permute-start(bf16[32,2048]{1,0:T(8,128)(2,1)S(1)} %get-tuple-element.71), channel_id=1, source_target_pairs={{0,12},{4,8},{8,4},{12,0},{1,13},{5,9},{9,5},{13,1},{2,14},{6,10},... | collective-permute-start | bytes 393224 | tf_op jit(solution)/shard_map/ppermute | solution.py:278
  44.5 8.9 %collective-permute-start.13 = (bf16[32,256]{1,0:T(8,128)(2,1)S(1)}, bf16[32,256]{1,0:T(8,128)(2,1)S(1)}, u32[]{:S(2)}, u32[]{:S(2)}) collective-permute-start(bf16[32,256]{1,0:T(8,128)(2,1)S(1)} %get-tuple-element.72), channel_id=1, source_target_pairs={{0,4},{4,0},{8,12},{12,8},{1,5},{5,1},{9,13},{13,9},{2,6},{6,2},{1... | collective-permute-start | bytes 49160 | tf_op jit(solution)/shard_map/ppermute | solution.py:278
  44.6 10.6 %collective-permute-start.14 = (bf16[32,256]{1,0:T(8,128)(2,1)S(1)}, bf16[32,256]{1,0:T(8,128)(2,1)S(1)}, u32[]{:S(2)}, u32[]{:S(2)}) collective-permute-start(bf16[32,256]{1,0:T(8,128)(2,1)S(1)} %get-tuple-element.73), channel_id=1, source_target_pairs={{0,8},{4,12},{8,0},{12,4},{1,9},{5,13},{9,1},{13,5},{2,10},{6,14},... | collective-permute-start | bytes 49160 | tf_op jit(solution)/shard_map/ppermute | solution.py:278
  46.8 8.4 %collective-permute-start.15 = (bf16[32,256]{1,0:T(8,128)(2,1)S(1)}, bf16[32,256]{1,0:T(8,128)(2,1)S(1)}, u32[]{:S(2)}, u32[]{:S(2)}) collective-permute-start(bf16[32,256]{1,0:T(8,128)(2,1)S(1)} %get-tuple-element.74), channel_id=1, source_target_pairs={{0,12},{4,8},{8,4},{12,0},{1,13},{5,9},{9,5},{13,1},{2,14},{6,10},... | collective-permute-start | bytes 49160 | tf_op jit(solution)/shard_map/ppermute | solution.py:278

commit v3 on v2

--- a/solution.py
+++ b/solution.py
@@ -27,15 +27,16 @@
     return pltpu.with_memory_space_constraint(x, pltpu.HBM)
 
 
-def kernel(body, name, outs, in_specs, out_specs, args, scratch=()):
+def kernel(body, name, outs, in_specs, out_specs, args, scratch=(), alias=None, flops=0):
     return pl.pallas_call(
         body,
         out_shape=outs,
         in_specs=in_specs,
         out_specs=out_specs,
         scratch_shapes=list(scratch),
+        input_output_aliases=alias or {},
         compiler_params=pltpu.CompilerParams(vmem_limit_bytes=VMEM_LIMIT),
-        cost_estimate=pl.CostEstimate(flops=0, bytes_accessed=0, transcendentals=0),
+        cost_estimate=pl.CostEstimate(flops=flops, bytes_accessed=0, transcendentals=0),
         name=name,
     )(*args)
 
@@ -58,15 +59,21 @@
     return lax.div(ident, I32(held)), lax.rem(ident, I32(held))
 
 
-def plan_kernel(cap, held, my_list, slot_ids, bank_a, bank_b, vslot, bank, lists, ids, place_v, sems):
+def plan_kernel(cap, held, *refs):
+    my_list, slot_ids, bank_a, bank_b, upstream, weight = refs[:6]
+    vslot, bank, upstream_v, weight_v = refs[6:10]
+    lists, ids, place_v, sems = refs[10:]
     slots = lists.shape[1]
     width = bank_a.shape[1]
+    half = upstream.shape[0] // 2
     copies = start_all(
         [
             pltpu.make_async_copy(my_list, lists, sems.at[0]),
             pltpu.make_async_copy(slot_ids, ids, sems.at[1]),
             pltpu.make_async_copy(bank_a, bank.at[:, pl.ds(0, width)], sems.at[2]),
             pltpu.make_async_copy(bank_b, bank.at[:, pl.ds(width, bank_b.shape[1])], sems.at[3]),
+            pltpu.make_async_copy(weight.at[pl.ds(0, weight_v.shape[0]), :], weight_v, sems.at[4]),
+            pltpu.make_async_copy(upstream.at[pl.ds(0, half), :], upstream_v.at[pl.ds(0, half), :], sems.at[5]),
         ]
     )
     me = lax.axis_index("rep")
@@ -110,56 +117,52 @@
             outs[s][c * rank : (c + 1) * rank, :] = bank[pl.ds(start, rank), :]
 
 
-def frozen_kernel(chunk, tile, upstream, weight, tokens, after, out, upstream_v, tokens_v, weight_v, sems):
-    del after
+def frozen_kernel(chunk, tile, *refs):
+    weight_first, weight, tokens, upstream_in_hbm = refs[1:5]
+    out, tokens_v, upstream, weight_v, sems = refs[6:]
     rows = upstream.shape[0]
-    width = weight.shape[0]
-    n_rows, n_cols = rows // chunk, width // tile
-
-    def fetch(source, to, i, size, sem):
-        at = pl.ds(i * size, size)
-        return pltpu.make_async_copy(source.at[at, :], to.at[at, :], sems.at[sem])
-
-    weights = [fetch(weight, weight_v, t, tile, t) for t in range(n_cols)]
-    ups = [fetch(upstream, upstream_v, r, chunk, n_cols + r) for r in range(n_rows)]
-    toks = [fetch(tokens, tokens_v, r, chunk, n_cols + n_rows + r) for r in range(n_rows)]
-    start_all(weights[:1] + ups + weights[1:] + toks)
-    for t in range(n_cols):
-        weights[t].wait()
+
+    def fetch(source, to, start, size, sem, base=0):
+        return pltpu.make_async_copy(
+            source.at[pl.ds(start, size), :], to.at[pl.ds(start - base, size), :], sems.at[sem]
+        )
+
+    half = rows // 2
+    late = fetch(upstream_in_hbm, upstream, half, rows - half, sems.shape[0] - 1)
+    late.start()
+    starts = range(tile, weight.shape[0], tile)
+    weights = start_all([fetch(weight, weight_v, at, tile, i, tile) for i, at in enumerate(starts)])
+    toks = start_all([fetch(tokens, tokens_v, at, chunk, len(starts) + i) for i, at in enumerate(range(0, rows, chunk))])
+    for t in range(len(starts) + 1):
+        if t > 0:
+            weights[t - 1].wait()
         cols = slice(t * tile, (t + 1) * tile)
-        for r in range(n_rows):
-            if t == 0:
-                ups[r].wait()
+        source = weight_first[...] if t == 0 else weight_v[(t - 1) * tile : t * tile, :]
+        for r in range(rows // chunk):
+            if t == 0 and r == half // chunk:
+                late.wait()
             at = slice(r * chunk, (r + 1) * chunk)
-            out[at, cols] = lax.dot_general(
-                upstream_v[at, :], weight_v[cols, :], NT, preferred_element_type=F32
-            )
+            out[at, cols] = lax.dot_general(upstream[at, :], source, NT, preferred_element_type=F32)
     wait_all(toks)
 
 
 def up_kernel(rep, cap, rank, nb, order, *refs):
     vslot, upstream, held_q, came_q, tokens = refs[:5]
     up_out = refs[6]
-    grads = refs[7:]
+    grads, b_all = refs[7:-1], refs[-1]
     width = rep * cap * rank
     per = cap * rank
     cols = held_q.shape[1]
     tp_rank = lax.axis_index("tp")
+    for i, s in enumerate(order):
+        for j, piece in ((0, held_q), (1, came_q)):
+            at = pl.multiple_of(jnp.bitwise_xor(tp_rank, s ^ j) * cols, cols)
+            b_all[:, pl.ds(at, cols)] = piece[i * width : (i + 1) * width, :]
     chunk = 4
     lane_slot = lax.broadcasted_iota(I32, (BLOCK, width), 1) // rank
     for r in range(nb // chunk):
         rows = slice(r * chunk * BLOCK, (r + 1) * chunk * BLOCK)
-        acc = None
-        for i, s in enumerate(order):
-            for j, piece in ((0, held_q), (1, came_q)):
-                at = pl.multiple_of(jnp.bitwise_xor(tp_rank, s ^ j) * cols, cols)
-                part = lax.dot_general(
-                    upstream[rows, pl.ds(at, cols)],
-                    piece[i * width : (i + 1) * width, :],
-                    NT,
-                    preferred_element_type=F32,
-                )
-                acc = part if acc is None else acc + part
+        acc = lax.dot_general(upstream[rows, :], b_all[...], NT, preferred_element_type=F32)
         acc = (SCALE * acc).astype(BF16)
         for b in range(chunk):
             blk = r * chunk + b
@@ -197,7 +200,7 @@
 
 
 def grad_b_kernel(rep, cap, rank, nb, *refs):
-    vslot, down_here, down_there, upstream = refs[:4]
+    vslot, down_here, down_there, upstream, near_a = refs[:5]
     grads = refs[5:-1]
     spread = refs[-1]
     per = cap * rank
@@ -210,26 +213,32 @@
         spread[pl.ds(start, rank), b * BLOCK : (b + 1) * BLOCK] = total[:, b * BLOCK : (b + 1) * BLOCK]
     grad = jnp.dot(spread[...], upstream[:, pl.ds(at, cols)], preferred_element_type=F32)
     for s in range(rep):
-        grads[s][...] = grad[s * per : (s + 1) * per, :].astype(grads[s].dtype)
-
-
-def token_kernel(chunk, tile, *refs):
+        part = grad[s * per : (s + 1) * per, :].astype(grads[s].dtype)
+        if s == 1:
+            grads[s][:, : near_a.shape[1]] = near_a[...]
+            grads[s][:, near_a.shape[1] :] = part
+        else:
+            grads[s][...] = part
+
+
+def token_kernel(chunk, tiles, *refs):
     frozen, up_scaled, a_all = refs[:3]
     out, buf, sems = refs[-3:]
-    rows, width = frozen.shape
+    rows = up_scaled.shape[0]
     pending = {}
-    for t in range(width // tile):
-        slot = t % 2
-        cols = slice(t * tile, (t + 1) * tile)
+    for n, (start, size) in enumerate(tiles):
+        slot = n % 2
+        cols = slice(start, start + size)
         for r in range(rows // chunk):
             at = slice(r * chunk, (r + 1) * chunk)
             if (slot, r) in pending:
                 pending.pop((slot, r)).wait()
-            low = jnp.dot(up_scaled[at, :], a_all[:, cols], preferred_element_type=F32)
-            buf[slot, at, :] = (frozen[at, cols] + low).astype(BF16)
+            total = jnp.dot(up_scaled[at, :], a_all[:, cols], preferred_element_type=F32)
+            total = frozen[at, cols] + total
+            buf[slot, at, :size] = total.astype(BF16)
             copy = pltpu.make_async_copy(
-                buf.at[slot, pl.ds(r * chunk, chunk), :],
-                out.at[pl.ds(r * chunk, chunk), pl.ds(t * tile, tile)],
+                buf.at[slot, pl.ds(r * chunk, chunk), pl.ds(0, size)],
+                out.at[pl.ds(r * chunk, chunk), pl.ds(start, size)],
                 sems.at[slot, r],
             )
             copy.start()
@@ -239,25 +248,38 @@
 
 def finish_kernel(rep, cap, rank, *refs):
     pick = refs[0]
-    in_a = refs[1 : 1 + rep]
-    in_b = refs[1 + rep : 1 + 2 * rep]
-    out_a, out_b, sum_a, sum_b, sem = refs[2 + 2 * rep :]
-    sum_a[...] = jnp.zeros_like(sum_a)
-    sum_b[...] = jnp.zeros_like(sum_b)
-    for s in range(rep):
-        for c in range(cap):
-            to = pick[s * cap + c]
-
-            @pl.when(to >= 0)
-            def _():
-                sum_a[to] += in_a[s][c * rank : (c + 1) * rank, :].astype(F32)
-                sum_b[to] += in_b[s][c * rank : (c + 1) * rank, :].astype(F32)
-
-    wait_all(
-        start_all(
-            [pltpu.make_async_copy(sum_a, out_a, sem.at[0]), pltpu.make_async_copy(sum_b, out_b, sem.at[1])]
-        )
-    )
+    far = rep - 2
+    near = refs[1 + far]
+    own_a, own_b = refs[2 + 2 * far : 4 + 2 * far]
+    in_a = (own_a, near, *refs[1 : 1 + far])
+    in_b = (own_b, near, *refs[2 + far : 2 + 2 * far])
+    out_a, out_b, sum_a, sum_b, sem = refs[1 + 2 * rep :]
+    halves = 2
+    width = sum_a.shape[2] // halves
+    copies = []
+    for h in range(halves):
+        cols = slice(h * width, (h + 1) * width)
+        sum_a[:, :, cols] = jnp.zeros(sum_a.shape[:2] + (width,), F32)
+        if h == 0:
+            sum_b[...] = jnp.zeros_like(sum_b)
+        for s in range(rep):
+            for c in range(cap):
+                to = pick[s * cap + c]
+                at = slice(c * rank, (c + 1) * rank)
+
+                @pl.when(to >= 0)
+                def _():
+                    sum_a[to, :, cols] += in_a[s][at, cols].astype(F32)
+                    if h == 0:
+                        sum_b[to] += in_b[s][at, in_b[s].shape[1] - sum_b.shape[2] :].astype(F32)
+
+        part = pl.ds(h * width, width)
+        copies.append(pltpu.make_async_copy(sum_a.at[:, :, part], out_a.at[:, :, part], sem.at[h]))
+        copies[-1].start()
+        if h == 0:
+            copies.append(pltpu.make_async_copy(sum_b, out_b, sem.at[halves]))
+            copies[-1].start()
+    wait_all(copies)
 
 
 def local(tokens_in, upstream, base_weight, bank_a, bank_b, slot_ids, used_lists):
@@ -282,18 +304,31 @@
 
     a_flat = in_hbm(bank_a.reshape(held * rank, width))
     b_flat = in_hbm(bank_b.reshape(held * rank, cols))
-    vslot, bank = kernel(
+    w_flat = in_hbm(base_weight)
+    vslot, bank, upstream_v, weight_first = kernel(
         functools.partial(plan_kernel, cap, held),
         "plan",
-        [struct((nb,), I32), pltpu.VMEM((held * rank, width + cols), BF16)],
-        [HBM, HBM, HBM, HBM],
-        [SMEM, VMEM],
-        [in_hbm(used_lists), in_hbm(slot_ids.reshape(nb, BLOCK)), a_flat, b_flat],
+        [
+            struct((nb,), I32),
+            pltpu.VMEM((held * rank, width + cols), BF16),
+            pltpu.VMEM((rows, outs), BF16),
+            pltpu.VMEM((tile, outs), BF16),
+        ],
+        [HBM] * 6,
+        [SMEM, VMEM, VMEM, VMEM],
+        [
+            in_hbm(used_lists),
+            in_hbm(slot_ids.reshape(nb, BLOCK)),
+            a_flat,
+            b_flat,
+            in_hbm(upstream),
+            w_flat,
+        ],
         [
             pltpu.SMEM((1, slots), I32),
             pltpu.SMEM((nb, BLOCK), I32),
             pltpu.SMEM((slots,), I32),
-            pltpu.SemaphoreType.DMA((4,)),
+            pltpu.SemaphoreType.DMA((6,)),
         ],
     )
 
@@ -302,28 +337,30 @@
         functools.partial(pick_kernel, rep, cap, held),
         "pick",
         [struct((per, width + cols), BF16)] * rep + [struct((rep * cap,), I32)],
-        [ANY] * rep + [VMEM],
+        [HBM] + [ANY] * (rep - 1) + [VMEM],
         [VMEM] * rep + [SMEM],
-        [used_lists, *lists[: rep - 1], lists[rep]],
+        [in_hbm(used_lists), *lists[: rep - 1], lists[rep]],
         [pltpu.SMEM((1, slots), I32)] * rep + [pltpu.SemaphoreType.DMA((rep,))],
     )
     vslot = lists[rep - 1]
-    fetched = {s: swap("rep", sends[s], s) for s in range(rep - 1, 0, -1)}
+    fetched = {s: swap("rep", sends[s], s) for s in range(1, rep)}
     fetched[0] = sends[0]
 
-    n_fetch = width // tile + 2 * (rows // chunk)
-    frozen, upstream_v, tokens_v = kernel(
+    frozen, tokens_v, upstream_v = kernel(
         functools.partial(frozen_kernel, chunk, tile),
         "frozen",
-        [pltpu.VMEM((rows, width), F32), pltpu.VMEM((rows, outs), BF16), pltpu.VMEM((rows, width), BF16)],
-        [HBM, HBM, HBM, ANY],
-        [VMEM, VMEM, VMEM],
-        [in_hbm(upstream), in_hbm(base_weight), in_hbm(tokens_in), sends[0]],
-        [pltpu.VMEM((width, outs), BF16), pltpu.SemaphoreType.DMA((n_fetch,))],
-    )
-    *fetched, upstream_v, tokens_v, frozen = tie(
-        (*[fetched[s] for s in range(rep)], upstream_v, tokens_v, frozen)
-    )
+        [pltpu.VMEM((rows, width), F32), pltpu.VMEM((rows, width), BF16), pltpu.VMEM((rows, outs), BF16)],
+        [VMEM, VMEM, HBM, HBM, HBM, ANY],
+        [VMEM] * 3,
+        [upstream_v, weight_first, w_flat, in_hbm(tokens_in), in_hbm(upstream), sends[0]],
+        [
+            pltpu.VMEM((width - tile, outs), BF16),
+            pltpu.SemaphoreType.DMA((width // tile + rows // chunk,)),
+        ],
+        {0: 2},
+    )
+    *far, upstream_v, tokens_v, frozen = tie((*[fetched[s] for s in range(2, rep)], upstream_v, tokens_v, frozen))
+    *fetched, upstream_v = tie((fetched[0], fetched[1], *far, upstream_v))
 
     quarter = jnp.concatenate([x[:, width:] for x in fetched], axis=0)
     down, a_all = kernel(
@@ -354,43 +391,43 @@
         [SMEM] + [VMEM] * 4 + [ANY],
         [VMEM] * (rep + 1),
         [vslot, upstream_v, held_q, came_q, tokens_v, down],
-    )
-    recv_ga = {s: swap("rep", grads_a[s], s) for s in range(rep - 1, 0, -1)}
-    recv_ga[0] = grads_a[0]
-
+        [pltpu.VMEM((depth, outs), BF16)],
+    )
     grads_b = kernel(
         functools.partial(grad_b_kernel, rep, cap, rank, nb),
         "grad_b",
-        [struct((per, cols), F32)] + [struct((per, cols), BF16)] * (rep - 1),
-        [SMEM, VMEM, VMEM, VMEM, ANY],
+        [struct((per, cols), F32), struct((per, width + cols), BF16)] + [struct((per, cols), BF16)] * (rep - 2),
+        [SMEM] + [VMEM] * 4,
         [VMEM] * rep,
-        [vslot, down, down_there, upstream_v, up_scaled],
+        [vslot, down, down_there, upstream_v, grads_a[1]],
         [pltpu.VMEM((depth, rows), BF16)],
     )
-    recv_gb = {s: swap("rep", grads_b[s], s) for s in range(rep - 1, 0, -1)}
-    recv_gb[0] = grads_b[0]
+    far_a = [swap("rep", grads_a[s], s) for s in range(2, rep)]
+    near = swap("rep", grads_b[1], 1)
+    far_b = [swap("rep", grads_b[s], s) for s in range(2, rep)]
 
     token_gradient = kernel(
-        functools.partial(token_kernel, chunk, tile),
+        functools.partial(token_kernel, chunk, [(at, tile) for at in range(0, width, tile)]),
         "token_gradient",
         pltpu.HBM((rows, width), BF16),
         [VMEM] * 3 + [ANY],
         HBM,
         [frozen, up_scaled, a_all, grads_b[0]],
         [pltpu.VMEM((2, rows, tile), BF16), pltpu.SemaphoreType.DMA((2, rows // chunk))],
+        flops=8 * rows * width * depth,
     )
 
     grad_a, grad_b = kernel(
         functools.partial(finish_kernel, rep, cap, rank),
         "finish",
         [pltpu.HBM((held, rank, width), F32), pltpu.HBM((held, rank, cols), F32)],
-        [SMEM] + [VMEM] * (2 * rep) + [HBM],
+        [SMEM] + [VMEM] * (2 * rep - 1) + [HBM],
         [HBM] * 2,
-        [pick, *[recv_ga[s] for s in range(rep)], *[recv_gb[s] for s in range(rep)], in_hbm(token_gradient)],
+        [pick, *far_a, near, *far_b, grads_a[0], grads_b[0], in_hbm(token_gradient)],
         [
             pltpu.VMEM((held, rank, width), F32),
             pltpu.VMEM((held, rank, cols), F32),
-            pltpu.SemaphoreType.DMA((2,)),
+            pltpu.SemaphoreType.DMA((3,)),
         ],
     )
     return token_gradient, grad_a, grad_b

time: 57.3 us -> 54.1 us (0.944)
  starting transfers between devices: 22.4 us -> 20.2 us
  Pallas kernels: 28.1 us -> 27.3 us
  local copies, waits for them, and re-layouts: 0.68 us -> 0.03 us
    ppermute x16 -> x15, starting transfers between devices: 22.4 us -> 20.2 us  [swap(): lax.ppermute(x, axis, [(i, i ^ s) for i in range(lax.axis_size(axis))])]
    pallas_call x8, Pallas kernels: 28.1 us -> 27.3 us  [kernel(): pl.pallas_call(body, out_shape=outs, in_specs=in_specs, out_specs=out_spe...]
    unnamed x2 -> x0, local copies, waits for them, and re-layouts: 0.66 us -> none
    ppermute x16 -> x15, waiting for transfers between devices: 4.96 us -> 5.42 us  [swap(): lax.ppermute(x, axis, [(i, i ^ s) for i in range(lax.axis_size(axis))])]
  transfers between devices with their start and end apart: 16 -> 15, of which waited for: 4 -> 4; matrix products, arithmetic and copies ran while one was open for 0% -> 0% of each run, Pallas kernels for 44% -> 45%
where the time goes in v3:
time: 54.1 us; the launch traced here: 54 us
  Pallas kernels  27.3 us (50%)
  starting transfers between devices  20.2 us (37%)
  waiting for transfers between devices  5.42 us (10%)
  between operations  0.96 us (2%)
    pallas_call x8, Pallas kernels, kernel(): pl.pallas_call(body, out_shape=outs, in_specs=in_specs, out_specs=out_spe...  27.3 us
    ppermute x15, starting transfers between devices, swap(): lax.ppermute(x, axis, [(i, i ^ s) for i in range(lax.axis_size(axis))])  20.2 us
    ppermute x15, waiting for transfers between devices, swap(): lax.ppermute(x, axis, [(i, i ^ s) for i in range(lax.axis_size(axis))])  5.42 us
  transfers between devices with their start and end apart: 15, of which 4 were waited for; matrix products, arithmetic and copies ran while one was open for 0% of the time, Pallas kernels for 45%

profile of v3, /device:TPU:0, one launch (start us, length us, event | category | flops | bytes accessed | tf_op | source)
XLA Modules:
  0.0 54.0 jit_solution(7595002751531485595)
XLA Ops:
  0.6 5.1 %collective-permute-start.2 = (s32[1,8]{1,0:T(1,128)}, s32[1,8]{1,0:T(1,128)S(1)}, u32[]{:S(2)}, u32[]{:S(2)}) collective-permute-start(s32[1,8]{1,0:T(1,128)} %refs_0_.3), channel_id=1, source_target_pairs={{0,12},{4,8},{8,4},{12,0},{1,13},{5,9},{9,5},{13,1},{2,14},{6,10},... | collective-permute-start | bytes 104 | tf_op jit(solution)/shard_map/ppermute | solution.py:300
  5.7 0.0 collective-permute-start.1
  5.7 0.6 %collective-permute-start = (s32[1,8]{1,0:T(1,128)}, s32[1,8]{1,0:T(1,128)S(1)}, u32[]{:S(2)}, u32[]{:S(2)}) collective-permute-start(s32[1,8]{1,0:T(1,128)} %refs_0_.3), channel_id=1, source_target_pairs={{0,4},{4,0},{8,12},{12,8},{1,5},{5,1},{9,13},{13,9},{2,6},{6,2},{1... | collective-permute-start | bytes 104 | tf_op jit(solution)/shard_map/ppermute | solution.py:300
  6.4 2.7 %plan.1 = (s32[16]{0:T(128)S(1)}, bf16[128,2304]{1,0:T(8,128)(2,1)S(1)}, bf16[2048,1024]{1,0:T(8,128)(2,1)S(1)}, bf16[512,1024]{1,0:T(8,128)(2,1)S(1)}) custom-call(s32[1,8]{1,0:T(1,128)} %refs_0_.3, s32[16,128]{1,0:T(8,128)} %bitcast.5, bf16[128,2048]{1,0:T(8,128)(2,1)} %bitcast.3, bf16[128,256]{1,0:T(8,128)(2,1)} %bitcast.4, bf16[2048,1024]{1,0:T(8,128)(2,1)} %refs_4_.3, ...), custom_call_target="tpu_custom_call" | custom-call | tf_op jit(solution)/shard_map/plan/pallas_call | solution.py:31
  9.1 0.0 collective-permute-done.2.refs_3_
  9.2 1.2 %collective-permute-done.1.refs_2_ = s32[1,8]{1,0:T(1,128)S(1)} collective-permute-done((s32[1,8]{1,0:T(1,128)}, s32[1,8]{1,0:T(1,128)S(1)}, u32[]{:S(2)}, u32[]{:S(2)}) %collective-permute-start.1) | collective-permute-done | bytes 64 | tf_op jit(solution)/shard_map/ppermute | solution.py:300
  10.3 0.0 collective-permute-done.refs_1_
  10.3 1.4 %pick.1 = (bf16[32,2304]{1,0:T(8,128)(2,1)S(1)}, bf16[32,2304]{1,0:T(8,128)(2,1)S(1)}, bf16[32,2304]{1,0:T(8,128)(2,1)S(1)}, bf16[32,2304]{1,0:T(8,128)(2,1)S(1)}, s32[8]{0:T(128)S(1)}) custom-call(s32[1,8]{1,0:T(1,128)} %refs_0_.3, s32[1,8]{1,0:T(1,128)S(1)} %collective-permute-done.refs_1_, s32[1,8]{1,0:T(1,128)S(1)} %collective-permute-done.1.refs_2_, ...), custom_call_target="tpu_custom_call" | custom-call | tf_op jit(solution)/shard_map/pick/pallas_call | solution.py:31
  11.8 2.1 %collective-permute-start.3 = (bf16[32,2304]{1,0:T(8,128)(2,1)S(1)}, bf16[32,2304]{1,0:T(8,128)(2,1)S(1)}, u32[]{:S(2)}, u32[]{:S(2)}) collective-permute-start(bf16[32,2304]{1,0:T(8,128)(2,1)S(1)} %get-tuple-element.51), channel_id=1, source_target_pairs={{0,8},{4,12},{8,0},{12,4},{1,9},{5,13},{9,1},{13,5},{2,10},{6,14},... | collective-permute-start | bytes 442376 | tf_op jit(solution)/shard_map/ppermute | solution.py:300
  13.9 0.7 %collective-permute-start.4 = (bf16[32,2304]{1,0:T(8,128)(2,1)S(1)}, bf16[32,2304]{1,0:T(8,128)(2,1)S(1)}, u32[]{:S(2)}, u32[]{:S(2)}) collective-permute-start(bf16[32,2304]{1,0:T(8,128)(2,1)S(1)} %get-tuple-element.52), channel_id=1, source_target_pairs={{0,12},{4,8},{8,4},{12,0},{1,13},{5,9},{9,5},{13,1},{2,14},{6,10},... | collective-permute-start | bytes 442376 | tf_op jit(solution)/shard_map/ppermute | solution.py:300
  14.5 0.8 %collective-permute-start.5 = (bf16[32,2304]{1,0:T(8,128)(2,1)S(1)}, bf16[32,2304]{1,0:T(8,128)(2,1)S(1)}, u32[]{:S(2)}, u32[]{:S(2)}) collective-permute-start(bf16[32,2304]{1,0:T(8,128)(2,1)S(1)} %get-tuple-element.61), channel_id=1, source_target_pairs={{0,4},{4,0},{8,12},{12,8},{1,5},{5,1},{9,13},{13,9},{2,6},{6,2},{1... | collective-permute-start | bytes 442376 | tf_op jit(solution)/shard_map/ppermute | solution.py:300
  15.3 10.1 %frozen.1 = (f32[2048,2048]{1,0:T(8,128)S(1)}, bf16[2048,2048]{1,0:T(8,128)(2,1)S(1)}, bf16[2048,1024]{1,0:T(8,128)(2,1)S(1)}) custom-call(bf16[2048,1024]{1,0:T(8,128)(2,1)S(1)} %get-tuple-element.53.refs_0_, bf16[512,1024]{1,0:T(8,128)(2,1)S(1)} %get-tuple-element.54.refs_1_, bf16[2048,1024]{1,0:T(8,128)(2,1)} %refs_2_.1, ...), custom_call_target="tpu_custom_call", output_to_operand_aliasing={{2}: (0, {})} | custom-call | tf_op jit(solution)/shard_map/frozen/pallas_call | solution.py:31
  25.4 0.0 collective-permute-done.3.refs_4_
  25.4 0.0 collective-permute-done.4.refs_5_
  25.4 0.0 collective-permute-done.5.refs_3_
  25.5 1.5 %collective-permute-start.6 = (bf16[128,256]{1,0:T(8,128)(2,1)S(1)}, bf16[128,256]{1,0:T(8,128)(2,1)S(1)}, u32[]{:S(2)}, u32[]{:S(2)}) collective-permute-start(bf16[128,256]{1,0:T(8,128)(2,1)S(1)} %pad_maximum_fusion.refs_6_), channel_id=1, source_target_pairs={{0,2},{1,3},{2,0},{3,1},{4,6},{5,7},{6,4},{7,5},{8,10},{9,11},{10,... | collective-permute-start | bytes 196616 | tf_op jit(solution)/shard_map/ppermute | solution.py:300
  27.0 3.0 %down.1 = (f32[16,2048]{1,0:T(8,128)S(1)}, bf16[128,2048]{1,0:T(8,128)(2,1)S(1)}) custom-call(s32[16]{0:T(128)S(1)} %get-tuple-element.60.refs_0_, bf16[2048,2048]{1,0:T(8,128)(2,1)S(1)} %get-tuple-element.70.refs_1_.refs_4_, bf16[32,2304]{1,0:T(8,128)(2,1)S(1)} %get-tuple-element.66.refs_5_.refs_2_, bf16[32,2304]{1,0:T(8,128)(2,1)S(1)} %collective-permute-done.5.refs_3_, ...), custom_call_target="tpu_custom_call" | custom-call | tf_op jit(solution)/shard_map/down/pallas_call | solution.py:31
  30.0 0.0 collective-permute-done.6
  30.0 0.1 collective-permute-start.8
  30.1 0.5 collective-permute-start.7
  30.6 0.8 %collective-permute-done.8 = f32[16,2048]{1,0:T(8,128)S(1)} collective-permute-done((f32[16,2048]{1,0:T(8,128)S(1)}, f32[16,2048]{1,0:T(8,128)S(1)}, u32[]{:S(2)}, u32[]{:S(2)}) %collective-permute-start.8) | collective-permute-done | bytes 131104 | tf_op jit(solution)/shard_map/ppermute | solution.py:300
  31.5 1.3 %collective-permute-start.9 = (f32[16,2048]{1,0:T(8,128)S(1)}, f32[16,2048]{1,0:T(8,128)S(1)}, u32[]{:S(2)}, u32[]{:S(2)}) collective-permute-start(f32[16,2048]{1,0:T(8,128)S(1)} %add.3.refs_5_.refs_1_), channel_id=1, source_target_pairs={{0,2},{1,3},{2,0},{3,1},{4,6},{5,7},{6,4},{7,5},{8,10},{9,11},{10,... | collective-permute-start | bytes 393224 | tf_op jit(solution)/shard_map/ppermute | solution.py:300
  32.7 0.0 collective-permute-done.7.refs_3_
  32.8 3.1 %up_grad_a.1 = (bf16[2048,128]{1,0:T(8,128)(2,1)S(1)}, f32[32,2048]{1,0:T(8,128)S(1)}, bf16[32,2048]{1,0:T(8,128)(2,1)S(1)}, bf16[32,2048]{1,0:T(8,128)(2,1)S(1)}, bf16[32,2048]{1,0:T(8,128)(2,1)S(1)}) custom-call(s32[16]{0:T(128)S(1)} %get-tuple-element.60.refs_0_, bf16[2048,1024]{1,0:T(8,128)(2,1)S(1)} %get-tuple-element.65.refs_1_.refs_3_, ...), custom_call_target="tpu_custom_call" | custom-call | tf_op jit(solution)/shard_map/up_grad_a/pallas_call | solution.py:31
  35.8 3.1 %collective-permute-start.10 = (bf16[32,2048]{1,0:T(8,128)(2,1)S(1)}, bf16[32,2048]{1,0:T(8,128)(2,1)S(1)}, u32[]{:S(2)}, u32[]{:S(2)}) collective-permute-start(bf16[32,2048]{1,0:T(8,128)(2,1)S(1)} %get-tuple-element.79), channel_id=1, source_target_pairs={{0,8},{4,12},{8,0},{12,4},{1,9},{5,13},{9,1},{13,5},{2,10},{6,14},... | collective-permute-start | bytes 393224 | tf_op jit(solution)/shard_map/ppermute | solution.py:300
  38.9 0.9 %collective-permute-start.11 = (bf16[32,2048]{1,0:T(8,128)(2,1)S(1)}, bf16[32,2048]{1,0:T(8,128)(2,1)S(1)}, u32[]{:S(2)}, u32[]{:S(2)}) collective-permute-start(bf16[32,2048]{1,0:T(8,128)(2,1)S(1)} %get-tuple-element.80), channel_id=1, source_target_pairs={{0,12},{4,8},{8,4},{12,0},{1,13},{5,9},{9,5},{13,1},{2,14},{6,10},... | collective-permute-start | bytes 393224 | tf_op jit(solution)/shard_map/ppermute | solution.py:300
  39.8 0.0 collective-permute-done.9.refs_2_
  39.8 0.9 %grad_b.1 = (f32[32,256]{1,0:T(8,128)S(1)}, bf16[32,2304]{1,0:T(8,128)(2,1)S(1)}, bf16[32,256]{1,0:T(8,128)(2,1)S(1)}, bf16[32,256]{1,0:T(8,128)(2,1)S(1)}) custom-call(s32[16]{0:T(128)S(1)} %get-tuple-element.60.refs_0_, f32[16,2048]{1,0:T(8,128)S(1)} %add.3.refs_5_.refs_1_, f32[16,2048]{1,0:T(8,128)S(1)} %collective-permute-done.9.refs_2_, ...), custom_call_target="tpu_custom_call" | custom-call | tf_op jit(solution)/shard_map/grad_b/pallas_call | solution.py:31
  40.7 0.8 %collective-permute-start.13 = (bf16[32,256]{1,0:T(8,128)(2,1)S(1)}, bf16[32,256]{1,0:T(8,128)(2,1)S(1)}, u32[]{:S(2)}, u32[]{:S(2)}) collective-permute-start(bf16[32,256]{1,0:T(8,128)(2,1)S(1)} %get-tuple-element.82), channel_id=1, source_target_pairs={{0,8},{4,12},{8,0},{12,4},{1,9},{5,13},{9,1},{13,5},{2,10},{6,14},... | collective-permute-start | bytes 49160 | tf_op jit(solution)/shard_map/ppermute | solution.py:300
  41.5 2.3 %collective-permute-start.14 = (bf16[32,256]{1,0:T(8,128)(2,1)S(1)}, bf16[32,256]{1,0:T(8,128)(2,1)S(1)}, u32[]{:S(2)}, u32[]{:S(2)}) collective-permute-start(bf16[32,256]{1,0:T(8,128)(2,1)S(1)} %get-tuple-element.83), channel_id=1, source_target_pairs={{0,12},{4,8},{8,4},{12,0},{1,13},{5,9},{9,5},{13,1},{2,14},{6,10},... | collective-permute-start | bytes 49160 | tf_op jit(solution)/shard_map/ppermute | solution.py:300
  43.8 0.5 collective-permute-start.12
  44.3 4.4 %token_gradient.1.refs_8_ = bf16[2048,2048]{1,0:T(8,128)(2,1)} custom-call(f32[2048,2048]{1,0:T(8,128)S(1)} %get-tuple-element.59.refs_0_, bf16[2048,128]{1,0:T(8,128)(2,1)S(1)} %get-tuple-element.74.refs_1_, bf16[128,2048]{1,0:T(8,128)(2,1)S(1)} %get-tuple-element.75.refs_2_, f32[32,256]{1,0:T(8,128)S(1)} %get-tuple-element.77.refs_3_.refs_7_), custom_call_target="tpu_custom_call" | custom-call | flops 4294967296 | tf_op jit(solution)/shard_map/token_gradient/pallas_call | solution.py:31
  48.7 0.7 %collective-permute-done.10.refs_1_ = bf16[32,2048]{1,0:T(8,128)(2,1)S(1)} collective-permute-done((bf16[32,2048]{1,0:T(8,128)(2,1)S(1)}, bf16[32,2048]{1,0:T(8,128)(2,1)S(1)}, u32[]{:S(2)}, u32[]{:S(2)}) %collective-permute-start.10) | collective-permute-done | bytes 131104 | tf_op jit(solution)/shard_map/ppermute | solution.py:300
  49.4 0.0 collective-permute-done.11.refs_2_
  49.4 2.7 %collective-permute-done.13.refs_4_ = bf16[32,256]{1,0:T(8,128)(2,1)S(1)} collective-permute-done((bf16[32,256]{1,0:T(8,128)(2,1)S(1)}, bf16[32,256]{1,0:T(8,128)(2,1)S(1)}, u32[]{:S(2)}, u32[]{:S(2)}) %collective-permute-start.13) | collective-permute-done | bytes 16416 | tf_op jit(solution)/shard_map/ppermute | solution.py:300
  52.1 0.0 collective-permute-done.14.refs_5_
  52.1 0.0 collective-permute-done.12.refs_3_
  52.1 1.7 %finish.1 = (f32[8,16,2048]{2,1,0:T(8,128)}, f32[8,16,256]{2,1,0:T(8,128)}) custom-call(s32[8]{0:T(128)S(1)} %get-tuple-element.78.refs_0_, bf16[32,2048]{1,0:T(8,128)(2,1)S(1)} %collective-permute-done.10.refs_1_, bf16[32,2048]{1,0:T(8,128)(2,1)S(1)} %collective-permute-done.11.refs_2_, bf16[32,2304]{1,0:T(8,128)(2,1)S(1)} %collective-permute-done.12.refs_3_, ...), custom_call_target="tpu_custom_call" | custom-call | tf_op jit(solution)/shard_map/finish/pallas_call | solution.py:31
  (7 shorter events, 0.0 us)
Async XLA Ops:
  0.6 8.5 %collective-permute-start.2 = (s32[1,8]{1,0:T(1,128)}, s32[1,8]{1,0:T(1,128)S(1)}, u32[]{:S(2)}, u32[]{:S(2)}) collective-permute-start(s32[1,8]{1,0:T(1,128)} %refs_0_.3), channel_id=1, source_target_pairs={{0,12},{4,8},{8,4},{12,0},{1,13},{5,9},{9,5},{13,1},{2,14},{6,10},... | collective-permute-start | bytes 104 | tf_op jit(solution)/shard_map/ppermute | solution.py:300
  5.7 4.6 %collective-permute-start.1 = (s32[1,8]{1,0:T(1,128)}, s32[1,8]{1,0:T(1,128)S(1)}, u32[]{:S(2)}, u32[]{:S(2)}) collective-permute-start(s32[1,8]{1,0:T(1,128)} %refs_0_.3), channel_id=1, source_target_pairs={{0,8},{4,12},{8,0},{12,4},{1,9},{5,13},{9,1},{13,5},{2,10},{6,14},... | collective-permute-start | bytes 104 | tf_op jit(solution)/shard_map/ppermute | solution.py:300
  5.7 4.6 %collective-permute-start = (s32[1,8]{1,0:T(1,128)}, s32[1,8]{1,0:T(1,128)S(1)}, u32[]{:S(2)}, u32[]{:S(2)}) collective-permute-start(s32[1,8]{1,0:T(1,128)} %refs_0_.3), channel_id=1, source_target_pairs={{0,4},{4,0},{8,12},{12,8},{1,5},{5,1},{9,13},{13,9},{2,6},{6,2},{1... | collective-permute-start | bytes 104 | tf_op jit(solution)/shard_map/ppermute | solution.py:300
  11.8 13.6 %collective-permute-start.3 = (bf16[32,2304]{1,0:T(8,128)(2,1)S(1)}, bf16[32,2304]{1,0:T(8,128)(2,1)S(1)}, u32[]{:S(2)}, u32[]{:S(2)}) collective-permute-start(bf16[32,2304]{1,0:T(8,128)(2,1)S(1)} %get-tuple-element.51), channel_id=1, source_target_pairs={{0,8},{4,12},{8,0},{12,4},{1,9},{5,13},{9,1},{13,5},{2,10},{6,14},... | collective-permute-start | bytes 442376 | tf_op jit(solution)/shard_map/ppermute | solution.py:300
  13.9 11.6 %collective-permute-start.4 = (bf16[32,2304]{1,0:T(8,128)(2,1)S(1)}, bf16[32,2304]{1,0:T(8,128)(2,1)S(1)}, u32[]{:S(2)}, u32[]{:S(2)}) collective-permute-start(bf16[32,2304]{1,0:T(8,128)(2,1)S(1)} %get-tuple-element.52), channel_id=1, source_target_pairs={{0,12},{4,8},{8,4},{12,0},{1,13},{5,9},{9,5},{13,1},{2,14},{6,10},... | collective-permute-start | bytes 442376 | tf_op jit(solution)/shard_map/ppermute | solution.py:300
  14.5 10.9 %collective-permute-start.5 = (bf16[32,2304]{1,0:T(8,128)(2,1)S(1)}, bf16[32,2304]{1,0:T(8,128)(2,1)S(1)}, u32[]{:S(2)}, u32[]{:S(2)}) collective-permute-start(bf16[32,2304]{1,0:T(8,128)(2,1)S(1)} %get-tuple-element.61), channel_id=1, source_target_pairs={{0,4},{4,0},{8,12},{12,8},{1,5},{5,1},{9,13},{13,9},{2,6},{6,2},{1... | collective-permute-start | bytes 442376 | tf_op jit(solution)/shard_map/ppermute | solution.py:300
  25.5 4.5 %collective-permute-start.6 = (bf16[128,256]{1,0:T(8,128)(2,1)S(1)}, bf16[128,256]{1,0:T(8,128)(2,1)S(1)}, u32[]{:S(2)}, u32[]{:S(2)}) collective-permute-start(bf16[128,256]{1,0:T(8,128)(2,1)S(1)} %pad_maximum_fusion.refs_6_), channel_id=1, source_target_pairs={{0,2},{1,3},{2,0},{3,1},{4,6},{5,7},{6,4},{7,5},{8,10},{9,11},{10,... | collective-permute-start | bytes 196616 | tf_op jit(solution)/shard_map/ppermute | solution.py:300
  30.0 1.4 %collective-permute-start.8 = (f32[16,2048]{1,0:T(8,128)S(1)}, f32[16,2048]{1,0:T(8,128)S(1)}, u32[]{:S(2)}, u32[]{:S(2)}) collective-permute-start(f32[16,2048]{1,0:T(8,128)S(1)} %get-tuple-element.73), channel_id=1, source_target_pairs={{0,1},{1,0},{2,3},{3,2},{4,5},{5,4},{6,7},{7,6},{8,9},{9,8},{10,11... | collective-permute-start | bytes 393224 | tf_op jit(solution)/shard_map/ppermute | solution.py:300
  30.1 2.6 %collective-permute-start.7 = (bf16[256,256]{1,0:T(8,128)(2,1)S(1)}, bf16[256,256]{1,0:T(8,128)(2,1)S(1)}, u32[]{:S(2)}, u32[]{:S(2)}) collective-permute-start(bf16[256,256]{1,0:T(8,128)(2,1)S(1)} %constant_dynamic-update-slice_fusion.refs_2_), channel_id=1, source_target_pairs={{0,1},{1,0},{2,3},{3,2},{4,5},{5,4},{6,7},{7,6},{8,9},{9,8},{10,11... | collective-permute-start | bytes 393224 | tf_op jit(solution)/shard_map/ppermute | solution.py:300
  31.5 8.3 %collective-permute-start.9 = (f32[16,2048]{1,0:T(8,128)S(1)}, f32[16,2048]{1,0:T(8,128)S(1)}, u32[]{:S(2)}, u32[]{:S(2)}) collective-permute-start(f32[16,2048]{1,0:T(8,128)S(1)} %add.3.refs_5_.refs_1_), channel_id=1, source_target_pairs={{0,2},{1,3},{2,0},{3,1},{4,6},{5,7},{6,4},{7,5},{8,10},{9,11},{10,... | collective-permute-start | bytes 393224 | tf_op jit(solution)/shard_map/ppermute | solution.py:300
  35.8 13.6 %collective-permute-start.10 = (bf16[32,2048]{1,0:T(8,128)(2,1)S(1)}, bf16[32,2048]{1,0:T(8,128)(2,1)S(1)}, u32[]{:S(2)}, u32[]{:S(2)}) collective-permute-start(bf16[32,2048]{1,0:T(8,128)(2,1)S(1)} %get-tuple-element.79), channel_id=1, source_target_pairs={{0,8},{4,12},{8,0},{12,4},{1,9},{5,13},{9,1},{13,5},{2,10},{6,14},... | collective-permute-start | bytes 393224 | tf_op jit(solution)/shard_map/ppermute | solution.py:300
  38.9 10.5 %collective-permute-start.11 = (bf16[32,2048]{1,0:T(8,128)(2,1)S(1)}, bf16[32,2048]{1,0:T(8,128)(2,1)S(1)}, u32[]{:S(2)}, u32[]{:S(2)}) collective-permute-start(bf16[32,2048]{1,0:T(8,128)(2,1)S(1)} %get-tuple-element.80), channel_id=1, source_target_pairs={{0,12},{4,8},{8,4},{12,0},{1,13},{5,9},{9,5},{13,1},{2,14},{6,10},... | collective-permute-start | bytes 393224 | tf_op jit(solution)/shard_map/ppermute | solution.py:300
  40.7 11.4 %collective-permute-start.13 = (bf16[32,256]{1,0:T(8,128)(2,1)S(1)}, bf16[32,256]{1,0:T(8,128)(2,1)S(1)}, u32[]{:S(2)}, u32[]{:S(2)}) collective-permute-start(bf16[32,256]{1,0:T(8,128)(2,1)S(1)} %get-tuple-element.82), channel_id=1, source_target_pairs={{0,8},{4,12},{8,0},{12,4},{1,9},{5,13},{9,1},{13,5},{2,10},{6,14},... | collective-permute-start | bytes 49160 | tf_op jit(solution)/shard_map/ppermute | solution.py:300
  41.5 10.6 %collective-permute-start.14 = (bf16[32,256]{1,0:T(8,128)(2,1)S(1)}, bf16[32,256]{1,0:T(8,128)(2,1)S(1)}, u32[]{:S(2)}, u32[]{:S(2)}) collective-permute-start(bf16[32,256]{1,0:T(8,128)(2,1)S(1)} %get-tuple-element.83), channel_id=1, source_target_pairs={{0,12},{4,8},{8,4},{12,0},{1,13},{5,9},{9,5},{13,1},{2,14},{6,10},... | collective-permute-start | bytes 49160 | tf_op jit(solution)/shard_map/ppermute | solution.py:300
  43.8 8.3 %collective-permute-start.12 = (bf16[32,2304]{1,0:T(8,128)(2,1)S(1)}, bf16[32,2304]{1,0:T(8,128)(2,1)S(1)}, u32[]{:S(2)}, u32[]{:S(2)}) collective-permute-start(bf16[32,2304]{1,0:T(8,128)(2,1)S(1)} %get-tuple-element.81), channel_id=1, source_target_pairs={{0,4},{4,0},{8,12},{12,8},{1,5},{5,1},{9,13},{13,9},{2,6},{6,2},{1... | collective-permute-start | bytes 442376 | tf_op jit(solution)/shard_map/ppermute | solution.py:300

commit v4 on v3

--- a/solution.py
+++ b/solution.py
@@ -146,23 +146,36 @@
     wait_all(toks)
 
 
+def up_terms(upstream, rows, piece, owners, width):
+    cols = piece.shape[1]
+    tp_rank = lax.axis_index("tp")
+    acc = None
+    for i, s in enumerate(owners):
+        at = pl.multiple_of(jnp.bitwise_xor(tp_rank, s) * cols, cols)
+        part = lax.dot_general(
+            upstream[rows, pl.ds(at, cols)], piece[i * width : (i + 1) * width, :], NT, preferred_element_type=F32
+        )
+        acc = part if acc is None else acc + part
+    return acc
+
+
+def up_first_kernel(chunk, order, upstream, held_q, out):
+    for r in range(out.shape[0] // chunk):
+        rows = slice(r * chunk, (r + 1) * chunk)
+        out[rows, :] = up_terms(upstream, rows, held_q, order, out.shape[1])
+
+
 def up_kernel(rep, cap, rank, nb, order, *refs):
-    vslot, upstream, held_q, came_q, tokens = refs[:5]
+    vslot, upstream, up_first, came_q, tokens = refs[:5]
     up_out = refs[6]
-    grads, b_all = refs[7:-1], refs[-1]
+    grads = refs[7:]
     width = rep * cap * rank
     per = cap * rank
-    cols = held_q.shape[1]
-    tp_rank = lax.axis_index("tp")
-    for i, s in enumerate(order):
-        for j, piece in ((0, held_q), (1, came_q)):
-            at = pl.multiple_of(jnp.bitwise_xor(tp_rank, s ^ j) * cols, cols)
-            b_all[:, pl.ds(at, cols)] = piece[i * width : (i + 1) * width, :]
     chunk = 4
     lane_slot = lax.broadcasted_iota(I32, (BLOCK, width), 1) // rank
     for r in range(nb // chunk):
         rows = slice(r * chunk * BLOCK, (r + 1) * chunk * BLOCK)
-        acc = lax.dot_general(upstream[rows, :], b_all[...], NT, preferred_element_type=F32)
+        acc = up_first[rows, :] + up_terms(upstream, rows, came_q, [s ^ 1 for s in order], width)
         acc = (SCALE * acc).astype(BF16)
         for b in range(chunk):
             blk = r * chunk + b
@@ -380,8 +393,19 @@
         came_q = swap("tp", held_q, bit)
         if bit == tp // 2:
             came_q, down = tie((came_q, down))
+    up_first = kernel(
+        functools.partial(up_first_kernel, chunk, order),
+        "up_first",
+        pltpu.VMEM((rows, depth), F32),
+        [VMEM] * 2,
+        VMEM,
+        [upstream_v, held_q],
+    )
     for bit in bits(tp)[:-1]:
-        down = down + swap("tp", down, bit)
+        came = swap("tp", down, bit)
+        if bit == 1:
+            came, up_first = tie((came, up_first))
+        down = down + came
     down_there = swap("tp", down, tp // 2)
 
     up_scaled, *grads_a = kernel(
@@ -390,8 +414,7 @@
         [struct((rows, depth), BF16), struct((per, width), F32)] + [struct((per, width), BF16)] * (rep - 1),
         [SMEM] + [VMEM] * 4 + [ANY],
         [VMEM] * (rep + 1),
-        [vslot, upstream_v, held_q, came_q, tokens_v, down],
-        [pltpu.VMEM((depth, outs), BF16)],
+        [vslot, upstream_v, up_first, came_q, tokens_v, down],
     )
     grads_b = kernel(
         functools.partial(grad_b_kernel, rep, cap, rank, nb),

time: 54.1 us -> 53.6 us (level)
  waiting for transfers between devices: 5.42 us -> 4.56 us
    ppermute x15, waiting for transfers between devices: 5.42 us -> 4.56 us  [swap(): lax.ppermute(x, axis, [(i, i ^ s) for i in range(lax.axis_size(axis))])]
    pallas_call x8 -> x9, Pallas kernels: 27.3 us -> 27.7 us  [kernel(): pl.pallas_call(body, out_shape=outs, in_specs=in_specs, out_specs=out_spe...]
  transfers between devices with their start and end apart: 15 -> 15, of which waited for: 4 -> 4; matrix products, arithmetic and copies ran while one was open for 0% -> 0% of each run, Pallas kernels for 45% -> 46%
where the time goes in v4:
time: 53.6 us; the launch traced here: 53.5 us
  Pallas kernels  27.7 us (52%)
  starting transfers between devices  20.2 us (38%)
  waiting for transfers between devices  4.56 us (9%)
  between operations  0.96 us (2%)
    pallas_call x9, Pallas kernels, kernel(): pl.pallas_call(body, out_shape=outs, in_specs=in_specs, out_specs=out_spe...  27.7 us
    ppermute x15, starting transfers between devices, swap(): lax.ppermute(x, axis, [(i, i ^ s) for i in range(lax.axis_size(axis))])  20.2 us
    ppermute x15, waiting for transfers between devices, swap(): lax.ppermute(x, axis, [(i, i ^ s) for i in range(lax.axis_size(axis))])  4.56 us
  transfers between devices with their start and end apart: 15, of which 4 were waited for; matrix products, arithmetic and copies ran while one was open for 0% of the time, Pallas kernels for 46%

profile of v4, /device:TPU:0, one launch (start us, length us, event | category | flops | bytes accessed | tf_op | source)
XLA Modules:
  0.0 53.5 jit_solution(3512997533917477091)
XLA Ops:
  0.6 5.1 %collective-permute-start.2 = (s32[1,8]{1,0:T(1,128)}, s32[1,8]{1,0:T(1,128)S(1)}, u32[]{:S(2)}, u32[]{:S(2)}) collective-permute-start(s32[1,8]{1,0:T(1,128)} %refs_0_.3), channel_id=1, source_target_pairs={{0,12},{4,8},{8,4},{12,0},{1,13},{5,9},{9,5},{13,1},{2,14},{6,10},... | collective-permute-start | bytes 104 | tf_op jit(solution)/shard_map/ppermute | solution.py:313
  5.7 0.0 collective-permute-start.1
  5.7 0.6 %collective-permute-start = (s32[1,8]{1,0:T(1,128)}, s32[1,8]{1,0:T(1,128)S(1)}, u32[]{:S(2)}, u32[]{:S(2)}) collective-permute-start(s32[1,8]{1,0:T(1,128)} %refs_0_.3), channel_id=1, source_target_pairs={{0,4},{4,0},{8,12},{12,8},{1,5},{5,1},{9,13},{13,9},{2,6},{6,2},{1... | collective-permute-start | bytes 104 | tf_op jit(solution)/shard_map/ppermute | solution.py:313
  6.4 2.7 %plan.1 = (s32[16]{0:T(128)S(1)}, bf16[128,2304]{1,0:T(8,128)(2,1)S(1)}, bf16[2048,1024]{1,0:T(8,128)(2,1)S(1)}, bf16[512,1024]{1,0:T(8,128)(2,1)S(1)}) custom-call(s32[1,8]{1,0:T(1,128)} %refs_0_.3, s32[16,128]{1,0:T(8,128)} %bitcast.5, bf16[128,2048]{1,0:T(8,128)(2,1)} %bitcast.3, bf16[128,256]{1,0:T(8,128)(2,1)} %bitcast.4, bf16[2048,1024]{1,0:T(8,128)(2,1)} %refs_4_.3, ...), custom_call_target="tpu_custom_call" | custom-call | tf_op jit(solution)/shard_map/plan/pallas_call | solution.py:31
  9.1 0.0 collective-permute-done.2.refs_3_
  9.2 1.2 %collective-permute-done.1.refs_2_ = s32[1,8]{1,0:T(1,128)S(1)} collective-permute-done((s32[1,8]{1,0:T(1,128)}, s32[1,8]{1,0:T(1,128)S(1)}, u32[]{:S(2)}, u32[]{:S(2)}) %collective-permute-start.1) | collective-permute-done | bytes 64 | tf_op jit(solution)/shard_map/ppermute | solution.py:313
  10.3 0.0 collective-permute-done.refs_1_
  10.3 1.4 %pick.1 = (bf16[32,2304]{1,0:T(8,128)(2,1)S(1)}, bf16[32,2304]{1,0:T(8,128)(2,1)S(1)}, bf16[32,2304]{1,0:T(8,128)(2,1)S(1)}, bf16[32,2304]{1,0:T(8,128)(2,1)S(1)}, s32[8]{0:T(128)S(1)}) custom-call(s32[1,8]{1,0:T(1,128)} %refs_0_.3, s32[1,8]{1,0:T(1,128)S(1)} %collective-permute-done.refs_1_, s32[1,8]{1,0:T(1,128)S(1)} %collective-permute-done.1.refs_2_, ...), custom_call_target="tpu_custom_call" | custom-call | tf_op jit(solution)/shard_map/pick/pallas_call | solution.py:31
  11.8 2.1 %collective-permute-start.3 = (bf16[32,2304]{1,0:T(8,128)(2,1)S(1)}, bf16[32,2304]{1,0:T(8,128)(2,1)S(1)}, u32[]{:S(2)}, u32[]{:S(2)}) collective-permute-start(bf16[32,2304]{1,0:T(8,128)(2,1)S(1)} %get-tuple-element.53), channel_id=1, source_target_pairs={{0,8},{4,12},{8,0},{12,4},{1,9},{5,13},{9,1},{13,5},{2,10},{6,14},... | collective-permute-start | bytes 442376 | tf_op jit(solution)/shard_map/ppermute | solution.py:313
  13.9 0.7 %collective-permute-start.4 = (bf16[32,2304]{1,0:T(8,128)(2,1)S(1)}, bf16[32,2304]{1,0:T(8,128)(2,1)S(1)}, u32[]{:S(2)}, u32[]{:S(2)}) collective-permute-start(bf16[32,2304]{1,0:T(8,128)(2,1)S(1)} %get-tuple-element.54), channel_id=1, source_target_pairs={{0,12},{4,8},{8,4},{12,0},{1,13},{5,9},{9,5},{13,1},{2,14},{6,10},... | collective-permute-start | bytes 442376 | tf_op jit(solution)/shard_map/ppermute | solution.py:313
  14.5 0.8 %collective-permute-start.5 = (bf16[32,2304]{1,0:T(8,128)(2,1)S(1)}, bf16[32,2304]{1,0:T(8,128)(2,1)S(1)}, u32[]{:S(2)}, u32[]{:S(2)}) collective-permute-start(bf16[32,2304]{1,0:T(8,128)(2,1)S(1)} %get-tuple-element.63), channel_id=1, source_target_pairs={{0,4},{4,0},{8,12},{12,8},{1,5},{5,1},{9,13},{13,9},{2,6},{6,2},{1... | collective-permute-start | bytes 442376 | tf_op jit(solution)/shard_map/ppermute | solution.py:313
  15.3 10.1 %frozen.1 = (f32[2048,2048]{1,0:T(8,128)S(1)}, bf16[2048,2048]{1,0:T(8,128)(2,1)S(1)}, bf16[2048,1024]{1,0:T(8,128)(2,1)S(1)}) custom-call(bf16[2048,1024]{1,0:T(8,128)(2,1)S(1)} %get-tuple-element.55.refs_0_, bf16[512,1024]{1,0:T(8,128)(2,1)S(1)} %get-tuple-element.56.refs_1_, bf16[2048,1024]{1,0:T(8,128)(2,1)} %refs_2_.1, ...), custom_call_target="tpu_custom_call", output_to_operand_aliasing={{2}: (0, {})} | custom-call | tf_op jit(solution)/shard_map/frozen/pallas_call | solution.py:31
  25.4 0.0 collective-permute-done.3.refs_4_
  25.4 0.0 collective-permute-done.4.refs_5_
  25.4 0.0 collective-permute-done.5.refs_3_
  25.5 1.5 %collective-permute-start.6 = (bf16[128,256]{1,0:T(8,128)(2,1)S(1)}, bf16[128,256]{1,0:T(8,128)(2,1)S(1)}, u32[]{:S(2)}, u32[]{:S(2)}) collective-permute-start(bf16[128,256]{1,0:T(8,128)(2,1)S(1)} %pad_maximum_fusion.refs_6_), channel_id=1, source_target_pairs={{0,2},{1,3},{2,0},{3,1},{4,6},{5,7},{6,4},{7,5},{8,10},{9,11},{10,... | collective-permute-start | bytes 196616 | tf_op jit(solution)/shard_map/ppermute | solution.py:313
  27.0 3.0 %down.1 = (f32[16,2048]{1,0:T(8,128)S(1)}, bf16[128,2048]{1,0:T(8,128)(2,1)S(1)}) custom-call(s32[16]{0:T(128)S(1)} %get-tuple-element.62.refs_0_, bf16[2048,2048]{1,0:T(8,128)(2,1)S(1)} %get-tuple-element.72.refs_1_.refs_4_, bf16[32,2304]{1,0:T(8,128)(2,1)S(1)} %get-tuple-element.68.refs_5_.refs_2_, bf16[32,2304]{1,0:T(8,128)(2,1)S(1)} %collective-permute-done.5.refs_3_, ...), custom_call_target="tpu_custom_call" | custom-call | tf_op jit(solution)/shard_map/down/pallas_call | solution.py:31
  30.0 0.0 collective-permute-done.6
  30.0 0.1 collective-permute-start.7
  30.1 0.5 collective-permute-start.8
  30.6 0.7 %up_first.1.refs_2_ = f32[2048,128]{1,0:T(8,128)S(1)} custom-call(bf16[2048,1024]{1,0:T(8,128)(2,1)S(1)} %get-tuple-element.67.upstream.refs_1_.refs_3_, bf16[256,256]{1,0:T(8,128)(2,1)S(1)} %constant_dynamic-update-slice_fusion.held_q), custom_call_target="tpu_custom_call" | custom-call | tf_op jit(solution)/shard_map/up_first/pallas_call | solution.py:31
  31.3 0.1 collective-permute-done.7
  31.5 1.3 %collective-permute-start.9 = (f32[16,2048]{1,0:T(8,128)S(1)}, f32[16,2048]{1,0:T(8,128)S(1)}, u32[]{:S(2)}, u32[]{:S(2)}) collective-permute-start(f32[16,2048]{1,0:T(8,128)S(1)} %add.3.refs_5_.refs_1_), channel_id=1, source_target_pairs={{0,2},{1,3},{2,0},{3,1},{4,6},{5,7},{6,4},{7,5},{8,10},{9,11},{10,... | collective-permute-start | bytes 393224 | tf_op jit(solution)/shard_map/ppermute | solution.py:313
  32.7 0.0 collective-permute-done.8.refs_3_
  32.8 2.6 %up_grad_a.1 = (bf16[2048,128]{1,0:T(8,128)(2,1)S(1)}, f32[32,2048]{1,0:T(8,128)S(1)}, bf16[32,2048]{1,0:T(8,128)(2,1)S(1)}, bf16[32,2048]{1,0:T(8,128)(2,1)S(1)}, bf16[32,2048]{1,0:T(8,128)(2,1)S(1)}) custom-call(s32[16]{0:T(128)S(1)} %get-tuple-element.62.refs_0_, bf16[2048,1024]{1,0:T(8,128)(2,1)S(1)} %get-tuple-element.67.upstream.refs_1_.refs_3_, ...), custom_call_target="tpu_custom_call" | custom-call | tf_op jit(solution)/shard_map/up_grad_a/pallas_call | solution.py:31
  35.3 3.1 %collective-permute-start.10 = (bf16[32,2048]{1,0:T(8,128)(2,1)S(1)}, bf16[32,2048]{1,0:T(8,128)(2,1)S(1)}, u32[]{:S(2)}, u32[]{:S(2)}) collective-permute-start(bf16[32,2048]{1,0:T(8,128)(2,1)S(1)} %get-tuple-element.83), channel_id=1, source_target_pairs={{0,8},{4,12},{8,0},{12,4},{1,9},{5,13},{9,1},{13,5},{2,10},{6,14},... | collective-permute-start | bytes 393224 | tf_op jit(solution)/shard_map/ppermute | solution.py:313
  38.4 0.9 %collective-permute-start.11 = (bf16[32,2048]{1,0:T(8,128)(2,1)S(1)}, bf16[32,2048]{1,0:T(8,128)(2,1)S(1)}, u32[]{:S(2)}, u32[]{:S(2)}) collective-permute-start(bf16[32,2048]{1,0:T(8,128)(2,1)S(1)} %get-tuple-element.84), channel_id=1, source_target_pairs={{0,12},{4,8},{8,4},{12,0},{1,13},{5,9},{9,5},{13,1},{2,14},{6,10},... | collective-permute-start | bytes 393224 | tf_op jit(solution)/shard_map/ppermute | solution.py:313
  39.3 0.0 collective-permute-done.9.refs_2_
  39.3 1.1 %grad_b.1 = (f32[32,256]{1,0:T(8,128)S(1)}, bf16[32,2304]{1,0:T(8,128)(2,1)S(1)}, bf16[32,256]{1,0:T(8,128)(2,1)S(1)}, bf16[32,256]{1,0:T(8,128)(2,1)S(1)}) custom-call(s32[16]{0:T(128)S(1)} %get-tuple-element.62.refs_0_, f32[16,2048]{1,0:T(8,128)S(1)} %add.3.refs_5_.refs_1_, f32[16,2048]{1,0:T(8,128)S(1)} %collective-permute-done.9.refs_2_, ...), custom_call_target="tpu_custom_call" | custom-call | tf_op jit(solution)/shard_map/grad_b/pallas_call | solution.py:31
  40.3 0.9 %collective-permute-start.13 = (bf16[32,256]{1,0:T(8,128)(2,1)S(1)}, bf16[32,256]{1,0:T(8,128)(2,1)S(1)}, u32[]{:S(2)}, u32[]{:S(2)}) collective-permute-start(bf16[32,256]{1,0:T(8,128)(2,1)S(1)} %get-tuple-element.86), channel_id=1, source_target_pairs={{0,8},{4,12},{8,0},{12,4},{1,9},{5,13},{9,1},{13,5},{2,10},{6,14},... | collective-permute-start | bytes 49160 | tf_op jit(solution)/shard_map/ppermute | solution.py:313
  41.2 2.2 %collective-permute-start.14 = (bf16[32,256]{1,0:T(8,128)(2,1)S(1)}, bf16[32,256]{1,0:T(8,128)(2,1)S(1)}, u32[]{:S(2)}, u32[]{:S(2)}) collective-permute-start(bf16[32,256]{1,0:T(8,128)(2,1)S(1)} %get-tuple-element.87), channel_id=1, source_target_pairs={{0,12},{4,8},{8,4},{12,0},{1,13},{5,9},{9,5},{13,1},{2,14},{6,10},... | collective-permute-start | bytes 49160 | tf_op jit(solution)/shard_map/ppermute | solution.py:313
  43.5 0.5 collective-permute-start.12
  43.9 4.4 %token_gradient.1.refs_8_ = bf16[2048,2048]{1,0:T(8,128)(2,1)} custom-call(f32[2048,2048]{1,0:T(8,128)S(1)} %get-tuple-element.61.refs_0_, bf16[2048,128]{1,0:T(8,128)(2,1)S(1)} %get-tuple-element.78.refs_1_, bf16[128,2048]{1,0:T(8,128)(2,1)S(1)} %get-tuple-element.79.refs_2_, f32[32,256]{1,0:T(8,128)S(1)} %get-tuple-element.81.refs_3_.refs_7_), custom_call_target="tpu_custom_call" | custom-call | flops 4294967296 | tf_op jit(solution)/shard_map/token_gradient/pallas_call | solution.py:31
  48.3 0.6 %collective-permute-done.10.refs_1_ = bf16[32,2048]{1,0:T(8,128)(2,1)S(1)} collective-permute-done((bf16[32,2048]{1,0:T(8,128)(2,1)S(1)}, bf16[32,2048]{1,0:T(8,128)(2,1)S(1)}, u32[]{:S(2)}, u32[]{:S(2)}) %collective-permute-start.10) | collective-permute-done | bytes 131104 | tf_op jit(solution)/shard_map/ppermute | solution.py:313
  48.9 0.0 collective-permute-done.11.refs_2_
  48.9 2.7 %collective-permute-done.13.refs_4_ = bf16[32,256]{1,0:T(8,128)(2,1)S(1)} collective-permute-done((bf16[32,256]{1,0:T(8,128)(2,1)S(1)}, bf16[32,256]{1,0:T(8,128)(2,1)S(1)}, u32[]{:S(2)}, u32[]{:S(2)}) %collective-permute-start.13) | collective-permute-done | bytes 16416 | tf_op jit(solution)/shard_map/ppermute | solution.py:313
  51.6 0.0 collective-permute-done.14.refs_5_
  51.6 0.0 collective-permute-done.12.refs_3_
  51.6 1.7 %finish.1 = (f32[8,16,2048]{2,1,0:T(8,128)}, f32[8,16,256]{2,1,0:T(8,128)}) custom-call(s32[8]{0:T(128)S(1)} %get-tuple-element.82.refs_0_, bf16[32,2048]{1,0:T(8,128)(2,1)S(1)} %collective-permute-done.10.refs_1_, bf16[32,2048]{1,0:T(8,128)(2,1)S(1)} %collective-permute-done.11.refs_2_, bf16[32,2304]{1,0:T(8,128)(2,1)S(1)} %collective-permute-done.12.refs_3_, ...), custom_call_target="tpu_custom_call" | custom-call | tf_op jit(solution)/shard_map/finish/pallas_call | solution.py:31
  (7 shorter events, 0.0 us)
Async XLA Ops:
  0.6 8.5 %collective-permute-start.2 = (s32[1,8]{1,0:T(1,128)}, s32[1,8]{1,0:T(1,128)S(1)}, u32[]{:S(2)}, u32[]{:S(2)}) collective-permute-start(s32[1,8]{1,0:T(1,128)} %refs_0_.3), channel_id=1, source_target_pairs={{0,12},{4,8},{8,4},{12,0},{1,13},{5,9},{9,5},{13,1},{2,14},{6,10},... | collective-permute-start | bytes 104 | tf_op jit(solution)/shard_map/ppermute | solution.py:313
  5.7 4.6 %collective-permute-start.1 = (s32[1,8]{1,0:T(1,128)}, s32[1,8]{1,0:T(1,128)S(1)}, u32[]{:S(2)}, u32[]{:S(2)}) collective-permute-start(s32[1,8]{1,0:T(1,128)} %refs_0_.3), channel_id=1, source_target_pairs={{0,8},{4,12},{8,0},{12,4},{1,9},{5,13},{9,1},{13,5},{2,10},{6,14},... | collective-permute-start | bytes 104 | tf_op jit(solution)/shard_map/ppermute | solution.py:313
  5.7 4.6 %collective-permute-start = (s32[1,8]{1,0:T(1,128)}, s32[1,8]{1,0:T(1,128)S(1)}, u32[]{:S(2)}, u32[]{:S(2)}) collective-permute-start(s32[1,8]{1,0:T(1,128)} %refs_0_.3), channel_id=1, source_target_pairs={{0,4},{4,0},{8,12},{12,8},{1,5},{5,1},{9,13},{13,9},{2,6},{6,2},{1... | collective-permute-start | bytes 104 | tf_op jit(solution)/shard_map/ppermute | solution.py:313
  11.8 13.6 %collective-permute-start.3 = (bf16[32,2304]{1,0:T(8,128)(2,1)S(1)}, bf16[32,2304]{1,0:T(8,128)(2,1)S(1)}, u32[]{:S(2)}, u32[]{:S(2)}) collective-permute-start(bf16[32,2304]{1,0:T(8,128)(2,1)S(1)} %get-tuple-element.53), channel_id=1, source_target_pairs={{0,8},{4,12},{8,0},{12,4},{1,9},{5,13},{9,1},{13,5},{2,10},{6,14},... | collective-permute-start | bytes 442376 | tf_op jit(solution)/shard_map/ppermute | solution.py:313
  13.9 11.6 %collective-permute-start.4 = (bf16[32,2304]{1,0:T(8,128)(2,1)S(1)}, bf16[32,2304]{1,0:T(8,128)(2,1)S(1)}, u32[]{:S(2)}, u32[]{:S(2)}) collective-permute-start(bf16[32,2304]{1,0:T(8,128)(2,1)S(1)} %get-tuple-element.54), channel_id=1, source_target_pairs={{0,12},{4,8},{8,4},{12,0},{1,13},{5,9},{9,5},{13,1},{2,14},{6,10},... | collective-permute-start | bytes 442376 | tf_op jit(solution)/shard_map/ppermute | solution.py:313
  14.5 10.9 %collective-permute-start.5 = (bf16[32,2304]{1,0:T(8,128)(2,1)S(1)}, bf16[32,2304]{1,0:T(8,128)(2,1)S(1)}, u32[]{:S(2)}, u32[]{:S(2)}) collective-permute-start(bf16[32,2304]{1,0:T(8,128)(2,1)S(1)} %get-tuple-element.63), channel_id=1, source_target_pairs={{0,4},{4,0},{8,12},{12,8},{1,5},{5,1},{9,13},{13,9},{2,6},{6,2},{1... | collective-permute-start | bytes 442376 | tf_op jit(solution)/shard_map/ppermute | solution.py:313
  25.5 4.5 %collective-permute-start.6 = (bf16[128,256]{1,0:T(8,128)(2,1)S(1)}, bf16[128,256]{1,0:T(8,128)(2,1)S(1)}, u32[]{:S(2)}, u32[]{:S(2)}) collective-permute-start(bf16[128,256]{1,0:T(8,128)(2,1)S(1)} %pad_maximum_fusion.refs_6_), channel_id=1, source_target_pairs={{0,2},{1,3},{2,0},{3,1},{4,6},{5,7},{6,4},{7,5},{8,10},{9,11},{10,... | collective-permute-start | bytes 196616 | tf_op jit(solution)/shard_map/ppermute | solution.py:313
  30.0 1.4 %collective-permute-start.7 = (f32[16,2048]{1,0:T(8,128)S(1)}, f32[16,2048]{1,0:T(8,128)S(1)}, u32[]{:S(2)}, u32[]{:S(2)}) collective-permute-start(f32[16,2048]{1,0:T(8,128)S(1)} %get-tuple-element.74), channel_id=1, source_target_pairs={{0,1},{1,0},{2,3},{3,2},{4,5},{5,4},{6,7},{7,6},{8,9},{9,8},{10,11... | collective-permute-start | bytes 393224 | tf_op jit(solution)/shard_map/ppermute | solution.py:313
  30.1 2.6 %collective-permute-start.8 = (bf16[256,256]{1,0:T(8,128)(2,1)S(1)}, bf16[256,256]{1,0:T(8,128)(2,1)S(1)}, u32[]{:S(2)}, u32[]{:S(2)}) collective-permute-start(bf16[256,256]{1,0:T(8,128)(2,1)S(1)} %constant_dynamic-update-slice_fusion.held_q), channel_id=1, source_target_pairs={{0,1},{1,0},{2,3},{3,2},{4,5},{5,4},{6,7},{7,6},{8,9},{9,8},{10,11... | collective-permute-start | bytes 393224 | tf_op jit(solution)/shard_map/ppermute | solution.py:313
  31.5 7.8 %collective-permute-start.9 = (f32[16,2048]{1,0:T(8,128)S(1)}, f32[16,2048]{1,0:T(8,128)S(1)}, u32[]{:S(2)}, u32[]{:S(2)}) collective-permute-start(f32[16,2048]{1,0:T(8,128)S(1)} %add.3.refs_5_.refs_1_), channel_id=1, source_target_pairs={{0,2},{1,3},{2,0},{3,1},{4,6},{5,7},{6,4},{7,5},{8,10},{9,11},{10,... | collective-permute-start | bytes 393224 | tf_op jit(solution)/shard_map/ppermute | solution.py:313
  35.3 13.6 %collective-permute-start.10 = (bf16[32,2048]{1,0:T(8,128)(2,1)S(1)}, bf16[32,2048]{1,0:T(8,128)(2,1)S(1)}, u32[]{:S(2)}, u32[]{:S(2)}) collective-permute-start(bf16[32,2048]{1,0:T(8,128)(2,1)S(1)} %get-tuple-element.83), channel_id=1, source_target_pairs={{0,8},{4,12},{8,0},{12,4},{1,9},{5,13},{9,1},{13,5},{2,10},{6,14},... | collective-permute-start | bytes 393224 | tf_op jit(solution)/shard_map/ppermute | solution.py:313
  38.4 10.5 %collective-permute-start.11 = (bf16[32,2048]{1,0:T(8,128)(2,1)S(1)}, bf16[32,2048]{1,0:T(8,128)(2,1)S(1)}, u32[]{:S(2)}, u32[]{:S(2)}) collective-permute-start(bf16[32,2048]{1,0:T(8,128)(2,1)S(1)} %get-tuple-element.84), channel_id=1, source_target_pairs={{0,12},{4,8},{8,4},{12,0},{1,13},{5,9},{9,5},{13,1},{2,14},{6,10},... | collective-permute-start | bytes 393224 | tf_op jit(solution)/shard_map/ppermute | solution.py:313
  40.3 11.2 %collective-permute-start.13 = (bf16[32,256]{1,0:T(8,128)(2,1)S(1)}, bf16[32,256]{1,0:T(8,128)(2,1)S(1)}, u32[]{:S(2)}, u32[]{:S(2)}) collective-permute-start(bf16[32,256]{1,0:T(8,128)(2,1)S(1)} %get-tuple-element.86), channel_id=1, source_target_pairs={{0,8},{4,12},{8,0},{12,4},{1,9},{5,13},{9,1},{13,5},{2,10},{6,14},... | collective-permute-start | bytes 49160 | tf_op jit(solution)/shard_map/ppermute | solution.py:313
  41.2 10.4 %collective-permute-start.14 = (bf16[32,256]{1,0:T(8,128)(2,1)S(1)}, bf16[32,256]{1,0:T(8,128)(2,1)S(1)}, u32[]{:S(2)}, u32[]{:S(2)}) collective-permute-start(bf16[32,256]{1,0:T(8,128)(2,1)S(1)} %get-tuple-element.87), channel_id=1, source_target_pairs={{0,12},{4,8},{8,4},{12,0},{1,13},{5,9},{9,5},{13,1},{2,14},{6,10},... | collective-permute-start | bytes 49160 | tf_op jit(solution)/shard_map/ppermute | solution.py:313
  43.5 8.1 %collective-permute-start.12 = (bf16[32,2304]{1,0:T(8,128)(2,1)S(1)}, bf16[32,2304]{1,0:T(8,128)(2,1)S(1)}, u32[]{:S(2)}, u32[]{:S(2)}) collective-permute-start(bf16[32,2304]{1,0:T(8,128)(2,1)S(1)} %get-tuple-element.85), channel_id=1, source_target_pairs={{0,4},{4,0},{8,12},{12,8},{1,5},{5,1},{9,13},{13,9},{2,6},{6,2},{1... | collective-permute-start | bytes 442376 | tf_op jit(solution)/shard_map/ppermute | solution.py:313

commit v5 on v4

--- a/solution.py
+++ b/solution.py
@@ -61,8 +61,8 @@
 
 def plan_kernel(cap, held, *refs):
     my_list, slot_ids, bank_a, bank_b, upstream, weight = refs[:6]
-    vslot, bank, upstream_v, weight_v = refs[6:10]
-    lists, ids, place_v, sems = refs[10:]
+    vslot, bank, upstream_v, weight_v, my_list_v = refs[6:11]
+    lists, ids, place_v, sems = refs[11:]
     slots = lists.shape[1]
     width = bank_a.shape[1]
     half = upstream.shape[0] // 2
@@ -72,6 +72,7 @@
             pltpu.make_async_copy(slot_ids, ids, sems.at[1]),
             pltpu.make_async_copy(bank_a, bank.at[:, pl.ds(0, width)], sems.at[2]),
             pltpu.make_async_copy(bank_b, bank.at[:, pl.ds(width, bank_b.shape[1])], sems.at[3]),
+            pltpu.make_async_copy(my_list, my_list_v, sems.at[6]),
             pltpu.make_async_copy(weight.at[pl.ds(0, weight_v.shape[0]), :], weight_v, sems.at[4]),
             pltpu.make_async_copy(upstream.at[pl.ds(0, half), :], upstream_v.at[pl.ds(0, half), :], sems.at[5]),
         ]
@@ -267,7 +268,7 @@
     in_a = (own_a, near, *refs[1 : 1 + far])
     in_b = (own_b, near, *refs[2 + far : 2 + 2 * far])
     out_a, out_b, sum_a, sum_b, sem = refs[1 + 2 * rep :]
-    halves = 2
+    halves = 4
     width = sum_a.shape[2] // halves
     copies = []
     for h in range(halves):
@@ -318,7 +319,7 @@
     a_flat = in_hbm(bank_a.reshape(held * rank, width))
     b_flat = in_hbm(bank_b.reshape(held * rank, cols))
     w_flat = in_hbm(base_weight)
-    vslot, bank, upstream_v, weight_first = kernel(
+    vslot, bank, upstream_v, weight_first, own_list = kernel(
         functools.partial(plan_kernel, cap, held),
         "plan",
         [
@@ -326,9 +327,10 @@
             pltpu.VMEM((held * rank, width + cols), BF16),
             pltpu.VMEM((rows, outs), BF16),
             pltpu.VMEM((tile, outs), BF16),
+            pltpu.VMEM((1, slots), I32),
         ],
         [HBM] * 6,
-        [SMEM, VMEM, VMEM, VMEM],
+        [SMEM] + [VMEM] * 4,
         [
             in_hbm(used_lists),
             in_hbm(slot_ids.reshape(nb, BLOCK)),
@@ -341,7 +343,7 @@
             pltpu.SMEM((1, slots), I32),
             pltpu.SMEM((nb, BLOCK), I32),
             pltpu.SMEM((slots,), I32),
-            pltpu.SemaphoreType.DMA((6,)),
+            pltpu.SemaphoreType.DMA((7,)),
         ],
     )
 
@@ -350,9 +352,9 @@
         functools.partial(pick_kernel, rep, cap, held),
         "pick",
         [struct((per, width + cols), BF16)] * rep + [struct((rep * cap,), I32)],
-        [HBM] + [ANY] * (rep - 1) + [VMEM],
+        [ANY] * rep + [VMEM],
         [VMEM] * rep + [SMEM],
-        [in_hbm(used_lists), *lists[: rep - 1], lists[rep]],
+        [own_list, *lists[: rep - 1], lists[rep]],
         [pltpu.SMEM((1, slots), I32)] * rep + [pltpu.SemaphoreType.DMA((rep,))],
     )
     vslot = lists[rep - 1]
@@ -450,7 +452,7 @@
         [
             pltpu.VMEM((held, rank, width), F32),
             pltpu.VMEM((held, rank, cols), F32),
-            pltpu.SemaphoreType.DMA((3,)),
+            pltpu.SemaphoreType.DMA((5,)),
         ],
     )
     return token_gradient, grad_a, grad_b

time: 53.6 us -> 53.6 us (level)
  transfers between devices with their start and end apart: 15 -> 15, of which waited for: 4 -> 5; matrix products, arithmetic and copies ran while one was open for 0% -> 0% of each run, Pallas kernels for 46% -> 46%
where the time goes in v5:
time: 53.6 us; the launch traced here: 53.4 us
  Pallas kernels  27.6 us (51%)
  starting transfers between devices  20.2 us (38%)
  waiting for transfers between devices  4.65 us (9%)
  between operations  0.97 us (2%)
    pallas_call x9, Pallas kernels, kernel(): pl.pallas_call(body, out_shape=outs, in_specs=in_specs, out_specs=out_spe...  27.6 us
    ppermute x15, starting transfers between devices, swap(): lax.ppermute(x, axis, [(i, i ^ s) for i in range(lax.axis_size(axis))])  20.2 us
    ppermute x15, waiting for transfers between devices, swap(): lax.ppermute(x, axis, [(i, i ^ s) for i in range(lax.axis_size(axis))])  4.65 us
  transfers between devices with their start and end apart: 15, of which 5 were waited for; matrix products, arithmetic and copies ran while one was open for 0% of the time, Pallas kernels for 46%

profile of v5, /device:TPU:0, one launch (start us, length us, event | category | flops | bytes accessed | tf_op | source)
XLA Modules:
  0.0 53.4 jit_solution(8525015590972298977)
XLA Ops:
  0.6 3.1 %collective-permute-start = (s32[1,8]{1,0:T(1,128)}, s32[1,8]{1,0:T(1,128)S(1)}, u32[]{:S(2)}, u32[]{:S(2)}) collective-permute-start(s32[1,8]{1,0:T(1,128)} %refs_0_.1), channel_id=1, source_target_pairs={{0,4},{4,0},{8,12},{12,8},{1,5},{5,1},{9,13},{13,9},{2,6},{6,2},{1... | collective-permute-start | bytes 104 | tf_op jit(solution)/shard_map/ppermute | solution.py:314
  3.7 2.5 %collective-permute-start.2 = (s32[1,8]{1,0:T(1,128)}, s32[1,8]{1,0:T(1,128)S(1)}, u32[]{:S(2)}, u32[]{:S(2)}) collective-permute-start(s32[1,8]{1,0:T(1,128)} %refs_0_.1), channel_id=1, source_target_pairs={{0,12},{4,8},{8,4},{12,0},{1,13},{5,9},{9,5},{13,1},{2,14},{6,10},... | collective-permute-start | bytes 104 | tf_op jit(solution)/shard_map/ppermute | solution.py:314
  6.2 0.1 collective-permute-start.1
  6.3 2.8 %plan.1 = (s32[16]{0:T(128)S(1)}, bf16[128,2304]{1,0:T(8,128)(2,1)S(1)}, bf16[2048,1024]{1,0:T(8,128)(2,1)S(1)}, bf16[512,1024]{1,0:T(8,128)(2,1)S(1)}, s32[1,8]{1,0:T(1,128)S(1)}) custom-call(s32[1,8]{1,0:T(1,128)} %refs_0_.1, s32[16,128]{1,0:T(8,128)} %bitcast.5, bf16[128,2048]{1,0:T(8,128)(2,1)} %bitcast.3, bf16[128,256]{1,0:T(8,128)(2,1)} %bitcast.4, ...), custom_call_target="tpu_custom_call" | custom-call | tf_op jit(solution)/shard_map/plan/pallas_call | solution.py:31
  9.1 0.0 collective-permute-done.refs_1_
  9.1 0.1 collective-permute-done.2.refs_3_
  9.2 1.6 %collective-permute-done.1.refs_2_ = s32[1,8]{1,0:T(1,128)S(1)} collective-permute-done((s32[1,8]{1,0:T(1,128)}, s32[1,8]{1,0:T(1,128)S(1)}, u32[]{:S(2)}, u32[]{:S(2)}) %collective-permute-start.1) | collective-permute-done | bytes 64 | tf_op jit(solution)/shard_map/ppermute | solution.py:314
  10.8 1.3 %pick.1 = (bf16[32,2304]{1,0:T(8,128)(2,1)S(1)}, bf16[32,2304]{1,0:T(8,128)(2,1)S(1)}, bf16[32,2304]{1,0:T(8,128)(2,1)S(1)}, bf16[32,2304]{1,0:T(8,128)(2,1)S(1)}, s32[8]{0:T(128)S(1)}) custom-call(s32[1,8]{1,0:T(1,128)S(1)} %get-tuple-element.48.refs_0_, s32[1,8]{1,0:T(1,128)S(1)} %collective-permute-done.refs_1_, ...), custom_call_target="tpu_custom_call" | custom-call | tf_op jit(solution)/shard_map/pick/pallas_call | solution.py:31
  12.1 1.2 %collective-permute-start.3 = (bf16[32,2304]{1,0:T(8,128)(2,1)S(1)}, bf16[32,2304]{1,0:T(8,128)(2,1)S(1)}, u32[]{:S(2)}, u32[]{:S(2)}) collective-permute-start(bf16[32,2304]{1,0:T(8,128)(2,1)S(1)} %get-tuple-element.55), channel_id=1, source_target_pairs={{0,8},{4,12},{8,0},{12,4},{1,9},{5,13},{9,1},{13,5},{2,10},{6,14},... | collective-permute-start | bytes 442376 | tf_op jit(solution)/shard_map/ppermute | solution.py:314
  13.3 1.9 %collective-permute-start.4 = (bf16[32,2304]{1,0:T(8,128)(2,1)S(1)}, bf16[32,2304]{1,0:T(8,128)(2,1)S(1)}, u32[]{:S(2)}, u32[]{:S(2)}) collective-permute-start(bf16[32,2304]{1,0:T(8,128)(2,1)S(1)} %get-tuple-element.56), channel_id=1, source_target_pairs={{0,12},{4,8},{8,4},{12,0},{1,13},{5,9},{9,5},{13,1},{2,14},{6,10},... | collective-permute-start | bytes 442376 | tf_op jit(solution)/shard_map/ppermute | solution.py:314
  15.2 0.4 collective-permute-start.5
  15.6 10.1 %frozen.1 = (f32[2048,2048]{1,0:T(8,128)S(1)}, bf16[2048,2048]{1,0:T(8,128)(2,1)S(1)}, bf16[2048,1024]{1,0:T(8,128)(2,1)S(1)}) custom-call(bf16[2048,1024]{1,0:T(8,128)(2,1)S(1)} %get-tuple-element.57.refs_0_, bf16[512,1024]{1,0:T(8,128)(2,1)S(1)} %get-tuple-element.58.refs_1_, bf16[2048,1024]{1,0:T(8,128)(2,1)} %refs_2_.1, ...), custom_call_target="tpu_custom_call", output_to_operand_aliasing={{2}: (0, {})} | custom-call | tf_op jit(solution)/shard_map/frozen/pallas_call | solution.py:31
  25.7 0.0 collective-permute-done.3.refs_4_
  25.7 0.0 collective-permute-done.4.refs_5_
  25.8 0.0 collective-permute-done.5.refs_3_
  25.8 1.6 %collective-permute-start.6 = (bf16[128,256]{1,0:T(8,128)(2,1)S(1)}, bf16[128,256]{1,0:T(8,128)(2,1)S(1)}, u32[]{:S(2)}, u32[]{:S(2)}) collective-permute-start(bf16[128,256]{1,0:T(8,128)(2,1)S(1)} %pad_maximum_fusion.refs_6_), channel_id=1, source_target_pairs={{0,2},{1,3},{2,0},{3,1},{4,6},{5,7},{6,4},{7,5},{8,10},{9,11},{10,... | collective-permute-start | bytes 196616 | tf_op jit(solution)/shard_map/ppermute | solution.py:314
  27.4 3.0 %down.1 = (f32[16,2048]{1,0:T(8,128)S(1)}, bf16[128,2048]{1,0:T(8,128)(2,1)S(1)}) custom-call(s32[16]{0:T(128)S(1)} %get-tuple-element.64.refs_0_, bf16[2048,2048]{1,0:T(8,128)(2,1)S(1)} %get-tuple-element.74.refs_1_.refs_4_, bf16[32,2304]{1,0:T(8,128)(2,1)S(1)} %get-tuple-element.70.refs_5_.refs_2_, bf16[32,2304]{1,0:T(8,128)(2,1)S(1)} %collective-permute-done.5.refs_3_, ...), custom_call_target="tpu_custom_call" | custom-call | tf_op jit(solution)/shard_map/down/pallas_call | solution.py:31
  30.4 0.0 collective-permute-done.6
  30.4 0.1 collective-permute-start.7
  30.5 0.5 collective-permute-start.8
  31.0 0.7 %up_first.1.refs_2_ = f32[2048,128]{1,0:T(8,128)S(1)} custom-call(bf16[2048,1024]{1,0:T(8,128)(2,1)S(1)} %get-tuple-element.69.upstream.refs_1_.refs_3_, bf16[256,256]{1,0:T(8,128)(2,1)S(1)} %constant_dynamic-update-slice_fusion.held_q), custom_call_target="tpu_custom_call" | custom-call | tf_op jit(solution)/shard_map/up_first/pallas_call | solution.py:31
  31.7 0.1 collective-permute-done.7
  31.8 1.3 %collective-permute-start.9 = (f32[16,2048]{1,0:T(8,128)S(1)}, f32[16,2048]{1,0:T(8,128)S(1)}, u32[]{:S(2)}, u32[]{:S(2)}) collective-permute-start(f32[16,2048]{1,0:T(8,128)S(1)} %add.3.refs_5_.refs_1_), channel_id=1, source_target_pairs={{0,2},{1,3},{2,0},{3,1},{4,6},{5,7},{6,4},{7,5},{8,10},{9,11},{10,... | collective-permute-start | bytes 393224 | tf_op jit(solution)/shard_map/ppermute | solution.py:314
  33.1 0.0 collective-permute-done.8.refs_3_
  33.1 2.6 %up_grad_a.1 = (bf16[2048,128]{1,0:T(8,128)(2,1)S(1)}, f32[32,2048]{1,0:T(8,128)S(1)}, bf16[32,2048]{1,0:T(8,128)(2,1)S(1)}, bf16[32,2048]{1,0:T(8,128)(2,1)S(1)}, bf16[32,2048]{1,0:T(8,128)(2,1)S(1)}) custom-call(s32[16]{0:T(128)S(1)} %get-tuple-element.64.refs_0_, bf16[2048,1024]{1,0:T(8,128)(2,1)S(1)} %get-tuple-element.69.upstream.refs_1_.refs_3_, ...), custom_call_target="tpu_custom_call" | custom-call | tf_op jit(solution)/shard_map/up_grad_a/pallas_call | solution.py:31
  35.7 2.1 %collective-permute-start.10 = (bf16[32,2048]{1,0:T(8,128)(2,1)S(1)}, bf16[32,2048]{1,0:T(8,128)(2,1)S(1)}, u32[]{:S(2)}, u32[]{:S(2)}) collective-permute-start(bf16[32,2048]{1,0:T(8,128)(2,1)S(1)} %get-tuple-element.85), channel_id=1, source_target_pairs={{0,8},{4,12},{8,0},{12,4},{1,9},{5,13},{9,1},{13,5},{2,10},{6,14},... | collective-permute-start | bytes 393224 | tf_op jit(solution)/shard_map/ppermute | solution.py:314
  37.8 1.9 %collective-permute-start.11 = (bf16[32,2048]{1,0:T(8,128)(2,1)S(1)}, bf16[32,2048]{1,0:T(8,128)(2,1)S(1)}, u32[]{:S(2)}, u32[]{:S(2)}) collective-permute-start(bf16[32,2048]{1,0:T(8,128)(2,1)S(1)} %get-tuple-element.86), channel_id=1, source_target_pairs={{0,12},{4,8},{8,4},{12,0},{1,13},{5,9},{9,5},{13,1},{2,14},{6,10},... | collective-permute-start | bytes 393224 | tf_op jit(solution)/shard_map/ppermute | solution.py:314
  39.7 0.0 collective-permute-done.9.refs_2_
  39.7 1.1 %grad_b.1 = (f32[32,256]{1,0:T(8,128)S(1)}, bf16[32,2304]{1,0:T(8,128)(2,1)S(1)}, bf16[32,256]{1,0:T(8,128)(2,1)S(1)}, bf16[32,256]{1,0:T(8,128)(2,1)S(1)}) custom-call(s32[16]{0:T(128)S(1)} %get-tuple-element.64.refs_0_, f32[16,2048]{1,0:T(8,128)S(1)} %add.3.refs_5_.refs_1_, f32[16,2048]{1,0:T(8,128)S(1)} %collective-permute-done.9.refs_2_, ...), custom_call_target="tpu_custom_call" | custom-call | tf_op jit(solution)/shard_map/grad_b/pallas_call | solution.py:31
  40.8 0.1 collective-permute-start.13
  40.9 2.0 %collective-permute-start.14 = (bf16[32,256]{1,0:T(8,128)(2,1)S(1)}, bf16[32,256]{1,0:T(8,128)(2,1)S(1)}, u32[]{:S(2)}, u32[]{:S(2)}) collective-permute-start(bf16[32,256]{1,0:T(8,128)(2,1)S(1)} %get-tuple-element.89), channel_id=1, source_target_pairs={{0,12},{4,8},{8,4},{12,0},{1,13},{5,9},{9,5},{13,1},{2,14},{6,10},... | collective-permute-start | bytes 49160 | tf_op jit(solution)/shard_map/ppermute | solution.py:314
  42.9 1.5 %collective-permute-start.12 = (bf16[32,2304]{1,0:T(8,128)(2,1)S(1)}, bf16[32,2304]{1,0:T(8,128)(2,1)S(1)}, u32[]{:S(2)}, u32[]{:S(2)}) collective-permute-start(bf16[32,2304]{1,0:T(8,128)(2,1)S(1)} %get-tuple-element.87), channel_id=1, source_target_pairs={{0,4},{4,0},{8,12},{12,8},{1,5},{5,1},{9,13},{13,9},{2,6},{6,2},{1... | collective-permute-start | bytes 442376 | tf_op jit(solution)/shard_map/ppermute | solution.py:314
  44.3 4.4 %token_gradient.1.refs_8_ = bf16[2048,2048]{1,0:T(8,128)(2,1)} custom-call(f32[2048,2048]{1,0:T(8,128)S(1)} %get-tuple-element.63.refs_0_, bf16[2048,128]{1,0:T(8,128)(2,1)S(1)} %get-tuple-element.80.refs_1_, bf16[128,2048]{1,0:T(8,128)(2,1)S(1)} %get-tuple-element.81.refs_2_, f32[32,256]{1,0:T(8,128)S(1)} %get-tuple-element.83.refs_3_.refs_7_), custom_call_target="tpu_custom_call" | custom-call | flops 4294967296 | tf_op jit(solution)/shard_map/token_gradient/pallas_call | solution.py:31
  48.7 0.6 %collective-permute-done.10.refs_1_ = bf16[32,2048]{1,0:T(8,128)(2,1)S(1)} collective-permute-done((bf16[32,2048]{1,0:T(8,128)(2,1)S(1)}, bf16[32,2048]{1,0:T(8,128)(2,1)S(1)}, u32[]{:S(2)}, u32[]{:S(2)}) %collective-permute-start.10) | collective-permute-done | bytes 131104 | tf_op jit(solution)/shard_map/ppermute | solution.py:314
  49.3 0.0 collective-permute-done.11.refs_2_
  49.3 2.2 %collective-permute-done.13.refs_4_ = bf16[32,256]{1,0:T(8,128)(2,1)S(1)} collective-permute-done((bf16[32,256]{1,0:T(8,128)(2,1)S(1)}, bf16[32,256]{1,0:T(8,128)(2,1)S(1)}, u32[]{:S(2)}, u32[]{:S(2)}) %collective-permute-start.13) | collective-permute-done | bytes 16416 | tf_op jit(solution)/shard_map/ppermute | solution.py:314
  51.6 0.0 collective-permute-done.14.refs_5_
  51.6 0.0 collective-permute-done.12.refs_3_
  51.6 1.7 %finish.1 = (f32[8,16,2048]{2,1,0:T(8,128)}, f32[8,16,256]{2,1,0:T(8,128)}) custom-call(s32[8]{0:T(128)S(1)} %get-tuple-element.84.refs_0_, bf16[32,2048]{1,0:T(8,128)(2,1)S(1)} %collective-permute-done.10.refs_1_, bf16[32,2048]{1,0:T(8,128)(2,1)S(1)} %collective-permute-done.11.refs_2_, bf16[32,2304]{1,0:T(8,128)(2,1)S(1)} %collective-permute-done.12.refs_3_, ...), custom_call_target="tpu_custom_call" | custom-call | tf_op jit(solution)/shard_map/finish/pallas_call | solution.py:31
  (7 shorter events, 0.0 us)
Async XLA Ops:
  0.6 8.5 %collective-permute-start = (s32[1,8]{1,0:T(1,128)}, s32[1,8]{1,0:T(1,128)S(1)}, u32[]{:S(2)}, u32[]{:S(2)}) collective-permute-start(s32[1,8]{1,0:T(1,128)} %refs_0_.1), channel_id=1, source_target_pairs={{0,4},{4,0},{8,12},{12,8},{1,5},{5,1},{9,13},{13,9},{2,6},{6,2},{1... | collective-permute-start | bytes 104 | tf_op jit(solution)/shard_map/ppermute | solution.py:314
  3.7 5.5 %collective-permute-start.2 = (s32[1,8]{1,0:T(1,128)}, s32[1,8]{1,0:T(1,128)S(1)}, u32[]{:S(2)}, u32[]{:S(2)}) collective-permute-start(s32[1,8]{1,0:T(1,128)} %refs_0_.1), channel_id=1, source_target_pairs={{0,12},{4,8},{8,4},{12,0},{1,13},{5,9},{9,5},{13,1},{2,14},{6,10},... | collective-permute-start | bytes 104 | tf_op jit(solution)/shard_map/ppermute | solution.py:314
  6.2 4.6 %collective-permute-start.1 = (s32[1,8]{1,0:T(1,128)}, s32[1,8]{1,0:T(1,128)S(1)}, u32[]{:S(2)}, u32[]{:S(2)}) collective-permute-start(s32[1,8]{1,0:T(1,128)} %refs_0_.1), channel_id=1, source_target_pairs={{0,8},{4,12},{8,0},{12,4},{1,9},{5,13},{9,1},{13,5},{2,10},{6,14},... | collective-permute-start | bytes 104 | tf_op jit(solution)/shard_map/ppermute | solution.py:314
  12.1 13.6 %collective-permute-start.3 = (bf16[32,2304]{1,0:T(8,128)(2,1)S(1)}, bf16[32,2304]{1,0:T(8,128)(2,1)S(1)}, u32[]{:S(2)}, u32[]{:S(2)}) collective-permute-start(bf16[32,2304]{1,0:T(8,128)(2,1)S(1)} %get-tuple-element.55), channel_id=1, source_target_pairs={{0,8},{4,12},{8,0},{12,4},{1,9},{5,13},{9,1},{13,5},{2,10},{6,14},... | collective-permute-start | bytes 442376 | tf_op jit(solution)/shard_map/ppermute | solution.py:314
  13.3 12.4 %collective-permute-start.4 = (bf16[32,2304]{1,0:T(8,128)(2,1)S(1)}, bf16[32,2304]{1,0:T(8,128)(2,1)S(1)}, u32[]{:S(2)}, u32[]{:S(2)}) collective-permute-start(bf16[32,2304]{1,0:T(8,128)(2,1)S(1)} %get-tuple-element.56), channel_id=1, source_target_pairs={{0,12},{4,8},{8,4},{12,0},{1,13},{5,9},{9,5},{13,1},{2,14},{6,10},... | collective-permute-start | bytes 442376 | tf_op jit(solution)/shard_map/ppermute | solution.py:314
  15.2 10.6 %collective-permute-start.5 = (bf16[32,2304]{1,0:T(8,128)(2,1)S(1)}, bf16[32,2304]{1,0:T(8,128)(2,1)S(1)}, u32[]{:S(2)}, u32[]{:S(2)}) collective-permute-start(bf16[32,2304]{1,0:T(8,128)(2,1)S(1)} %get-tuple-element.65), channel_id=1, source_target_pairs={{0,4},{4,0},{8,12},{12,8},{1,5},{5,1},{9,13},{13,9},{2,6},{6,2},{1... | collective-permute-start | bytes 442376 | tf_op jit(solution)/shard_map/ppermute | solution.py:314
  25.8 4.6 %collective-permute-start.6 = (bf16[128,256]{1,0:T(8,128)(2,1)S(1)}, bf16[128,256]{1,0:T(8,128)(2,1)S(1)}, u32[]{:S(2)}, u32[]{:S(2)}) collective-permute-start(bf16[128,256]{1,0:T(8,128)(2,1)S(1)} %pad_maximum_fusion.refs_6_), channel_id=1, source_target_pairs={{0,2},{1,3},{2,0},{3,1},{4,6},{5,7},{6,4},{7,5},{8,10},{9,11},{10,... | collective-permute-start | bytes 196616 | tf_op jit(solution)/shard_map/ppermute | solution.py:314
  30.4 1.4 %collective-permute-start.7 = (f32[16,2048]{1,0:T(8,128)S(1)}, f32[16,2048]{1,0:T(8,128)S(1)}, u32[]{:S(2)}, u32[]{:S(2)}) collective-permute-start(f32[16,2048]{1,0:T(8,128)S(1)} %get-tuple-element.76), channel_id=1, source_target_pairs={{0,1},{1,0},{2,3},{3,2},{4,5},{5,4},{6,7},{7,6},{8,9},{9,8},{10,11... | collective-permute-start | bytes 393224 | tf_op jit(solution)/shard_map/ppermute | solution.py:314
  30.5 2.6 %collective-permute-start.8 = (bf16[256,256]{1,0:T(8,128)(2,1)S(1)}, bf16[256,256]{1,0:T(8,128)(2,1)S(1)}, u32[]{:S(2)}, u32[]{:S(2)}) collective-permute-start(bf16[256,256]{1,0:T(8,128)(2,1)S(1)} %constant_dynamic-update-slice_fusion.held_q), channel_id=1, source_target_pairs={{0,1},{1,0},{2,3},{3,2},{4,5},{5,4},{6,7},{7,6},{8,9},{9,8},{10,11... | collective-permute-start | bytes 393224 | tf_op jit(solution)/shard_map/ppermute | solution.py:314
  31.8 7.9 %collective-permute-start.9 = (f32[16,2048]{1,0:T(8,128)S(1)}, f32[16,2048]{1,0:T(8,128)S(1)}, u32[]{:S(2)}, u32[]{:S(2)}) collective-permute-start(f32[16,2048]{1,0:T(8,128)S(1)} %add.3.refs_5_.refs_1_), channel_id=1, source_target_pairs={{0,2},{1,3},{2,0},{3,1},{4,6},{5,7},{6,4},{7,5},{8,10},{9,11},{10,... | collective-permute-start | bytes 393224 | tf_op jit(solution)/shard_map/ppermute | solution.py:314
  35.7 13.7 %collective-permute-start.10 = (bf16[32,2048]{1,0:T(8,128)(2,1)S(1)}, bf16[32,2048]{1,0:T(8,128)(2,1)S(1)}, u32[]{:S(2)}, u32[]{:S(2)}) collective-permute-start(bf16[32,2048]{1,0:T(8,128)(2,1)S(1)} %get-tuple-element.85), channel_id=1, source_target_pairs={{0,8},{4,12},{8,0},{12,4},{1,9},{5,13},{9,1},{13,5},{2,10},{6,14},... | collective-permute-start | bytes 393224 | tf_op jit(solution)/shard_map/ppermute | solution.py:314
  37.8 11.5 %collective-permute-start.11 = (bf16[32,2048]{1,0:T(8,128)(2,1)S(1)}, bf16[32,2048]{1,0:T(8,128)(2,1)S(1)}, u32[]{:S(2)}, u32[]{:S(2)}) collective-permute-start(bf16[32,2048]{1,0:T(8,128)(2,1)S(1)} %get-tuple-element.86), channel_id=1, source_target_pairs={{0,12},{4,8},{8,4},{12,0},{1,13},{5,9},{9,5},{13,1},{2,14},{6,10},... | collective-permute-start | bytes 393224 | tf_op jit(solution)/shard_map/ppermute | solution.py:314
  40.8 10.8 %collective-permute-start.13 = (bf16[32,256]{1,0:T(8,128)(2,1)S(1)}, bf16[32,256]{1,0:T(8,128)(2,1)S(1)}, u32[]{:S(2)}, u32[]{:S(2)}) collective-permute-start(bf16[32,256]{1,0:T(8,128)(2,1)S(1)} %get-tuple-element.88), channel_id=1, source_target_pairs={{0,8},{4,12},{8,0},{12,4},{1,9},{5,13},{9,1},{13,5},{2,10},{6,14},... | collective-permute-start | bytes 49160 | tf_op jit(solution)/shard_map/ppermute | solution.py:314
  40.9 10.7 %collective-permute-start.14 = (bf16[32,256]{1,0:T(8,128)(2,1)S(1)}, bf16[32,256]{1,0:T(8,128)(2,1)S(1)}, u32[]{:S(2)}, u32[]{:S(2)}) collective-permute-start(bf16[32,256]{1,0:T(8,128)(2,1)S(1)} %get-tuple-element.89), channel_id=1, source_target_pairs={{0,12},{4,8},{8,4},{12,0},{1,13},{5,9},{9,5},{13,1},{2,14},{6,10},... | collective-permute-start | bytes 49160 | tf_op jit(solution)/shard_map/ppermute | solution.py:314
  42.9 8.7 %collective-permute-start.12 = (bf16[32,2304]{1,0:T(8,128)(2,1)S(1)}, bf16[32,2304]{1,0:T(8,128)(2,1)S(1)}, u32[]{:S(2)}, u32[]{:S(2)}) collective-permute-start(bf16[32,2304]{1,0:T(8,128)(2,1)S(1)} %get-tuple-element.87), channel_id=1, source_target_pairs={{0,4},{4,0},{8,12},{12,8},{1,5},{5,1},{9,13},{13,9},{2,6},{6,2},{1... | collective-permute-start | bytes 442376 | tf_op jit(solution)/shard_map/ppermute | solution.py:314
